TPU v7x, 32 devices: a whole 2x2x4 slice. The times are simulated.
32 devices in a mesh: dp: 8 (over y, x, core), head: 4 (over z).
Axes of the slice: x: 2, y: 2, z: 4, core: 2. Of those that a mesh axis runs over, the one named last changes fastest.
Arguments:
- features: bfloat16 [2048, 16384], P(None, ('dp', 'head'))
- crop_rows: int32 [2], replicated, may hold values from 32 to 64, as said below
- crop_cols: int32 [2], replicated, may hold values from 64 to 128, as said below
- labels: int32 [16384], P('dp'), may hold values from 0 to 18
- offset_targets: float32 [2, 16384], P(None, 'dp'), may hold values from -6 to 6
- depth_targets: float32 [16384], P('dp'), may hold values from 0.1 to 3
- lidar_mask: int32 [16384], P('dp'), may hold values from 0 to 1, as said below
- trunk_aspp: float32 [4, 30336, 128], P('head', 'dp')
- aspp_first: float32 [4, 30336, 128], P('head', 'dp'), may hold values from -7.6293945e-06 to 7.6293945e-06
- aspp_second: float32 [4, 30336, 128], P('head', 'dp'), may hold values from 6.5348386e-12 to 2.6040343e-11
- trunk_neck: float32 [4, 8704, 128], P('head', 'dp')
- neck_first: float32 [4, 8704, 128], P('head', 'dp'), may hold values from -7.6293945e-06 to 7.6293945e-06
- neck_second: float32 [4, 8704, 128], P('head', 'dp'), may hold values from 6.5348386e-12 to 2.6040343e-11
- norm_params: float32 [2, 4352], replicated
- norm_first: float32 [2, 4352], replicated, may hold values from -7.6293945e-05 to 7.6293945e-05
- norm_second: float32 [2, 4352], replicated, may hold values from 6.534839e-10 to 2.6040343e-09
- decoders: float32 [790, 256], replicated
- decoder_first: float32 [790, 256], replicated, may hold values from -2.2888184e-05 to 2.2888184e-05
- decoder_second: float32 [790, 256], replicated, may hold values from 5.84175e-11 to 2.3466012e-10
- log_vars: float32 [3], replicated, may hold values from -0.5 to 0.5
- log_first: float32 [3], replicated, may hold values from -0.0068359375 to 0.0068359375
- log_second: float32 [3], replicated, may hold values from 5.3e-06 to 2.1e-05
Outputs:
- total_loss: float32 [], replicated
- grad_norm: float32 [], replicated
- aspp_new: float32 [4, 30336, 128], P('head', 'dp')
- aspp_first_new: float32 [4, 30336, 128], P('head', 'dp')
- aspp_second_new: float32 [4, 30336, 128], P('head', 'dp')
- neck_new: float32 [4, 8704, 128], P('head', 'dp')
- neck_first_new: float32 [4, 8704, 128], P('head', 'dp')
- neck_second_new: float32 [4, 8704, 128], P('head', 'dp')
- norm_new: float32 [2, 4352], replicated
- norm_first_new: float32 [2, 4352], replicated
- norm_second_new: float32 [2, 4352], replicated
- decoder_new: float32 [790, 256], replicated
- decoder_first_new: float32 [790, 256], replicated
- decoder_second_new: float32 [790, 256], replicated
- log_new: float32 [3], replicated
- log_first_new: float32 [3], replicated
- log_second_new: float32 [3], replicated
Inputs may be any that keep to these rules, and one draw needn't show every extreme that they name: `crop_rows`: one crop, drawn from the seed, has all 64 rows. `crop_cols`: one crop, drawn from the seed, has all 128 columns. `lidar_mask`: every pixel of column 0 is 1.
All inputs are finite; a program needn't handle non-finite values.
Results may differ from a plain program's by a relative error of at most 0.014.
Values may be sent and summed in bfloat16 or wider, within the bound.
No kernel may reach another device: no remote copies, remote signals or barrier semaphores. Data moves between devices by JAX's collectives and lax.ppermute only.
A program may use at most 384 MiB of HBM per device.

v0:
```python
import jax
import jax.numpy as jnp
from jax import lax
from jax.sharding import PartitionSpec as P

FEAT = 2048
BOT = 512
ASP = 256
CLS = 19
WIDTH = 128
ROWS_DEV = 4
CROP_DEV = 16
STEP = 10


EPSILON = 1e-05
BETA_ONE = 0.9
BETA_TWO = 0.95
ADAM_EPSILON = 1e-08
CLIP_LIMIT = 0.05
RATES = (12, 24, 36)


def shifted_2(x, axis, by):
    length = lax.axis_size(axis)
    pairs = [(i, i + by) for i in range(length) if 0 <= i + by < length]
    return lax.ppermute(x, axis, pairs)


def silu_slope(pre_norm):
    sigmoid_value = jax.nn.sigmoid(pre_norm)
    return sigmoid_value * (1.0 + pre_norm * (1.0 - sigmoid_value))


def matmul(operand_one, operand_two):
    return jnp.dot(operand_one, operand_two, preferred_element_type=jnp.float32)


def contract_rows(operand_one, operand_two):
    return lax.dot_general(
        operand_one, operand_two, (((0,), (0,)), ((), ())), preferred_element_type=jnp.float32
    )


def contract_cols(operand_one, operand_two):
    return lax.dot_general(
        operand_one, operand_two, (((1,), (1,)), ((), ())), preferred_element_type=jnp.float32
    )


def unpack_front(flat):
    quarters = flat.shape[0]
    quarter = ASP // 4
    flat_line = flat.reshape(quarters, -1)
    first_end = quarter * FEAT
    taps_end = first_end + 27 * quarter * FEAT
    pool_end = taps_end + quarter * FEAT
    proj_end = pool_end + quarter * 5 * ASP
    one_w = flat_line[:, :first_end].reshape(quarters * quarter, FEAT)
    taps = flat_line[:, first_end:taps_end].reshape(quarters, 27, quarter, FEAT)
    taps = jnp.moveaxis(taps, 0, 1).reshape(27, quarters * quarter, FEAT)
    pool_w = flat_line[:, taps_end:pool_end].reshape(quarters * quarter, FEAT)
    project_w = flat_line[:, pool_end:proj_end].reshape(quarters * quarter, 5 * ASP)
    return (one_w, taps, pool_w, project_w)


def unpack_back(flat):
    quarters = flat.shape[0]
    quarter = BOT // 4
    flat_line = flat.reshape(quarters, -1)
    first_end = quarter * FEAT
    second_end = first_end + 9 * quarter * BOT
    third_end = second_end + FEAT // 4 * BOT
    reduce_w = flat_line[:, :first_end].reshape(quarters * quarter, FEAT)
    middle = flat_line[:, first_end:second_end].reshape(quarters, 9, quarter, BOT)
    middle = jnp.moveaxis(middle, 0, 1).reshape(9, quarters * quarter, BOT)
    expand_w = flat_line[:, second_end:third_end].reshape(quarters * (FEAT // 4), BOT)
    return (reduce_w, middle, expand_w)


def by_quarter(gradient_in, axis, quarters):
    shape = gradient_in.shape
    split = shape[:axis] + (quarters, shape[axis] // quarters) + shape[axis + 1 :]
    return jnp.moveaxis(gradient_in.reshape(split), axis, 0).reshape(quarters, -1)


def pack_quarters(pieces, row_total, quarters):
    joined = jnp.concatenate(
        [by_quarter(gradient_in, axis, quarters) for gradient_in, axis in pieces], axis=1
    )
    return joined.reshape(quarters, row_total, 128)


def column_shift(tensor, offset):
    shaped = tensor.reshape(tensor.shape[0], -1, WIDTH)
    if offset > 0:
        shaped = jnp.pad(shaped[:, :, offset:], ((0, 0), (0, 0), (0, offset)))
    elif offset < 0:
        shaped = jnp.pad(shaped[:, :, :offset], ((0, 0), (0, 0), (-offset, 0)))
    return shaped.reshape(tensor.shape)


def crop_keep(received, device, amount):
    inside = (device - amount) // CROP_DEV == device // CROP_DEV
    return jnp.where(inside, received, jnp.zeros_like(received))


def fetch_rows(tensor, groups_away, span_dev, device, backward):
    if groups_away == 0:
        return tensor
    amount = -groups_away * span_dev
    if backward:
        moved = shifted_2(tensor, ("dp", "head"), amount)
    else:
        moved = shifted_2(tensor, ("dp", "head"), amount)
    return crop_keep(moved, device, amount)


def rows_from(tensor, offset, span_dev, device, backward):
    span_rows = ROWS_DEV * span_dev
    lowest = offset // span_rows
    first = fetch_rows(tensor, lowest, span_dev, device, backward)
    return first


def conv_inputs(source, tap_weights, dilation, span_dev, device):
    summed = None
    for row_tap in range(3):
        shifted = rows_from(source, (row_tap - 1) * dilation, span_dev, device, False)
        for col_tap in range(3):
            product = matmul(
                tap_weights[3 * row_tap + col_tap], column_shift(shifted, (col_tap - 1) * dilation)
            )
            summed = product if summed is None else summed + product
    return summed


def conv_backward(grad_low, source, tap_weights, dilation, span_dev, device):
    grad_source = None
    grad_taps = []
    for row_tap in range(3):
        received = rows_from(grad_low, (1 - row_tap) * dilation, span_dev, device, True)
        for col_tap in range(3):
            shifted_grad = column_shift(received, (1 - col_tap) * dilation)
            product = contract_rows(tap_weights[3 * row_tap + col_tap], shifted_grad)
            grad_source = product if grad_source is None else grad_source + product
            grad_taps.append(contract_cols(shifted_grad, source))
    return (grad_source, jnp.stack(grad_taps))


def adam_step(weight, first_m, second_m, gradient, factor, rate, decay):
    clipped = gradient * factor
    new_first = BETA_ONE * first_m + (1.0 - BETA_ONE) * clipped
    new_second = BETA_TWO * second_m + (1.0 - BETA_TWO) * clipped * clipped
    corrected = (
        new_first
        / (1.0 - BETA_ONE**STEP)
        / (jnp.sqrt(new_second / (1.0 - BETA_TWO**STEP)) + ADAM_EPSILON)
    )
    return (weight - rate * (corrected + decay * weight), new_first, new_second)


def arrange(vector, groups):
    return vector[None, :] if groups == 1 else vector.T


def unarrange(matrix, groups):
    return matrix[0] if groups == 1 else matrix.T


def shards(
    features,
    crop_rows,
    crop_cols,
    labels,
    offset_targets,
    depth_targets,
    lidar_mask,
    trunk_aspp,
    aspp_first,
    aspp_second,
    trunk_neck,
    neck_first,
    neck_second,
    norm_params,
    norm_first,
    norm_second,
    decoders,
    decoder_first,
    decoder_second,
    log_vars,
    log_first,
    log_second,
):
    head_count = lax.axis_size("head")
    dp_count = lax.axis_size("dp")
    device = lax.axis_index(("dp", "head"))
    head_index = lax.axis_index("head")
    crop_index = device // CROP_DEV
    crop_total = crop_rows.shape[0]
    span_dev = 1
    working_first = device // span_dev * span_dev

    def to_full(portion):
        return portion.reshape(-1)

    def from_full(complete, groups):
        return complete.reshape(groups, -1)

    low_pair = (trunk_aspp.astype(jnp.bfloat16), trunk_neck.astype(jnp.bfloat16))
    held_aspp, held_neck = (
        lax.all_gather(low_pair[0], "dp", axis=1, tiled=True),
        lax.all_gather(low_pair[1], "dp", axis=1, tiled=True),
    )
    held_aspp, held_neck = (
        lax.all_gather(held_aspp, "head", axis=0, tiled=True),
        lax.all_gather(held_neck, "head", axis=0, tiled=True),
    )
    quarters = held_aspp.shape[0]
    one_w, aspp_taps, pool_w, project_w = unpack_front(held_aspp)
    reduce_w, middle, expand_w = unpack_back(held_neck)

    def valid_rows(first_device, device_span):
        pixel_place = jnp.arange(device_span * ROWS_DEV * WIDTH, dtype=jnp.int32)
        row_place = first_device % CROP_DEV * ROWS_DEV + pixel_place // WIDTH
        col_place = pixel_place % WIDTH
        return ((row_place < crop_rows[crop_index]) & (col_place < crop_cols[crop_index])).astype(
            jnp.float32
        )[None, :]

    valid_mask = valid_rows(working_first, span_dev)
    group_mask = valid_rows(lax.axis_index("dp") * head_count, head_count)
    valid_count = jnp.sum((crop_rows * crop_cols).astype(jnp.float32))
    crop_count = (crop_rows[crop_index] * crop_cols[crop_index]).astype(jnp.float32)
    gains, shifts = (norm_params[0], norm_params[1])
    bounds = [0, BOT, 2 * BOT, 2 * BOT + FEAT, 2 * BOT + FEAT + 4 * ASP, 2 * BOT + FEAT + 5 * ASP]

    def segment(vector, slot_index, groups):
        return unarrange(
            from_full(vector[bounds[slot_index] : bounds[slot_index + 1]], groups), groups
        )

    def norm_forward(pre_norm, slot_index, residual, carried_in):
        groups = 1 if pre_norm.ndim == 2 else 4
        local_sum = jnp.sum(pre_norm * valid_mask, axis=-1)
        local_square = jnp.sum(pre_norm * pre_norm * valid_mask, axis=-1)
        total_sum, total_square, carried = lax.psum(
            (
                to_full(arrange(local_sum, groups)),
                to_full(arrange(local_square, groups)),
                carried_in,
            ),
            ("dp", "head"),
        )
        mean_value = unarrange(from_full(total_sum, groups), groups) / valid_count
        second = unarrange(from_full(total_square, groups), groups) / valid_count
        inv_std = lax.rsqrt(second - mean_value * mean_value + EPSILON)
        normed = (pre_norm - mean_value[..., None]) * inv_std[..., None]
        gain_vec = segment(gains, slot_index, groups)
        shift_vec = segment(shifts, slot_index, groups)
        activation_in = gain_vec[..., None] * normed + shift_vec[..., None] + residual
        return (jax.nn.silu(activation_in) * valid_mask, (normed, inv_std, activation_in), carried)

    def norm_backward(grad_act, kept_state, slot_index, carried_in):
        normed, inv_std, activation_in = kept_state
        groups = 1 if normed.ndim == 2 else 4
        grad_out = grad_act * valid_mask * silu_slope(activation_in)
        full_shift, full_gain, carried = lax.psum(
            (
                to_full(arrange(jnp.sum(grad_out, axis=-1), groups)),
                to_full(arrange(jnp.sum(grad_out * normed, axis=-1), groups)),
                carried_in,
            ),
            ("dp", "head"),
        )
        grad_shift = unarrange(from_full(full_shift, groups), groups)
        grad_gain = unarrange(from_full(full_gain, groups), groups)
        gain_vec = segment(gains, slot_index, groups)
        grad_pre = (
            valid_mask
            * (gain_vec * inv_std)[..., None]
            * (
                grad_out
                - grad_shift[..., None] / valid_count
                - normed * grad_gain[..., None] / valid_count
            )
        )
        return (grad_pre, full_gain, full_shift, carried)

    no_extra = jnp.zeros((1,), jnp.float32)
    masked_in = features * valid_mask.astype(jnp.bfloat16)
    residual_in = masked_in.astype(jnp.float32)
    pool_share = 1.0
    pre_one = matmul(reduce_w, masked_in)
    act_one, kept_one, _ = norm_forward(pre_one, 0, 0.0, no_extra)
    low_one = act_one.astype(jnp.bfloat16)
    pre_two = conv_inputs(low_one, middle, 4, span_dev, device)
    act_two, kept_two, _ = norm_forward(pre_two, 1, 0.0, no_extra)
    low_two = act_two.astype(jnp.bfloat16)
    pre_three = matmul(expand_w, low_two)
    act_y, kept_three, _ = norm_forward(pre_three, 2, residual_in, no_extra)
    low_y = act_y.astype(jnp.bfloat16)
    branches = [matmul(one_w, low_y)]
    for branch_slot, dilation in enumerate(RATES):
        branches.append(
            conv_inputs(
                low_y, aspp_taps[9 * branch_slot : 9 * branch_slot + 9], dilation, span_dev, device
            )
        )
    pre_aspp = jnp.stack(branches, axis=1)
    crop_hot = (jnp.arange(crop_total, dtype=jnp.int32) == crop_index).astype(jnp.float32)
    local_pool = crop_hot[:, None] * jnp.sum(low_y, axis=1, dtype=jnp.float32)[None, :] * pool_share
    act_aspp, kept_aspp, pool_sums = norm_forward(pre_aspp, 3, 0.0, local_pool)
    pooled = (pool_sums[crop_index] / crop_count).astype(jnp.bfloat16)
    pool_pre = matmul(pool_w, pooled[:, None])[:, 0]
    pool_map = jax.nn.silu(pool_pre)[:, None] * valid_mask
    joined = jnp.concatenate([act_aspp, pool_map[:, None, :]], axis=1).astype(jnp.bfloat16)
    project_shaped = project_w.reshape(project_w.shape[0], 5, ASP)
    pre_proj = jnp.einsum("obc,cbp->op", project_shaped, joined, preferred_element_type=jnp.float32)
    act_proj, kept_proj, _ = norm_forward(pre_proj, 4, 0.0, no_extra)
    low_feat = act_proj.astype(jnp.bfloat16)
    group_feat = lax.all_gather(low_feat, "head", axis=1, tiled=True)
    task_slot = jnp.minimum(head_index, 2)
    active = (head_index < 3).astype(jnp.float32)
    low_dec = decoders.astype(jnp.bfloat16)
    hidden_weight = lax.dynamic_slice_in_dim(low_dec, task_slot * ASP, ASP, 0)
    out_weight = low_dec[3 * ASP :]
    dec_pre = matmul(hidden_weight, group_feat)
    low_hidden = jax.nn.silu(dec_pre).astype(jnp.bfloat16)
    logits = matmul(out_weight, low_hidden)
    valid_group = group_mask[0]
    lidar_group = lidar_mask.astype(jnp.float32) * valid_group
    sem_logits = logits[:CLS]
    label_hot = (jnp.arange(CLS, dtype=jnp.int32)[:, None] == labels[None, :]).astype(jnp.float32)
    log_total = jax.nn.logsumexp(sem_logits, axis=0)
    sem_sum = jnp.sum((log_total - jnp.sum(label_hot * sem_logits, axis=0)) * valid_group)
    off_diff = logits[CLS : CLS + 2] - offset_targets
    off_root = jnp.sqrt(off_diff * off_diff + 1.0)
    off_sum = jnp.sum((off_root - 1.0) * valid_group)
    dep_logit = logits[CLS + 2]
    dep_diff = jax.nn.softplus(dep_logit) - depth_targets
    dep_root = jnp.sqrt(dep_diff * dep_diff + 1.0)
    dep_sum = jnp.sum((dep_root - 1.0) * lidar_group)
    task_hot = (jnp.arange(3, dtype=jnp.int32) == task_slot).astype(jnp.float32) * active
    local_losses = task_hot * jnp.stack([sem_sum, off_sum, dep_sum])
    lidar_local = jnp.where(head_index == 0, jnp.sum(lidar_group), 0.0)
    loss_sums, lidar_count = lax.psum((local_losses, lidar_local), ("dp", "head"))
    divisors = jnp.stack([valid_count, valid_count, lidar_count])
    losses = loss_sums / divisors
    total_loss = jnp.sum(jnp.exp(-log_vars) * losses + log_vars)
    grad_logvar = 1.0 - jnp.exp(-log_vars) * losses
    task_weight = task_hot * jnp.exp(-log_vars) / divisors
    grad_sem = (jax.nn.softmax(sem_logits, axis=0) - label_hot) * valid_group * task_weight[0]
    grad_off = off_diff / off_root * valid_group * task_weight[1]
    grad_dep = (dep_diff / dep_root * jax.nn.sigmoid(dep_logit) * lidar_group * task_weight[2])[
        None, :
    ]
    grad_logits = jnp.concatenate([grad_sem, grad_off, grad_dep], axis=0).astype(jnp.bfloat16)
    grad_out_weight = contract_cols(grad_logits, low_hidden)
    grad_dec_pre = (contract_rows(out_weight, grad_logits) * silu_slope(dec_pre)).astype(
        jnp.bfloat16
    )
    grad_hidden_weight = contract_cols(grad_dec_pre, group_feat)
    grad_group = contract_rows(hidden_weight, grad_dec_pre) * active
    dec_grad_local = jnp.concatenate(
        [
            lax.dynamic_update_slice_in_dim(
                jnp.zeros((3 * ASP, ASP), jnp.float32), grad_hidden_weight, task_slot * ASP, 0
            ),
            grad_out_weight,
        ],
        axis=0,
    )
    grad_feat = lax.psum_scatter(
        grad_group.astype(jnp.bfloat16), "head", scatter_dimension=1, tiled=True
    ).astype(jnp.float32)
    grad_proj_pre, gain_proj, shift_proj, dec_grad = norm_backward(
        grad_feat, kept_proj, 4, dec_grad_local
    )
    grad_proj_low = grad_proj_pre.astype(jnp.bfloat16)
    grad_project = jnp.einsum(
        "op,cbp->obc", grad_proj_low, joined, preferred_element_type=jnp.float32
    ).reshape(project_w.shape[0], 5 * ASP)
    grad_joined = jnp.einsum(
        "obc,op->cbp", project_shaped, grad_proj_low, preferred_element_type=jnp.float32
    )
    pool_local = crop_hot[:, None] * jnp.sum(grad_joined[:, 4] * valid_mask, axis=1)[None, :]
    grad_aspp_pre, gain_aspp, shift_aspp, pool_grads = norm_backward(
        grad_joined[:, :4], kept_aspp, 3, to_full(pool_local)
    )
    pool_row = from_full(pool_grads, crop_total)[crop_index]
    grad_pool_pre = (pool_row * silu_slope(pool_pre)).astype(jnp.bfloat16)
    leader = (working_first % CROP_DEV == 0).astype(jnp.float32)
    grad_pool = leader * (
        grad_pool_pre.astype(jnp.float32)[:, None] * pooled.astype(jnp.float32)[None, :]
    )
    grad_pooled = contract_rows(pool_w, grad_pool_pre[:, None])[:, 0]
    grad_y = grad_pooled[:, None] / crop_count * valid_mask
    grad_aspp_low = grad_aspp_pre.astype(jnp.bfloat16)
    grad_one_w = contract_cols(grad_aspp_low[:, 0], low_y)
    grad_y = grad_y + contract_rows(one_w, grad_aspp_low[:, 0])
    tap_grads = []
    for branch_slot, dilation in enumerate(RATES):
        grad_part, grad_taps = conv_backward(
            grad_aspp_low[:, branch_slot + 1],
            low_y,
            aspp_taps[9 * branch_slot : 9 * branch_slot + 9],
            dilation,
            span_dev,
            device,
        )
        grad_y = grad_y + grad_part
        tap_grads.append(grad_taps)
    grad_three, gain_three, shift_three, _ = norm_backward(grad_y, kept_three, 2, no_extra)
    grad_three_low = grad_three.astype(jnp.bfloat16)
    grad_expand = contract_cols(grad_three_low, low_two)
    grad_two_act = contract_rows(expand_w, grad_three_low)
    grad_two, gain_two, shift_two, _ = norm_backward(grad_two_act, kept_two, 1, no_extra)
    grad_one_part, grad_middle = conv_backward(
        grad_two.astype(jnp.bfloat16), low_one, middle, 4, span_dev, device
    )
    grad_one, gain_one, shift_one, _ = norm_backward(grad_one_part, kept_one, 0, no_extra)
    grad_reduce = contract_cols(grad_one.astype(jnp.bfloat16), masked_in)
    flat_aspp = pack_quarters(
        [
            (grad_one_w, 0),
            (jnp.concatenate(tap_grads, axis=0), 1),
            (grad_pool, 0),
            (grad_project, 0),
        ],
        trunk_aspp.shape[1] * dp_count,
        quarters,
    )
    flat_neck = pack_quarters(
        [(grad_reduce, 0), (grad_middle, 1), (grad_expand, 0)],
        trunk_neck.shape[1] * dp_count,
        quarters,
    )
    flat_aspp, flat_neck = (
        lax.psum_scatter(
            flat_aspp.astype(jnp.bfloat16), "head", scatter_dimension=0, tiled=True
        ).astype(jnp.float32),
        lax.psum_scatter(
            flat_neck.astype(jnp.bfloat16), "head", scatter_dimension=0, tiled=True
        ).astype(jnp.float32),
    )
    shard_aspp, shard_neck = (
        lax.psum_scatter(flat_aspp, "dp", scatter_dimension=1, tiled=True),
        lax.psum_scatter(flat_neck, "dp", scatter_dimension=1, tiled=True),
    )
    grad_norms = jnp.stack(
        [
            jnp.concatenate([gain_one, gain_two, gain_three, gain_aspp, gain_proj]),
            jnp.concatenate([shift_one, shift_two, shift_three, shift_aspp, shift_proj]),
        ]
    )
    local_square = jnp.sum(shard_aspp * shard_aspp) + jnp.sum(shard_neck * shard_neck)
    total_square = (
        lax.psum(local_square, ("dp", "head"))
        + jnp.sum(grad_norms * grad_norms)
        + jnp.sum(dec_grad * dec_grad)
        + jnp.sum(grad_logvar * grad_logvar)
    )
    grad_norm = jnp.sqrt(total_square)
    factor = jnp.minimum(1.0, CLIP_LIMIT / grad_norm)
    aspp_out = adam_step(trunk_aspp, aspp_first, aspp_second, shard_aspp, factor, 0.04, 0.01)
    neck_out = adam_step(trunk_neck, neck_first, neck_second, shard_neck, factor, 0.04, 0.01)
    norm_out = adam_step(norm_params, norm_first, norm_second, grad_norms, factor, 0.6, 0.0)
    dec_out = adam_step(decoders, decoder_first, decoder_second, dec_grad, factor, 0.12, 0.01)
    log_out = adam_step(log_vars, log_first, log_second, grad_logvar, factor, 0.5, 0.0)
    return (
        total_loss,
        grad_norm,
        aspp_out[0],
        aspp_out[1],
        aspp_out[2],
        neck_out[0],
        neck_out[1],
        neck_out[2],
        norm_out[0],
        norm_out[1],
        norm_out[2],
        dec_out[0],
        dec_out[1],
        dec_out[2],
        log_out[0],
        log_out[1],
        log_out[2],
    )


def solution(mesh):
    placed = (
        P(None, ("dp", "head")),
        P(),
        P(),
        P("dp"),
        P(None, "dp"),
        P("dp"),
        P("dp"),
        P("head", "dp", None),
        P("head", "dp", None),
        P("head", "dp", None),
        P("head", "dp", None),
        P("head", "dp", None),
        P("head", "dp", None),
        P(),
        P(),
        P(),
        P(),
        P(),
        P(),
        P(),
        P(),
        P(),
    )
    return jax.shard_map(
        shards,
        mesh=mesh,
        in_specs=placed,
        out_specs=(
            P(),
            P(),
            P("head", "dp", None),
            P("head", "dp", None),
            P("head", "dp", None),
            P("head", "dp", None),
            P("head", "dp", None),
            P("head", "dp", None),
            P(),
            P(),
            P(),
            P(),
            P(),
            P(),
            P(),
            P(),
            P(),
        ),
        check_vma=False,
    )
```

profile of v0, /device:TPU:0, one launch (start us, length us, event | category | flops | bytes accessed | tf_op | source)
XLA Modules:
  0.0 3557.8 jit_solution(2449630976511181768)
XLA Ops:
  11.8 29.9 all-gather.6.cloned.1.call-done
  51.2 44.7 %all-gather.10.cloned.1.call-done = bf16[1,30336,128]{2,1,0:T(8,128)(2,1)} async-done(((bf16[1,3792,128]{2,1,0:T(8,128)(2,1)}), bf16[1,30336,128]{2,1,0:T(8,128)(2,1)}) %all-gather.10.cloned.1.call-update) | async-done | bytes 7766032 | tf_op jit(solution)/shard_map/all_gather | solution.py:212
  96.0 159.7 %all-gather.8.cloned.1.call-done = bf16[4,8704,128]{2,1,0:T(8,128)(2,1)} async-done(((bf16[1,8704,128]{2,1,0:T(8,128)(2,1)}), bf16[4,8704,128]{2,1,0:T(8,128)(2,1)}) %all-gather.8.cloned.1.call-update) | async-done | bytes 8912912 | tf_op jit(solution)/shard_map/all_gather | solution.py:217
  255.7 31.4 copy.330
  301.6 70.1 %all-reduce.58 = (f32[512]{0:T(512)S(1)}, f32[512]{0:T(512)S(1)}) all-reduce(f32[512]{0:T(512)S(1)} %get-tuple-element.28, f32[512]{0:T(512)S(1)} %get-tuple-element.27), channel_id=1, replica_groups=mesh['dp'=8,'head'=4] {'dp','head'}, use_global_device_ids=true, to_apply=%region_4.5 | all-reduce | flops 1024 | bytes 8192 | tf_op jit(solution)/shard_map/psum | solution.py:247
  374.6 5.5 collective-permute-start
  393.2 39.7 %collective-permute-done.1 = bf16[512,512]{0,1:T(8,128)(2,1)} collective-permute-done((bf16[512,512]{0,1:T(8,128)(2,1)S(1)}, bf16[512,512]{0,1:T(8,128)(2,1)}, u32[]{:S(2)}, u32[]{:S(2)}) %collective-permute-start.1) | collective-permute-done | bytes 524320 | tf_op jit(solution)/shard_map/ppermute | solution.py:27
  441.8 76.1 %all-reduce.57 = (f32[512]{0:T(512)S(1)}, f32[512]{0:T(512)S(1)}) all-reduce(f32[512]{0:T(512)S(1)} %get-tuple-element.26, f32[512]{0:T(512)S(1)} %get-tuple-element.25), channel_id=1, replica_groups=mesh['dp'=8,'head'=4] {'dp','head'}, use_global_device_ids=true, to_apply=%region_8.9 | all-reduce | flops 1024 | bytes 8192 | tf_op jit(solution)/shard_map/psum | solution.py:247
  524.4 77.8 %all-reduce.56 = (f32[2048]{0:T(1024)S(1)}, f32[2048]{0:T(1024)S(1)}) all-reduce(f32[2048]{0:T(1024)S(1)} %get-tuple-element.18, f32[2048]{0:T(1024)S(1)} %get-tuple-element.17), channel_id=1, replica_groups=mesh['dp'=8,'head'=4] {'dp','head'}, use_global_device_ids=true, to_apply=%region_10.11 | all-reduce | flops 4096 | bytes 32768 | tf_op jit(solution)/shard_map/psum | solution.py:247
  610.3 8.1 collective-permute-start.6
  637.9 162.8 %collective-permute-done.7 = bf16[2048,512]{0,1:T(8,128)(2,1)S(1)} collective-permute-done((bf16[2048,512]{0,1:T(8,128)(2,1)S(1)}, bf16[2048,512]{0,1:T(8,128)(2,1)S(1)}, u32[]{:S(2)}, u32[]{:S(2)}) %collective-permute-start.7) | collective-permute-done | bytes 2097184 | tf_op jit(solution)/shard_map/ppermute | solution.py:27
  811.7 131.4 %collective-permute-done.5 = bf16[2048,512]{0,1:T(8,128)(2,1)S(1)} collective-permute-done((bf16[2048,512]{0,1:T(8,128)(2,1)S(1)}, bf16[2048,512]{0,1:T(8,128)(2,1)S(1)}, u32[]{:S(2)}, u32[]{:S(2)}) %collective-permute-start.5) | collective-permute-done | bytes 2097184 | tf_op jit(solution)/shard_map/ppermute | solution.py:27
  962.3 89.2 %all-gather.12.cloned.1.call-done = bf16[4,30336,128]{2,1,0:T(8,128)(2,1)} async-done(((bf16[1,30336,128]{2,1,0:T(8,128)(2,1)}), bf16[4,30336,128]{2,1,0:T(8,128)(2,1)}) %all-gather.12.cloned.1.call-update) | async-done | bytes 31064080 | tf_op jit(solution)/shard_map/all_gather | solution.py:216
  1051.5 147.3 %copy.328 = bf16[1,4,30336,128]{3,1,2,0:T(4,128)(2,1)} copy(bf16[1,4,30336,128]{3,2,1,0:T(8,128)(2,1)} %bitcast.803) | data formatting | bytes 62128128
  1204.5 19.6 slice.612
  1224.1 19.7 copy.294
  1243.8 13.7 fusion.230
  1257.6 6.6 fusion.231
  1323.8 156.3 %all-reduce.55 = (f32[2,2048]{1,0:T(2,128)S(1)}, f32[1024]{0:T(1024)S(1)}, f32[1024]{0:T(1024)S(1)}) all-reduce(f32[2,2048]{1,0:T(2,128)S(1)} %broadcast_multiply_fusion, f32[1024]{0:T(1024)S(1)} %bitcast.988, f32[1024]{0:T(1024)S(1)} %bitcast.989), channel_id=1, replica_groups=mesh['dp'=8,'head'=4] {'dp','head'}, use_global_device_ids=true, to_apply=%region_18.19 | all-reduce | flops 6144 | bytes 49152 | tf_op jit(solution)/shard_map/psum | solution.py:247
  1485.5 38.6 %all-reduce.54 = (f32[256]{0:T(256)S(1)}, f32[256]{0:T(256)S(1)}) all-reduce(f32[256]{0:T(256)S(1)} %get-tuple-element.34, f32[256]{0:T(256)S(1)} %get-tuple-element.33), channel_id=1, replica_groups=mesh['dp'=8,'head'=4] {'dp','head'}, use_global_device_ids=true, to_apply=%region_20.21 | all-reduce | flops 512 | bytes 4096 | tf_op jit(solution)/shard_map/psum | solution.py:247
  1529.5 26.0 all-gather.14.cloned.1.call-done
  1563.4 40.8 %psum.194 = f32[1]{0:T(128)} all-reduce(f32[1]{0:T(128)} %bitcast.108), channel_id=1, replica_groups=mesh['dp'=8,'head'=4] {'dp','head'}, use_global_device_ids=true, to_apply=%region_31.32 | all-reduce | flops 1 | bytes 8 | tf_op jit(solution)/shard_map/psum | solution.py:347
  1621.7 25.8 reduce-scatter.6.cloned.1.call-done
  1649.6 38.8 %all-reduce.53 = (f32[256]{0:T(256)S(1)}, f32[256]{0:T(256)S(1)}) all-reduce(f32[256]{0:T(256)S(1)} %get-tuple-element.36, f32[256]{0:T(256)S(1)} %get-tuple-element.35), channel_id=1, replica_groups=mesh['dp'=8,'head'=4] {'dp','head'}, use_global_device_ids=true, to_apply=%region_38.39 | all-reduce | flops 512 | bytes 4096 | tf_op jit(solution)/shard_map/psum | solution.py:268
  1696.3 40.5 %all-reduce.52 = (f32[2,256]{1,0:T(2,128)S(1)}, f32[1024]{0:T(1024)S(1)}, f32[1024]{0:T(1024)S(1)}) all-reduce(f32[2,256]{1,0:T(2,128)S(1)} %broadcast_multiply_fusion.1, f32[1024]{0:T(1024)S(1)} %bitcast.986, f32[1024]{0:T(1024)S(1)} %bitcast.987), channel_id=1, replica_groups=mesh['dp'=8,'head'=4] {'dp','head'}, use_global_device_ids=true, to_apply=%region_44.45 | all-reduce | flops 2560 | bytes 20480 | tf_op jit(solution)/shard_map/psum | solution.py:268
  1742.5 6.6 collective-permute-start.9
  1750.5 5.9 collective-permute-start.11
  1788.5 5.9 collective-permute-start.13
  1847.7 39.0 %fusion.215 = (f32[2048]{0:T(1024)S(1)}, f32[2048]{0:T(1024)S(1)}, f32[2048,512]{0,1:T(8,128)}) fusion(f32[2048]{0:T(1024)S(1)} %copy-done.232, f32[512,2048]{1,0:T(8,128)S(1)} %copy-done.4, f32[2048]{0:T(1024)S(1)} %copy-done.228, bf16[2048,512]{0,1:T(8,128)(2,1)} %copy-done.18, bf16[512]{0:T(512)(128)(2,1)S(1)} %copy-done.276, f32[2048]{0:T(1024)S(1)} %bitcast.972, ...), kind=kOutput, calls=%fused_computation.486 | convolution fusion | flops 587198464 | bytes 125103104 | tf_op jit(solution)/shard_map/dot_general | solution.py:40
  1886.6 40.4 %all-reduce.51 = (f32[2048]{0:T(1024)S(1)}, f32[2048]{0:T(1024)S(1)}) all-reduce(f32[2048]{0:T(1024)S(1)} %get-tuple-element.20, f32[2048]{0:T(1024)S(1)} %get-tuple-element.19), channel_id=1, replica_groups=mesh['dp'=8,'head'=4] {'dp','head'}, use_global_device_ids=true, to_apply=%region_51.52 | all-reduce | flops 4096 | bytes 32768 | tf_op jit(solution)/shard_map/psum | solution.py:268
  1938.8 42.1 %all-reduce.50 = (f32[512]{0:T(512)S(1)}, f32[512]{0:T(512)S(1)}) all-reduce(f32[512]{0:T(512)S(1)} %get-tuple-element.32, f32[512]{0:T(512)S(1)} %get-tuple-element.31), channel_id=1, replica_groups=mesh['dp'=8,'head'=4] {'dp','head'}, use_global_device_ids=true, to_apply=%region_55.56 | all-reduce | flops 1024 | bytes 8192 | tf_op jit(solution)/shard_map/psum | solution.py:268
  1985.1 5.6 collective-permute-start.15
  2029.7 16.2 copy.303
  2055.3 43.8 %all-reduce.49 = (f32[512]{0:T(512)S(1)}, f32[512]{0:T(512)S(1)}) all-reduce(f32[512]{0:T(512)S(1)} %get-tuple-element.30, f32[512]{0:T(512)S(1)} %get-tuple-element.29), channel_id=1, replica_groups=mesh['dp'=8,'head'=4] {'dp','head'}, use_global_device_ids=true, to_apply=%region_59.60 | all-reduce | flops 1024 | bytes 8192 | tf_op jit(solution)/shard_map/psum | solution.py:268
  2109.4 42.9 %maximum_bitcast_fusion.1 = bf16[1,4,8704,128]{3,1,2,0:T(4,128)(2,1)S(1)} fusion(bf16[4,262144]{1,0:T(4,128)(2,1)S(1)} %copy-done.63, bf16[4,589824]{1,0:T(4,128)(2,1)} %bitcast.812, bf16[4,262144]{1,0:T(4,128)(2,1)} %reshape_reshape.18), kind=kLoop, calls=%fused_computation.5 | loop fusion | flops 26738688 | bytes 17825792
  2152.3 7.0 copy.329
  2260.7 9.4 copy-done.9
  2270.2 19.6 copy.209
  2289.8 36.0 %copy.299 = bf16[1,4,1728,2048]{3,1,2,0:T(4,128)(2,1)} copy(bf16[1,4,1728,2048]{3,2,1,0:T(8,128)(2,1)} %bitcast.795) | data formatting | bytes 56623104
  2325.9 328.0 %maximum_bitcast_fusion = bf16[1,4,30336,128]{3,1,2,0:T(4,128)(2,1)} fusion(bf16[4,81920]{1,0:T(4,128)(2,1)S(1)} %copy-done.169, bf16[4,131072]{1,0:T(4,128)(2,1)S(1)} %copy-done.117, bf16[4,3538944]{1,0:T(4,128)(2,1)} %bitcast.796, bf16[4,131072]{1,0:T(4,128)(2,1)S(1)} %copy-done.116), kind=kLoop, calls=%fused_computation.2 | loop fusion | flops 124256256 | bytes 62128128
  2653.9 21.8 copy.327
  2683.5 501.2 %reduce-scatter.8.cloned.1.call-done = bf16[1,30336,128]{2,1,0:T(8,128)(2,1)} async-done(((bf16[4,30336,128]{2,1,0:T(8,128)(2,1)}), bf16[1,30336,128]{2,1,0:T(8,128)(2,1)}) %reduce-scatter.8.cloned.1.call-update) | async-done | bytes 7766032 | tf_op jit(solution)/shard_map/reduce_scatter | solution.py:440
  3184.7 9.0 convert_element_type.229
  3198.5 122.3 %all-reduce.61.cloned.1.call-done = f32[790,256]{1,0:T(8,128)} async-done(((f32[790,256]{1,0:T(8,128)}), f32[790,256]{1,0:T(8,128)}) %all-reduce.61.cloned.1.call-update) | async-done | bytes 808976 | tf_op jit(solution)/shard_map/psum | solution.py:268
  3322.9 54.3 %reduce-scatter.14.cloned.1.call-done = f32[1,1088,128]{2,1,0:T(8,128)} async-done(((f32[1,8704,128]{2,1,0:T(8,128)}), f32[1,1088,128]{2,1,0:T(8,128)}) %reduce-scatter.14.cloned.1.call-update) | async-done | bytes 557072 | tf_op jit(solution)/shard_map/reduce_scatter | solution.py:449
  3379.0 110.4 %reduce-scatter.10.cloned.1.call-done = f32[1,3792,128]{2,1,0:T(8,128)} async-done(((f32[1,30336,128]{2,1,0:T(8,128)}), f32[1,3792,128]{2,1,0:T(8,128)}) %reduce-scatter.10.cloned.1.call-update) | async-done | bytes 1941520 | tf_op jit(solution)/shard_map/reduce_scatter | solution.py:448
  3494.0 39.3 %all-reduce.48 = (f32[3]{0:T(128)S(1)}, f32[]{:T(128)}) all-reduce(f32[3]{0:T(128)S(1)} %maximum_multiply_fusion, f32[]{:T(128)S(6)} %add.891), channel_id=1, replica_groups=mesh['dp'=8,'head'=4] {'dp','head'}, use_global_device_ids=true, to_apply=%region_29.30 | all-reduce | flops 4 | bytes 32 | tf_op jit(solution)/shard_map/psum | solution.py:347
  3539.3 6.3 multiply_subtract_fusion
  (1060 shorter events, 519.3 us)
Async XLA Ops:
  7.2 34.5 all-gather.6.cloned.1.call-start
  9.0 86.9 %all-gather.10.cloned.1.call-start = ((), (), s32[]{:S(2)}) async-start(), calls=%async_computation.7 | async-start | bytes 8736768 | tf_op jit(solution)/shard_map/all_gather | solution.py:212
  11.7 244.0 %all-gather.8.cloned.1.call-start = ((), (), s32[]{:S(2)}) async-start(), calls=%async_computation.6 | async-start | bytes 11141120 | tf_op jit(solution)/shard_map/all_gather | solution.py:217
  41.7 1009.8 %all-gather.12.cloned.1.call-start = ((), (), s32[]{:S(2)}) async-start(), calls=%async_computation.8 | async-start | bytes 38830080 | tf_op jit(solution)/shard_map/all_gather | solution.py:216
  45.9 252.6 %copy-start.18 = (bf16[2048,512]{0,1:T(8,128)(2,1)}, bf16[2048,512]{0,1:T(8,128)(2,1)S(1)}, u32[]{:S(2)}) copy-start(bf16[2048,512]{0,1:T(8,128)(2,1)S(1)} %copy.162) | copy-start | bytes 6291460
  48.7 589.1 %copy-start.305 = (f32[2]{0:T(128)}, f32[2]{0:T(128)S(1)}, u32[]{:S(2)}) copy-start(f32[2]{0:T(128)S(1)} %compare_convert_fusion) | copy-start | bytes 28
  50.0 554.2 %copy-start.275 = (bf16[512]{0:T(512)(128)(2,1)}, bf16[512]{0:T(512)(128)(2,1)S(1)}, u32[]{:S(2)}) copy-start(bf16[512]{0:T(512)(128)(2,1)S(1)} %get-tuple-element.222) | copy-start | bytes 3076
  51.1 321.8 %copy-start.260 = (f32[1,512]{1,0:T(1,128)}, f32[1,512]{1,0:T(1,128)S(1)}, u32[]{:S(2)}) copy-start(f32[1,512]{1,0:T(1,128)S(1)} %get-tuple-element.199) | copy-start | bytes 6148
  51.2 321.8 %copy-start.285 = (f32[1,512]{1,0:T(1,128)}, f32[1,512]{1,0:T(1,128)S(1)}, u32[]{:S(2)}) copy-start(f32[1,512]{1,0:T(1,128)S(1)} %get-tuple-element.198) | copy-start | bytes 6148
  51.2 468.0 %copy-start.289 = (f32[1,512]{1,0:T(1,128)}, f32[1,512]{1,0:T(1,128)S(1)}, u32[]{:S(2)}) copy-start(f32[1,512]{1,0:T(1,128)S(1)} %get-tuple-element.200) | copy-start | bytes 6148
  51.2 468.0 %copy-start.307 = (f32[1,512]{1,0:T(1,128)}, f32[1,512]{1,0:T(1,128)S(1)}, u32[]{:S(2)}) copy-start(f32[1,512]{1,0:T(1,128)S(1)} %get-tuple-element.197) | copy-start | bytes 6148
  51.2 553.0 %copy-start.233 = (f32[1,2048]{1,0:T(1,128)}, f32[1,2048]{1,0:T(1,128)S(1)}, u32[]{:S(2)}) copy-start(f32[1,2048]{1,0:T(1,128)S(1)} %get-tuple-element.201) | copy-start | bytes 24580
  51.2 553.0 %copy-start.237 = (f32[1,2048]{1,0:T(1,128)}, f32[1,2048]{1,0:T(1,128)S(1)}, u32[]{:S(2)}) copy-start(f32[1,2048]{1,0:T(1,128)S(1)} %get-tuple-element.202) | copy-start | bytes 24580
  96.0 1459.5 %all-gather.14.cloned.1.call-start = ((), (), s32[]{:S(2)}) async-start(), calls=%async_computation.9 | async-start | bytes 1310720 | tf_op jit(solution)/shard_map/all_gather | solution.py:322
  373.3 59.6 %collective-permute-start.1 = (bf16[512,512]{0,1:T(8,128)(2,1)S(1)}, bf16[512,512]{0,1:T(8,128)(2,1)}, u32[]{:S(2)}, u32[]{:S(2)}) collective-permute-start(bf16[512,512]{0,1:T(8,128)(2,1)S(1)} %multiply_convert_fusion.6), channel_id=1, source_target_pairs={{1,0},{2,1},{3,2},{4,3},{5,4},{6,5},{7,6},{8,7},{9,8},{10,9},{11,1... | collective-permute-start | bytes 1572872 | tf_op jit(solution)/shard_map/ppermute | solution.py:27
  374.6 59.6 %collective-permute-start = (bf16[512,512]{0,1:T(8,128)(2,1)S(1)}, bf16[512,512]{0,1:T(8,128)(2,1)}, u32[]{:S(2)}, u32[]{:S(2)}) collective-permute-start(bf16[512,512]{0,1:T(8,128)(2,1)S(1)} %multiply_convert_fusion.6), channel_id=1, source_target_pairs={{0,1},{1,2},{2,3},{3,4},{4,5},{5,6},{6,7},{7,8},{8,9},{9,10},{10,1... | collective-permute-start | bytes 1572872 | tf_op jit(solution)/shard_map/ppermute | solution.py:27
  608.6 696.7 %copy-start = (bf16[2048,512]{0,1:T(8,128)(2,1)}, bf16[2048,512]{0,1:T(8,128)(2,1)S(1)}, u32[]{:S(2)}) copy-start(bf16[2048,512]{0,1:T(8,128)(2,1)S(1)} %get-tuple-element.98) | copy-start | bytes 6291460
  608.6 192.1 %collective-permute-start.7 = (bf16[2048,512]{0,1:T(8,128)(2,1)S(1)}, bf16[2048,512]{0,1:T(8,128)(2,1)S(1)}, u32[]{:S(2)}, u32[]{:S(2)}) collective-permute-start(bf16[2048,512]{0,1:T(8,128)(2,1)S(1)} %get-tuple-element.98), channel_id=1, source_target_pairs={{9,0},{10,1},{11,2},{12,3},{13,4},{14,5},{15,6},{16,7},{17,8},{18,... | collective-permute-start | bytes 6291464 | tf_op jit(solution)/shard_map/ppermute | solution.py:27
  610.3 194.8 %collective-permute-start.6 = (bf16[2048,512]{0,1:T(8,128)(2,1)S(1)}, bf16[2048,512]{0,1:T(8,128)(2,1)S(1)}, u32[]{:S(2)}, u32[]{:S(2)}) collective-permute-start(bf16[2048,512]{0,1:T(8,128)(2,1)S(1)} %get-tuple-element.98), channel_id=1, source_target_pairs={{0,9},{1,10},{2,11},{3,12},{4,13},{5,14},{6,15},{7,16},{8,17},{9,1... | collective-permute-start | bytes 6291464 | tf_op jit(solution)/shard_map/ppermute | solution.py:27
  618.4 324.7 %collective-permute-start.5 = (bf16[2048,512]{0,1:T(8,128)(2,1)S(1)}, bf16[2048,512]{0,1:T(8,128)(2,1)S(1)}, u32[]{:S(2)}, u32[]{:S(2)}) collective-permute-start(bf16[2048,512]{0,1:T(8,128)(2,1)S(1)} %get-tuple-element.98), channel_id=1, source_target_pairs={{6,0},{7,1},{8,2},{9,3},{10,4},{11,5},{12,6},{13,7},{14,8},{15,9},... | collective-permute-start | bytes 6291464 | tf_op jit(solution)/shard_map/ppermute | solution.py:27
  619.7 326.5 %collective-permute-start.4 = (bf16[2048,512]{0,1:T(8,128)(2,1)S(1)}, bf16[2048,512]{0,1:T(8,128)(2,1)S(1)}, u32[]{:S(2)}, u32[]{:S(2)}) collective-permute-start(bf16[2048,512]{0,1:T(8,128)(2,1)S(1)} %get-tuple-element.98), channel_id=1, source_target_pairs={{0,6},{1,7},{2,8},{3,9},{4,10},{5,11},{6,12},{7,13},{8,14},{9,15},... | collective-permute-start | bytes 6291464 | tf_op jit(solution)/shard_map/ppermute | solution.py:27
  625.0 327.4 %collective-permute-start.3 = (bf16[2048,512]{0,1:T(8,128)(2,1)S(1)}, bf16[2048,512]{0,1:T(8,128)(2,1)S(1)}, u32[]{:S(2)}, u32[]{:S(2)}) collective-permute-start(bf16[2048,512]{0,1:T(8,128)(2,1)S(1)} %get-tuple-element.98), channel_id=1, source_target_pairs={{3,0},{4,1},{5,2},{6,3},{7,4},{8,5},{9,6},{10,7},{11,8},{12,9},{13... | collective-permute-start | bytes 6291464 | tf_op jit(solution)/shard_map/ppermute | solution.py:27
  800.6 154.9 %collective-permute-start.2 = (bf16[2048,512]{0,1:T(8,128)(2,1)S(1)}, bf16[2048,512]{0,1:T(8,128)(2,1)S(1)}, u32[]{:S(2)}, u32[]{:S(2)}) collective-permute-start(bf16[2048,512]{0,1:T(8,128)(2,1)S(1)} %get-tuple-element.98), channel_id=1, source_target_pairs={{0,3},{1,4},{2,5},{3,6},{4,7},{5,8},{6,9},{7,10},{8,11},{9,12},{10... | collective-permute-start | bytes 6291464 | tf_op jit(solution)/shard_map/ppermute | solution.py:27
  1323.3 156.8 %copy-start.22 = (bf16[256,2048]{1,0:T(8,128)(2,1)S(1)}, bf16[256,2048]{1,0:T(8,128)(2,1)}, u32[]{:S(2)}) copy-start(bf16[256,2048]{1,0:T(8,128)(2,1)} %reshape.961) | copy-start | bytes 3145732
  1323.3 158.8 %copy-start.239 = (f32[4,256]{1,0:T(4,128)S(1)}, f32[4,256]{1,0:T(4,128)}, u32[]{:S(2)}) copy-start(f32[4,256]{1,0:T(4,128)} %reshape.916) | copy-start | bytes 12292
  1323.3 159.4 %copy-start.243 = (f32[4,256]{1,0:T(4,128)S(1)}, f32[4,256]{1,0:T(4,128)}, u32[]{:S(2)}) copy-start(f32[4,256]{1,0:T(4,128)} %reshape.960) | copy-start | bytes 12292
  1526.3 121.3 %reduce-scatter.6.cloned.1.call-start = ((), (), s32[]{:S(2)}) async-start(), calls=%async_computation.10 | async-start | bytes 1310720 | tf_op jit(solution)/shard_map/reduce_scatter | solution.py:374
  1620.6 1058.5 %reduce-scatter.12.cloned.1.call-start = ((), (), s32[]{:S(2)}) async-start(), calls=%async_computation.13 | async-start | bytes 11141120 | tf_op jit(solution)/shard_map/reduce_scatter | solution.py:443
  1741.2 47.3 %collective-permute-start.8 = (bf16[256,512]{0,1:T(8,128)(2,1)S(1)}, bf16[256,512]{0,1:T(8,128)(2,1)}, u32[]{:S(2)}, u32[]{:S(2)}) collective-permute-start(bf16[256,512]{0,1:T(8,128)(2,1)S(1)} %get-tuple-element.158), channel_id=1, source_target_pairs={{3,0},{4,1},{5,2},{6,3},{7,4},{8,5},{9,6},{10,7},{11,8},{12,9},{13... | collective-permute-start | bytes 786440 | tf_op jit(solution)/shard_map/ppermute | solution.py:27
  1742.5 52.9 %collective-permute-start.9 = (bf16[256,512]{0,1:T(8,128)(2,1)S(1)}, bf16[256,512]{0,1:T(8,128)(2,1)S(1)}, u32[]{:S(2)}, u32[]{:S(2)}) collective-permute-start(bf16[256,512]{0,1:T(8,128)(2,1)S(1)} %get-tuple-element.158), channel_id=1, source_target_pairs={{0,3},{1,4},{2,5},{3,6},{4,7},{5,8},{6,9},{7,10},{8,11},{9,12},{10... | collective-permute-start | bytes 786440 | tf_op jit(solution)/shard_map/ppermute | solution.py:27
  1749.1 46.7 %collective-permute-start.10 = (bf16[256,512]{0,1:T(8,128)(2,1)}, bf16[256,512]{0,1:T(8,128)(2,1)}, u32[]{:S(2)}, u32[]{:S(2)}) collective-permute-start(bf16[256,512]{0,1:T(8,128)(2,1)} %get-tuple-element.159), channel_id=1, source_target_pairs={{6,0},{7,1},{8,2},{9,3},{10,4},{11,5},{12,6},{13,7},{14,8},{15,9},... | collective-permute-start | bytes 786440 | tf_op jit(solution)/shard_map/ppermute | solution.py:27
  1750.5 49.4 %collective-permute-start.11 = (bf16[256,512]{0,1:T(8,128)(2,1)}, bf16[256,512]{0,1:T(8,128)(2,1)}, u32[]{:S(2)}, u32[]{:S(2)}) collective-permute-start(bf16[256,512]{0,1:T(8,128)(2,1)} %get-tuple-element.159), channel_id=1, source_target_pairs={{0,6},{1,7},{2,8},{3,9},{4,10},{5,11},{6,12},{7,13},{8,14},{9,15},... | collective-permute-start | bytes 786440 | tf_op jit(solution)/shard_map/ppermute | solution.py:27
  1770.5 36.3 %collective-permute-start.12 = (bf16[256,512]{0,1:T(8,128)(2,1)}, bf16[256,512]{0,1:T(8,128)(2,1)S(1)}, u32[]{:S(2)}, u32[]{:S(2)}) collective-permute-start(bf16[256,512]{0,1:T(8,128)(2,1)} %get-tuple-element.160), channel_id=1, source_target_pairs={{9,0},{10,1},{11,2},{12,3},{13,4},{14,5},{15,6},{16,7},{17,8},{18,... | collective-permute-start | bytes 786440 | tf_op jit(solution)/shard_map/ppermute | solution.py:27
  1788.5 25.0 collective-permute-start.13
  1983.8 16.0 collective-permute-start.14
  1985.1 23.5 collective-permute-start.15
  2159.4 1025.4 %reduce-scatter.8.cloned.1.call-start = ((), (), s32[]{:S(2)}) async-start(), calls=%async_computation.11 | async-start | bytes 38830080 | tf_op jit(solution)/shard_map/reduce_scatter | solution.py:440
  2675.8 644.9 %all-reduce.61.cloned.1.call-start = ((), (), s32[]{:S(2)}) async-start(), calls=%async_computation.15 | async-start | bytes 1622016 | tf_op jit(solution)/shard_map/psum | solution.py:268
  2679.1 698.1 %reduce-scatter.14.cloned.1.call-start = ((), (), s32[]{:S(2)}) async-start(), calls=%async_computation.14 | async-start | bytes 5013504 | tf_op jit(solution)/shard_map/reduce_scatter | solution.py:449
  2683.4 805.9 %reduce-scatter.10.cloned.1.call-start = ((), (), s32[]{:S(2)}) async-start(), calls=%async_computation.12 | async-start | bytes 17473536 | tf_op jit(solution)/shard_map/reduce_scatter | solution.py:448
  3193.9 129.0 %copy-start.302 = (f32[256]{0:T(256)S(1)}, f32[256]{0:T(256)}, u32[]{:S(2)}) copy-start(f32[256]{0:T(256)} %copy-done.301) | copy-start | bytes 3076
  3193.9 339.3 %copy-start.298 = (f32[3]{0:T(128)S(1)}, f32[3]{0:T(128)}, u32[]{:S(2)}) copy-start(f32[3]{0:T(128)} %param.41) | copy-start | bytes 40
  3193.9 344.0 %copy-start.230 = (f32[2,4352]{1,0:T(2,128)S(1)}, f32[2,4352]{1,0:T(2,128)}, u32[]{:S(2)}) copy-start(f32[2,4352]{1,0:T(2,128)} %param.35) | copy-start | bytes 104452
  3193.9 344.0 %copy-start.245 = (f32[2,4352]{1,0:T(2,128)S(1)}, f32[2,4352]{1,0:T(2,128)}, u32[]{:S(2)}) copy-start(f32[2,4352]{1,0:T(2,128)} %param.36) | copy-start | bytes 104452
  3193.9 344.0 %copy-start.246 = (f32[2,4352]{1,0:T(2,128)S(1)}, f32[2,4352]{1,0:T(2,128)}, u32[]{:S(2)}) copy-start(f32[2,4352]{1,0:T(2,128)} %param.37) | copy-start | bytes 104452
  3193.9 344.8 %copy-start.309 = (f32[3]{0:T(128)S(1)}, f32[3]{0:T(128)}, u32[]{:S(2)}) copy-start(f32[3]{0:T(128)} %param.42) | copy-start | bytes 40
  3194.0 344.8 %copy-start.310 = (f32[3]{0:T(128)S(1)}, f32[3]{0:T(128)}, u32[]{:S(2)}) copy-start(f32[3]{0:T(128)} %param.43) | copy-start | bytes 40
  3194.0 345.3 %copy-start.80 = (f32[1,3792,128]{2,1,0:T(8,128)S(1)}, f32[1,3792,128]{2,1,0:T(8,128)}, u32[]{:S(2)}) copy-start(f32[1,3792,128]{2,1,0:T(8,128)} %param.29) | copy-start | bytes 5824516
  (292 other events, 3277.3 us)
Sparse Core Ops, SparseCore 0:
  10.5 31.1 all-gather.5
  44.1 51.7 all-gather.9
  97.5 158.1 all-gather.7
  257.2 794.2 all-gather.11
  1526.4 29.0 all-gather.13
  1620.8 26.7 reduce-scatter.5
  2159.5 152.4 reduce-scatter.11
  2675.9 508.7 reduce-scatter.7
  3190.6 130.1 all-reduce.60
  3324.0 53.0 reduce-scatter.13
  3381.3 108.0 reduce-scatter.9
where the time goes:
time: 3570 us; the launch traced here: 3560 us
  waiting for transfers between devices  1500 us (42%)
  blocking collectives  705 us (20%)
  local copies, waits for them, and re-layouts  585 us (16%)
  other arithmetic  474 us (13%)
  matrix products  215 us (6%)
  starting transfers between devices  55.7 us (2%)
    reduce_scatter x1, waiting for transfers between devices, shards(): lax.psum_scatter(flat_aspp.astype(jnp.bfloat16), 'head', scatter_dimensio...  501 us
    psum x5, blocking collectives, norm_forward(): lax.psum((to_full(arrange(local_sum, groups)), to_full(arrange(local_squa...  419 us
    unnamed x5, other arithmetic  372 us
    unnamed x659, local copies, waits for them, and re-layouts  358 us
    ppermute x16, waiting for transfers between devices, shifted_2(): return lax.ppermute(x, axis, pairs)  335 us
    psum x5, blocking collectives, norm_backward(): lax.psum((to_full(arrange(jnp.sum(grad_out, axis=-1), groups)), to_full(a...  206 us
    all_gather x1, waiting for transfers between devices, shards(): lax.all_gather(held_neck, 'head', axis=0, tiled=True)  160 us
    dot_general x41, matrix products, contract_rows(): lax.dot_general(operand_one, operand_two, (((0,), (0,)), ((), ())), prefe...  125 us
  transfers between devices with their start and end apart: 27, of which 14 were waited for; matrix products, arithmetic and copies ran while one was open for 20% of the time, Pallas kernels for 0%

commit v1 on v0

v1 whole, which is shorter than its diff:
```python
import functools

import jax
import jax.numpy as jnp
from jax import lax
from jax.experimental import pallas as pl
from jax.experimental.pallas import tpu as pltpu
from jax.sharding import PartitionSpec as P

FEAT = 2048
BOT = 512
ASP = 256
CLS = 19
OUTS = 22
WIDTH = 128
CROP_DP = 4
QUAD = 512
STEP = 10

EPSILON = 1e-05
BETA_ONE = 0.9
BETA_TWO = 0.95
ADAM_EPSILON = 1e-08
CLIP_LIMIT = 0.05
RATES = (12, 24, 36)

BF = jnp.bfloat16
F32 = jnp.float32


def silu_slope(pre_norm):
    sigmoid_value = jax.nn.sigmoid(pre_norm)
    return sigmoid_value * (1.0 + pre_norm * (1.0 - sigmoid_value))


def dot(a, b, ca, cb):
    return lax.dot_general(a, b, ((ca, cb), ((), ())), preferred_element_type=F32)


def xor_move(x, axis, mask):
    n = lax.axis_size(axis)
    return lax.ppermute(x, axis, [(i, i ^ mask) for i in range(n)])


def xor_round(x, axis, bits):
    if len(bits) == 1:
        return x + xor_move(x, axis, bits[0])
    one, two = bits
    a = xor_move(x, axis, one)
    b = xor_move(x, axis, two)
    c = xor_move(x, axis, one | two)
    return (x + a) + (b + c)


def sum_crop(x):
    return xor_round(xor_round(x, "dp", (1,)), "dp", (2,))


def rounds_of(first, n):
    bits = []
    while first < n:
        bits.append(first)
        first *= 2
    return [tuple(bits[i : i + 2]) for i in range(0, len(bits), 2)]


def sum_dp(x):
    x = xor_round(x, "dp", (1,))
    for bits in rounds_of(2, lax.axis_size("dp")):
        x = xor_round(x, "dp", bits)
    return x


def sum_head(x):
    for bits in rounds_of(1, lax.axis_size("head")):
        x = xor_round(x, "head", bits)
    return x


def sum_all(x):
    return sum_head(sum_dp(x))


def pack(vectors):
    return jnp.concatenate([v.reshape(-1) for v in vectors])


def unpack(joined, sizes):
    out, at = [], 0
    for size in sizes:
        out.append(joined[at : at + size])
        at += size
    return out


def crop_shift(x, by):
    n = lax.axis_size("dp")
    pairs = [(i, i + by) for i in range(n) if i // CROP_DP == (i + by) // CROP_DP and 0 <= i + by < n]
    return lax.ppermute(x, "dp", pairs)


def line_shift(x, by):
    n = lax.axis_size("head")
    return lax.ppermute(x, "head", [(i, i + by) for i in range(n) if 0 <= i + by < n])


def gather_line(own, z):
    n = lax.axis_size("head")
    left, right = [own], [own]
    for _ in range(n - 1):
        left.append(line_shift(left[-1], 1))
        right.append(line_shift(right[-1], -1))
    blocks = []
    for j in range(n):
        block = None
        for at in range(n):
            source = own if at == j else (left[at - j] if at > j else right[j - at])
            block = source if block is None else jnp.where(z == at, source, block)
        blocks.append(block)
    return blocks


def shift_lanes(tile, by, lanes):
    if by == 0:
        return tile
    rolled = pltpu.roll(tile, (-by) % WIDTH, 1)
    keep = (lanes < WIDTH - by) if by > 0 else (lanes >= -by)
    return jnp.where(keep, rolled, 0.0)


def neck_columns_kernel(flip, ext_ref, out_ref):
    rows = ext_ref.shape[0]
    lanes = lax.broadcasted_iota(jnp.int32, (rows, WIDTH), 1)
    count = ext_ref.shape[1] // WIDTH
    for t in range(count):
        tile = ext_ref[:, t * WIDTH : (t + 1) * WIDTH].astype(F32)
        for j in range(3):
            moved = shift_lanes(tile, (j - 1) * 4, lanes).astype(BF)
            for i in range(3):
                at = t - 4 * i
                if 0 <= at < count - 8:
                    tap = 3 * i + j
                    out_ref[8 - tap if flip else tap, :, at * WIDTH : (at + 1) * WIDTH] = moved


def neck_columns(ext, flip):
    rows, width = ext.shape
    block = 64
    return pl.pallas_call(
        functools.partial(neck_columns_kernel, flip),
        grid=(rows // block,),
        in_specs=[pl.BlockSpec((block, width), lambda i: (i, 0))],
        out_specs=pl.BlockSpec((9, block, width - 1024), lambda i: (0, i, 0)),
        out_shape=jax.ShapeDtypeStruct((9, rows, width - 1024), BF),
        compiler_params=pltpu.CompilerParams(vmem_limit_bytes=40 << 20),
        cost_estimate=pl.CostEstimate(flops=0, bytes_accessed=2 * 12 * rows * width, transcendentals=0),
    )(ext)


def aspp_gather_kernel(p_ref, core_ref, side_ref, pool_ref):
    lanes = lax.broadcasted_iota(jnp.int32, (64, WIDTH), 1)
    core_ref[0] = p_ref[0:64, :]
    pool_sum = jnp.zeros((64, WIDTH), F32)
    for t in range(4):
        part = slice(t * WIDTH, (t + 1) * WIDTH)
        pool_sum = pool_sum + p_ref[64 * 28 : 64 * 29, part]
        for br, rate in enumerate(RATES):
            for i in range(3):
                total = None
                for j in range(3):
                    at = 64 * (1 + 9 * br + 3 * i + j)
                    moved = shift_lanes(p_ref[at : at + 64, part], (j - 1) * rate, lanes)
                    total = moved if total is None else total + moved
                if i == 1:
                    core_ref[1 + br, :, part] = total
                else:
                    side_ref[2 * br + i // 2, 0, :, part] = total.astype(BF)
    pool_ref[0] = pool_sum


def aspp_gather(products):
    rows, width = products.shape
    quads = width // QUAD
    return pl.pallas_call(
        aspp_gather_kernel,
        grid=(quads,),
        in_specs=[pl.BlockSpec((rows, QUAD), lambda a: (0, a))],
        out_specs=[
            pl.BlockSpec((4, 64, QUAD), lambda a: (0, 0, a)),
            pl.BlockSpec((6, 1, 64, QUAD), lambda a: (0, a, 0, 0)),
            pl.BlockSpec((1, 64, WIDTH), lambda a: (a, 0, 0)),
        ],
        out_shape=[
            jax.ShapeDtypeStruct((4, 64, width), F32),
            jax.ShapeDtypeStruct((6, quads, 64, QUAD), BF),
            jax.ShapeDtypeStruct((quads, 64, WIDTH), F32),
        ],
        compiler_params=pltpu.CompilerParams(vmem_limit_bytes=40 << 20),
        cost_estimate=pl.CostEstimate(flops=0, bytes_accessed=5 * rows * width, transcendentals=0),
    )(products)


def aspp_spread_kernel(one_ref, rows_ref, pool_ref, mask_ref, out_ref):
    lanes = lax.broadcasted_iota(jnp.int32, (64, WIDTH), 1)
    out_ref[0:64, :] = one_ref[...].astype(BF)
    for t in range(4):
        part = slice(t * WIDTH, (t + 1) * WIDTH)
        out_ref[64 * 28 : 64 * 29, part] = (pool_ref[...] * mask_ref[0:1, part]).astype(BF)
        for br, rate in enumerate(RATES):
            for i in range(3):
                tile = rows_ref[br, i, 0, :, part].astype(F32)
                for j in range(3):
                    at = 64 * (1 + 9 * br + 3 * i + j)
                    out_ref[at : at + 64, part] = shift_lanes(tile, (1 - j) * rate, lanes).astype(BF)


def aspp_spread(one, rows, pool, mask):
    width = one.shape[1]
    quads = width // QUAD
    count = 64 * 29
    return pl.pallas_call(
        aspp_spread_kernel,
        grid=(quads,),
        in_specs=[
            pl.BlockSpec((64, QUAD), lambda a: (0, a)),
            pl.BlockSpec((3, 3, 1, 64, QUAD), lambda a: (0, 0, a, 0, 0)),
            pl.BlockSpec((64, WIDTH), lambda a: (0, 0)),
            pl.BlockSpec((8, QUAD), lambda a: (0, a)),
        ],
        out_specs=pl.BlockSpec((count, QUAD), lambda a: (0, a)),
        out_shape=jax.ShapeDtypeStruct((count, width), BF),
        compiler_params=pltpu.CompilerParams(vmem_limit_bytes=40 << 20),
        cost_estimate=pl.CostEstimate(flops=0, bytes_accessed=3 * count * width, transcendentals=0),
    )(one, rows, pool, mask)


def side_rows(side):
    zero = jnp.zeros_like(side[0, :1])
    result = []
    from_one = crop_shift(jnp.concatenate([side[0, 1:4], side[2, 0:2]]), 1)
    from_two = crop_shift(jnp.concatenate([side[2, 2:4], side[4, 0:3]]), 2)
    from_three = crop_shift(side[4, 3:4], 3)
    to_one = crop_shift(jnp.concatenate([side[1, 0:3], side[3, 2:4]]), -1)
    to_two = crop_shift(jnp.concatenate([side[3, 0:2], side[5, 1:4]]), -2)
    to_three = crop_shift(side[5, 0:1], -3)
    del zero
    result.append(jnp.concatenate([from_one[0:3], side[0, 0:1]]))
    result.append(jnp.concatenate([side[1, 3:4], to_one[0:3]]))
    result.append(jnp.concatenate([from_two[0:2], from_one[3:5]]))
    result.append(jnp.concatenate([to_one[3:5], to_two[0:2]]))
    result.append(jnp.concatenate([from_three, from_two[2:5]]))
    result.append(jnp.concatenate([to_two[2:5], to_three]))
    return result


def adam_step(weight, first_m, second_m, gradient, factor, rate, decay):
    clipped = gradient * factor
    new_first = BETA_ONE * first_m + (1.0 - BETA_ONE) * clipped
    new_second = BETA_TWO * second_m + (1.0 - BETA_TWO) * clipped * clipped
    corrected = (
        new_first
        / (1.0 - BETA_ONE**STEP)
        / (jnp.sqrt(new_second / (1.0 - BETA_TWO**STEP)) + ADAM_EPSILON)
    )
    return (weight - rate * (corrected + decay * weight), new_first, new_second)


def flat_rows(quads):
    return jnp.concatenate([quads[a] for a in range(quads.shape[0])], axis=1)


def quad_blocks(flat):
    return [flat[..., a * QUAD : (a + 1) * QUAD] for a in range(flat.shape[-1] // QUAD)]


def shards(
    features,
    crop_rows,
    crop_cols,
    labels,
    offset_targets,
    depth_targets,
    lidar_mask,
    trunk_aspp,
    aspp_first,
    aspp_second,
    trunk_neck,
    neck_first,
    neck_second,
    norm_params,
    norm_first,
    norm_second,
    decoders,
    decoder_first,
    decoder_second,
    log_vars,
    log_first,
    log_second,
):
    heads = lax.axis_size("head")
    z = lax.axis_index("head")
    group = lax.axis_index("dp")
    crop = group // CROP_DP
    pixels = heads * QUAD
    share = 1.0 / heads
    quarter = ASP // heads

    neck_low = lax.all_gather(trunk_neck.astype(BF), "head", axis=0, tiled=True)
    neck_low = lax.all_gather(neck_low, "dp", axis=1, tiled=True)
    line = neck_low.reshape(heads, -1)
    first_end = BOT // heads * FEAT
    second_end = first_end + 9 * BOT // heads * BOT
    third_end = second_end + FEAT // heads * BOT
    reduce_w = line[:, :first_end].reshape(BOT, FEAT)
    middle = line[:, first_end:second_end].reshape(heads, 9, BOT // heads, BOT)
    middle = jnp.moveaxis(middle, 0, 1).reshape(9, BOT, BOT)
    expand_w = line[:, second_end:third_end].reshape(FEAT, BOT)

    x_group = lax.all_gather(features, "head", axis=1, tiled=True)
    aspp_low = lax.all_gather(trunk_aspp[0].astype(BF), "dp", axis=0, tiled=True)
    aspp_rows = aspp_low.reshape(-1, FEAT)
    tap_w = aspp_rows[: 29 * quarter]
    project_q = aspp_rows[29 * quarter :].reshape(quarter, 5 * ASP)
    project_w = lax.all_gather(project_q, "head", axis=0, tiled=True)
    project_own = lax.dynamic_slice_in_dim(
        project_w.reshape(ASP, 5, heads, quarter), z, 1, 2
    ).reshape(ASP, 5 * quarter)

    place = jnp.arange(pixels, dtype=jnp.int32)
    row_place = group % CROP_DP * (pixels // WIDTH) + place // WIDTH
    col_place = place % WIDTH
    mask = ((row_place < crop_rows[crop]) & (col_place < crop_cols[crop])).astype(F32)[None, :]
    mask_own = lax.dynamic_slice_in_dim(mask, z * QUAD, QUAD, 1)
    total_n = jnp.sum((crop_rows * crop_cols).astype(F32))
    crop_n = (crop_rows[crop] * crop_cols[crop]).astype(F32)

    def own_pixels(a):
        return lax.dynamic_slice_in_dim(a, z * QUAD, QUAD, a.ndim - 1)

    labels_own = own_pixels(labels)
    offset_own = own_pixels(offset_targets)
    depth_own = own_pixels(depth_targets)
    lidar_own = own_pixels(lidar_mask).astype(F32) * mask_own[0]

    gains, shifts = (norm_params[0], norm_params[1])
    bounds = [0, BOT, 2 * BOT, 2 * BOT + FEAT, 2 * BOT + FEAT + 4 * ASP, 2 * BOT + FEAT + 5 * ASP]

    def slot(vector, index):
        return vector[bounds[index] : bounds[index + 1]]

    def own_aspp(vector):
        return lax.dynamic_slice_in_dim(vector.reshape(4, heads, quarter), z, 1, 1).reshape(-1)

    gain_one, gain_two, gain_three, gain_proj = [slot(gains, i) for i in (0, 1, 2, 4)]
    shift_one, shift_two, shift_three, shift_proj = [slot(shifts, i) for i in (0, 1, 2, 4)]
    gain_aspp, shift_aspp = own_aspp(slot(gains, 3)), own_aspp(slot(shifts, 3))

    def moments(pre, m):
        masked = pre * m
        return jnp.sum(masked, axis=-1), jnp.sum(masked * pre, axis=-1)

    def coefficients(total, square):
        mean = total / total_n
        inv = lax.rsqrt(square / total_n - mean * mean + EPSILON)
        return mean, inv

    def normed(pre, mean, inv):
        return (pre - mean[:, None]) * inv[:, None]

    def scaled(hat, gain, shift):
        return gain[:, None] * hat + shift[:, None]

    x_own = features * mask_own.astype(BF)
    pre_one = jnp.dot(reduce_w, x_own, preferred_element_type=F32)
    sums = sum_all(pack((*moments(pre_one, mask_own), jnp.broadcast_to(jnp.sum(lidar_own), (128,)))))
    total, square, lidar = unpack(sums, (BOT, BOT, 128))
    lidar_n = lidar[0]
    mean_one, inv_one = coefficients(total, square)
    low_one = (jax.nn.silu(scaled(normed(pre_one, mean_one, inv_one), gain_one, shift_one)) * mask_own).astype(BF)
    blocks = gather_line(low_one, z)
    before = crop_shift(blocks[-1], 1)
    after = crop_shift(blocks[0], -1)
    h_one = jnp.concatenate(blocks, axis=1)
    columns = neck_columns(jnp.concatenate([before, h_one, after], axis=1), False)
    pre_two = lax.dot_general(middle, columns, (((0, 2), (0, 1)), ((), ())), preferred_element_type=F32)
    mean_two, inv_two = coefficients(*unpack(sum_dp(pack(moments(pre_two, mask))), (BOT, BOT)))
    hat_two = normed(pre_two, mean_two, inv_two)
    in_two = scaled(hat_two, gain_two, shift_two)
    h_two = (jax.nn.silu(in_two) * mask).astype(BF)
    pre_three = jnp.dot(expand_w, h_two, preferred_element_type=F32)
    mean_three, inv_three = coefficients(*unpack(sum_dp(pack(moments(pre_three, mask))), (FEAT, FEAT)))
    x_group = x_group * mask.astype(BF)
    hat_three = normed(pre_three, mean_three, inv_three)
    in_three = scaled(hat_three, gain_three, shift_three) + x_group.astype(F32)
    y = (jax.nn.silu(in_three) * mask).astype(BF)

    products = jnp.dot(tap_w, y, preferred_element_type=F32)
    middle_rows, side, pool_part = aspp_gather(products)
    moved = side_rows(side)
    branches = [middle_rows[0]]
    for br in range(3):
        branches.append(
            middle_rows[1 + br]
            + flat_rows(moved[2 * br]).astype(F32)
            + flat_rows(moved[2 * br + 1]).astype(F32)
        )
    pre_aspp = jnp.concatenate(branches, axis=0)
    pool_local = jnp.sum(pool_part, axis=(0, 2))
    local = pack((*moments(pre_aspp, mask), pool_local, jnp.zeros((64,), F32)))
    local = sum_crop(local)
    pool_sum = local[2 * ASP : 2 * ASP + quarter]
    for bits in rounds_of(4, lax.axis_size("dp")):
        local = xor_round(local, "dp", bits)
    mean_aspp, inv_aspp = coefficients(local[:ASP], local[ASP : 2 * ASP])
    hat_aspp = normed(pre_aspp, mean_aspp, inv_aspp)
    in_aspp = scaled(hat_aspp, gain_aspp, shift_aspp)
    act_aspp = jax.nn.silu(in_aspp) * mask
    pool_pre = pool_sum / crop_n
    joined = jnp.concatenate([act_aspp, jax.nn.silu(pool_pre)[:, None] * mask], axis=0).astype(BF)

    part_proj = jnp.dot(project_own, joined, preferred_element_type=F32)
    pre_proj = lax.psum_scatter(part_proj.astype(BF), "head", scatter_dimension=1, tiled=True).astype(F32)
    mean_proj, inv_proj = coefficients(*unpack(sum_all(pack(moments(pre_proj, mask_own))), (ASP, ASP)))
    hat_proj = normed(pre_proj, mean_proj, inv_proj)
    in_proj = scaled(hat_proj, gain_proj, shift_proj)
    feat = (jax.nn.silu(in_proj) * mask_own).astype(BF)

    low_dec = decoders.astype(BF)
    hidden_w, out_w = low_dec[: 3 * ASP], low_dec[3 * ASP :]
    dec_pre = jnp.dot(hidden_w, feat, preferred_element_type=F32)
    hidden = jax.nn.silu(dec_pre).astype(BF)
    row_sets = ((0, CLS), (CLS, CLS + 2), (CLS + 2, CLS + 3))
    logits = [
        jnp.dot(out_w, hidden[t * ASP : (t + 1) * ASP], preferred_element_type=F32)[lo:hi]
        for t, (lo, hi) in enumerate(row_sets)
    ]
    sem_logits, off_logits, dep_logits = logits
    valid_own = mask_own[0]
    label_hot = (jnp.arange(CLS, dtype=jnp.int32)[:, None] == labels_own[None, :]).astype(F32)
    log_total = jax.nn.logsumexp(sem_logits, axis=0)
    sem_sum = jnp.sum((log_total - jnp.sum(label_hot * sem_logits, axis=0)) * valid_own)
    off_diff = off_logits - offset_own
    off_root = jnp.sqrt(off_diff * off_diff + 1.0)
    off_sum = jnp.sum((off_root - 1.0) * valid_own)
    dep_logit = dep_logits[0]
    dep_diff = jax.nn.softplus(dep_logit) - depth_own
    dep_root = jnp.sqrt(dep_diff * dep_diff + 1.0)
    dep_sum = jnp.sum((dep_root - 1.0) * lidar_own)
    divisors = jnp.stack([total_n, total_n, lidar_n])
    weights = jnp.exp(-log_vars) / divisors
    grad_sem = (jax.nn.softmax(sem_logits, axis=0) - label_hot) * valid_own * weights[0]
    grad_off = off_diff / off_root * valid_own * weights[1]
    grad_dep = (dep_diff / dep_root * jax.nn.sigmoid(dep_logit) * lidar_own * weights[2])[None, :]
    grad_logits = [g.astype(BF) for g in (grad_sem, grad_off, grad_dep)]
    grad_out_w = []
    grad_hidden = []
    for t, (lo, hi) in enumerate(row_sets):
        grad_out_w.append(dot(grad_logits[t], hidden[t * ASP : (t + 1) * ASP], (1,), (1,)))
        grad_hidden.append(dot(out_w[lo:hi], grad_logits[t], (0,), (0,)))
    grad_dec_pre = (jnp.concatenate(grad_hidden, axis=0) * silu_slope(dec_pre)).astype(BF)
    grad_hidden_w = dot(grad_dec_pre, feat, (1,), (1,))
    grad_feat = dot(hidden_w, grad_dec_pre, (0,), (0,))
    dec_grad = lax.psum(jnp.concatenate([grad_hidden_w, *grad_out_w], axis=0), ("dp", "head"))

    grad_act = grad_feat * mask_own * silu_slope(in_proj)
    sums = sum_all(
        pack(
            (
                jnp.sum(grad_act, axis=-1),
                jnp.sum(grad_act * hat_proj, axis=-1),
                jnp.stack([sem_sum, off_sum, dep_sum]),
                jnp.zeros((125,), F32),
            )
        )
    )
    back_shift_proj, back_gain_proj, loss_sums = unpack(sums, (ASP, ASP, 3))
    losses = loss_sums / divisors
    total_loss = jnp.sum(jnp.exp(-log_vars) * losses + log_vars)
    grad_logvar = 1.0 - jnp.exp(-log_vars) * losses
    grad_proj = (
        mask_own
        * (gain_proj * inv_proj)[:, None]
        * (grad_act - (back_shift_proj / total_n)[:, None] - hat_proj * (back_gain_proj / total_n)[:, None])
    ).astype(BF)
    grad_proj = lax.all_gather(grad_proj, "head", axis=1, tiled=True)
    grad_project = dot(grad_proj, joined, (1,), (1,))
    grad_joined = dot(project_own, grad_proj, (0,), (0,))

    grad_act = grad_joined[:ASP] * mask * silu_slope(in_aspp)
    local = pack(
        (
            jnp.sum(grad_act, axis=-1),
            jnp.sum(grad_act * hat_aspp, axis=-1),
            jnp.sum(grad_joined[ASP:] * mask, axis=-1),
            jnp.zeros((64,), F32),
        )
    )
    local = sum_crop(local)
    pool_row = local[2 * ASP : 2 * ASP + quarter]
    for bits in rounds_of(4, lax.axis_size("dp")):
        local = xor_round(local, "dp", bits)
    back_shift_aspp, back_gain_aspp = local[:ASP], local[ASP : 2 * ASP]
    grad_aspp = (
        mask
        * (gain_aspp * inv_aspp)[:, None]
        * (grad_act - (back_shift_aspp / total_n)[:, None] - hat_aspp * (back_gain_aspp / total_n)[:, None])
    ).astype(BF)
    grad_pool = (pool_row * silu_slope(pool_pre)).astype(BF).astype(F32) / crop_n
    parts = [jnp.stack(quad_blocks(grad_aspp[quarter * (br + 1) : quarter * (br + 2)])) for br in range(3)]
    moved = side_rows(jnp.stack([part for part in parts for _ in range(2)]))
    rows = jnp.stack(
        [jnp.stack([moved[2 * br + 1], parts[br], moved[2 * br]]) for br in range(3)]
    )
    spread = aspp_spread(
        grad_aspp[:quarter],
        rows,
        jnp.broadcast_to(grad_pool[:, None], (quarter, WIDTH)),
        jnp.broadcast_to(mask, (8, pixels)),
    )
    grad_y = dot(tap_w, spread, (0,), (0,))
    grad_taps = dot(spread, y, (1,), (1,))

    grad_act = grad_y * mask * silu_slope(in_three)
    sums = sum_all(pack((jnp.sum(grad_act, axis=-1), jnp.sum(grad_act * hat_three, axis=-1))))
    back_shift_three, back_gain_three = unpack(sums, (FEAT, FEAT))

    def norm_back(grad_act, hat, gain, inv, back_shift, back_gain):
        scale = share / total_n
        return (
            mask
            * (gain * inv)[:, None]
            * (grad_act - (back_shift * scale)[:, None] - hat * (back_gain * scale)[:, None])
        ).astype(BF)

    grad_three = norm_back(grad_act, hat_three, gain_three, inv_three, back_shift_three, back_gain_three)
    grad_expand = dot(grad_three, h_two, (1,), (1,))
    grad_act = dot(expand_w, grad_three, (0,), (0,)) * mask * silu_slope(in_two)
    sums = sum_all(pack((jnp.sum(grad_act, axis=-1), jnp.sum(grad_act * hat_two, axis=-1))))
    back_shift_two, back_gain_two = unpack(sums, (BOT, BOT))
    grad_two = norm_back(grad_act, hat_two, gain_two, inv_two, back_shift_two, back_gain_two)
    before = crop_shift(grad_two[:, -QUAD:], 1)
    after = crop_shift(grad_two[:, :QUAD], -1)
    columns = neck_columns(jnp.concatenate([before, grad_two, after], axis=1), True)
    grad_middle = dot(columns, h_one, (2,), (1,))
    grad_h_one = lax.dot_general(middle, columns, (((0, 1), (0, 1)), ((), ())), preferred_element_type=F32)
    group_one = jnp.dot(reduce_w, x_group, preferred_element_type=F32)
    hat_one = normed(group_one, mean_one, inv_one)
    grad_act = grad_h_one * mask * silu_slope(scaled(hat_one, gain_one, shift_one))
    sums = sum_all(pack((jnp.sum(grad_act, axis=-1), jnp.sum(grad_act * hat_one, axis=-1))))
    back_shift_one, back_gain_one = unpack(sums, (BOT, BOT))
    grad_one = norm_back(grad_act, hat_one, gain_one, inv_one, back_shift_one, back_gain_one)
    grad_reduce = dot(grad_one, x_group, (1,), (1,))

    swapped = lax.all_to_all(
        grad_project.astype(BF).reshape(heads, quarter, 5 * quarter), "head", 0, 0, tiled=True
    )
    own_project = jnp.moveaxis(swapped.reshape(heads, quarter, 5, quarter), 0, 2).reshape(-1, FEAT)
    flat_aspp = jnp.concatenate([grad_taps.astype(BF), own_project], axis=0).reshape(-1, 128)
    shard_aspp = lax.psum_scatter(flat_aspp, "dp", scatter_dimension=0, tiled=True).astype(F32)[None]
    flat_neck = jnp.concatenate(
        [
            grad_reduce.astype(BF).reshape(heads, -1),
            jnp.moveaxis(grad_middle.astype(BF).reshape(9, heads, BOT // heads, BOT), 1, 0).reshape(heads, -1),
            grad_expand.astype(BF).reshape(heads, -1),
        ],
        axis=1,
    ).reshape(heads, -1, 128)
    flat_neck = lax.psum_scatter(flat_neck, "dp", scatter_dimension=1, tiled=True)
    shard_neck = lax.psum_scatter(flat_neck, "head", scatter_dimension=0, tiled=True).astype(F32)

    both = lax.all_gather(jnp.stack([back_gain_aspp, back_shift_aspp]).reshape(2, 4, quarter), "head", axis=2)
    both = both.reshape(2, 4 * ASP)
    grad_norms = jnp.stack(
        [
            jnp.concatenate([back_gain_one, back_gain_two, back_gain_three, both[0], back_gain_proj]),
            jnp.concatenate([back_shift_one, back_shift_two, back_shift_three, both[1], back_shift_proj]),
        ]
    )
    local_square = jnp.sum(shard_aspp * shard_aspp) + jnp.sum(shard_neck * shard_neck)
    total_square = (
        sum_all(jnp.broadcast_to(local_square, (128,)))[0]
        + jnp.sum(grad_norms * grad_norms)
        + jnp.sum(dec_grad * dec_grad)
        + jnp.sum(grad_logvar * grad_logvar)
    )
    grad_norm = jnp.sqrt(total_square)
    factor = jnp.minimum(1.0, CLIP_LIMIT / grad_norm)
    aspp_out = adam_step(trunk_aspp, aspp_first, aspp_second, shard_aspp, factor, 0.04, 0.01)
    neck_out = adam_step(trunk_neck, neck_first, neck_second, shard_neck, factor, 0.04, 0.01)
    norm_out = adam_step(norm_params, norm_first, norm_second, grad_norms, factor, 0.6, 0.0)
    dec_out = adam_step(decoders, decoder_first, decoder_second, dec_grad, factor, 0.12, 0.01)
    log_out = adam_step(log_vars, log_first, log_second, grad_logvar, factor, 0.5, 0.0)
    return (total_loss, grad_norm, *aspp_out, *neck_out, *norm_out, *dec_out, *log_out)


def solution(mesh):
    trunk = P("head", "dp", None)
    return jax.shard_map(
        shards,
        mesh=mesh,
        in_specs=(
            P(None, ("dp", "head")),
            P(),
            P(),
            P("dp"),
            P(None, "dp"),
            P("dp"),
            P("dp"),
            *[trunk] * 6,
            *[P()] * 9,
        ),
        out_specs=(P(), P(), *[trunk] * 6, *[P()] * 9),
        check_vma=False,
    )
```

time: 3570 us -> 1270 us (0.36)
  waiting for transfers between devices: 1500 us -> 538 us
  blocking collectives: 705 us -> 43.2 us
  local copies, waits for them, and re-layouts: 585 us -> 145 us
  other arithmetic: 474 us -> 147 us
  starting transfers between devices: 55.7 us -> 146 us
    psum x12 -> x0, blocking collectives: 705 us -> none  [the longest x5 419 us: norm_forward(): lax.psum((to_full(arrange(local_sum, groups)), to_full(arrange(local_squa...]
    reduce_scatter x4 -> x3, waiting for transfers between devices: 637 us -> 113 us  [the longest x1 58.3 us: shards(): lax.psum_scatter(flat_aspp, 'dp', scatter_dimension=0, tiled=True)]
    unnamed x5 -> x10, other arithmetic: 372 us -> 49.3 us
    unnamed x659 -> x223, local copies, waits for them, and re-layouts: 358 us -> 75.3 us
    all_gather x5, waiting for transfers between devices: 350 us -> 111 us  [the longest x1 51.4 us: shards(): neck_low = lax.all_gather(neck_low, 'dp', axis=1, tiled=True)]
    ppermute x16 -> x85, waiting for transfers between devices: 335 us -> 161 us  [the longest x6 106 us: line_shift(): lax.ppermute(x, 'head', [(i, i + by) for i in range(n) if 0 <= i + by < n])]
    ppermute x16 -> x85, starting transfers between devices: 55.3 us -> 142 us  [the longest x63 78.2 us: xor_move(): return lax.ppermute(x, axis, [(i, i ^ mask) for i in range(n)])]
    pad x66 -> x0, local copies, waits for them, and re-layouts: 64.3 us -> none  [the longest x33 33.3 us: column_shift(): shaped = jnp.pad(shaped[:, :, :offset], ((0, 0), (0, 0), (-offset, 0)))]
  transfers between devices with their start and end apart: 27 -> 96, of which waited for: 14 -> 61; matrix products, arithmetic and copies ran while one was open for 20% -> 19% of each run, Pallas kernels for 0% -> 1%
where the time goes in v1:
time: 1270 us; the launch traced here: 1260 us
  waiting for transfers between devices  538 us (42%)
  matrix products  195 us (15%)
  other arithmetic  147 us (12%)
  starting transfers between devices  146 us (11%)
  local copies, waits for them, and re-layouts  145 us (11%)
  blocking collectives  43.2 us (3%)
  Pallas kernels  25.5 us (2%)
  between operations  23.4 us (2%)
    psum x1, waiting for transfers between devices, shards(): lax.psum(jnp.concatenate([grad_hidden_w, *grad_out_w], axis=0), ('dp', 'h...  133 us
    dot_general x15, matrix products, dot(): lax.dot_general(a, b, ((ca, cb), ((), ())), preferred_element_type=F32)  117 us
    ppermute x6, waiting for transfers between devices, line_shift(): lax.ppermute(x, 'head', [(i, i + by) for i in range(n) if 0 <= i + by < n])  106 us
    ppermute x63, starting transfers between devices, xor_move(): return lax.ppermute(x, axis, [(i, i ^ mask) for i in range(n)])  78.2 us
    unnamed x223, local copies, waits for them, and re-layouts  75.3 us
    reduce_scatter x1, waiting for transfers between devices, shards(): lax.psum_scatter(flat_aspp, 'dp', scatter_dimension=0, tiled=True)  58.3 us
    all_gather x1, waiting for transfers between devices, shards(): neck_low = lax.all_gather(neck_low, 'dp', axis=1, tiled=True)  51.4 us
    unnamed x10, other arithmetic  49.3 us
  transfers between devices with their start and end apart: 96, of which 61 were waited for; matrix products, arithmetic and copies ran while one was open for 19% of the time, Pallas kernels for 1%

profile of v1, /device:TPU:0, one launch (start us, length us, event | category | flops | bytes accessed | tf_op | source)
XLA Modules:
  0.0 1263.9 jit_solution(10328695904373242209)
XLA Ops:
  9.1 32.8 %all-gather.7.cloned.1.call-done = bf16[4,1088,128]{2,1,0:T(8,128)(2,1)} async-done(((bf16[1,1088,128]{2,1,0:T(8,128)(2,1)}), bf16[4,1088,128]{2,1,0:T(8,128)(2,1)}) %all-gather.7.cloned.1.call-update) | async-done | bytes 1114128 | tf_op jit(solution)/shard_map/all_gather | solution.py:308
  48.5 51.4 %all-gather.9.cloned.1.call-done = bf16[4,8704,128]{2,1,0:T(8,128)(2,1)} async-done(((bf16[4,1088,128]{2,1,0:T(8,128)(2,1)}), bf16[4,8704,128]{2,1,0:T(8,128)(2,1)}) %all-gather.9.cloned.1.call-update) | async-done | bytes 8912912 | tf_op jit(solution)/shard_map/all_gather | solution.py:309
  100.0 31.4 %copy.138 = bf16[1,4,8704,128]{3,1,2,0:T(4,128)(2,1)S(1)} copy(bf16[1,4,8704,128]{3,2,1,0:T(8,128)(2,1)} %bitcast.345) | data formatting | bytes 17825792
  137.4 4.8 reshape.226
  168.4 38.7 %collective-permute-done.7 = bf16[512,512]{1,0:T(8,128)(2,1)S(1)} collective-permute-done((bf16[512,512]{1,0:T(8,128)(2,1)S(1)}, bf16[512,512]{1,0:T(8,128)(2,1)S(1)}, u32[]{:S(2)}, u32[]{:S(2)}) %collective-permute-start.7) | collective-permute-done | bytes 524320 | tf_op jit(solution)/shard_map/ppermute | solution.py:104
  209.2 5.4 collective-permute-start.11
  214.6 29.8 %collective-permute-done.8 = bf16[512,512]{1,0:T(8,128)(2,1)} collective-permute-done((bf16[512,512]{1,0:T(8,128)(2,1)S(1)}, bf16[512,512]{1,0:T(8,128)(2,1)}, u32[]{:S(2)}, u32[]{:S(2)}) %collective-permute-start.8) | collective-permute-done | bytes 524320 | tf_op jit(solution)/shard_map/ppermute | solution.py:104
  245.7 5.6 collective-permute-start.12
  251.2 32.4 %collective-permute-done.9 = bf16[512,512]{1,0:T(8,128)(2,1)} collective-permute-done((bf16[512,512]{1,0:T(8,128)(2,1)}, bf16[512,512]{1,0:T(8,128)(2,1)}, u32[]{:S(2)}, u32[]{:S(2)}) %collective-permute-start.9) | collective-permute-done | bytes 524320 | tf_op jit(solution)/shard_map/ppermute | solution.py:104
  286.9 19.3 %collective-permute-start.13 = (bf16[512,512]{1,0:T(8,128)(2,1)}, bf16[512,512]{1,0:T(8,128)(2,1)S(1)}, u32[]{:S(2)}, u32[]{:S(2)}) collective-permute-start(bf16[512,512]{1,0:T(8,128)(2,1)} %collective-permute-done.12), channel_id=1, source_target_pairs={{0,1},{1,2},{2,3},{4,5},{5,6},{6,7},{8,9},{9,10},{10,11},{12,13},{... | collective-permute-start | bytes 1572872 | tf_op jit(solution)/shard_map/ppermute | solution.py:104
  306.2 4.6 slice.593
  312.3 5.0 collective-permute-done.13
  325.3 7.9 shard_map.341
  333.2 15.8 %multiply_reduce_fusion.2 = (f32[512]{0:T(512)S(1)}, f32[512]{0:T(512)S(1)}, f32[2048,512,1]{0,1,2:T(8,128)}) fusion(f32[2048]{0:T(1024)S(1)} %fusion.118, bf16[9,512,512]{2,1,0:T(8,128)(2,1)S(1)} %bitcast.350, bf16[9,512,2048]{2,1,0:T(8,128)(2,1)} %shard_map.341), kind=kOutput, calls=%fused_computation.18 | convolution fusion | flops 9667870720 | bytes 27799552 | tf_op jit(solution)/shard_map/dot_general | solution.py:385
  349.0 6.6 collective-permute-start.15
  364.6 13.2 %multiply_reduce_fusion = (f32[2048]{0:T(1024)S(1)}, f32[2048]{0:T(1024)S(1)}, f32[2048,2048]{1,0:T(8,128)}) fusion(f32[2048]{0:T(1024)S(1)} %fusion.118, bf16[2048,512]{1,0:T(8,128)(2,1)} %reshape.229, f32[2048,512,1]{0,1,2:T(8,128)} %get-tuple-element.195, f32[512]{0:T(512)S(1)} %bitcast.388, f32[512]{0:T(512)S(1)} %get-tuple-element.68, ...), kind=kOutput, calls=%fused_computation.1 | convolution fusion | flops 4322226176 | bytes 23101440 | tf_op jit(solution)/shard_map/dot_general | solution.py:390
  386.6 6.6 slice.600
  393.2 12.5 slice.481
  406.4 13.2 %multiply_convert_fusion.1 = bf16[2048,2048]{0,1:T(8,128)(2,1)S(1)} fusion(f32[2048]{0:T(1024)S(1)} %fusion.118, f32[2048]{0:T(1024)S(1)} %bitcast.376, f32[2048]{0:T(1024)S(1)} %get-tuple-element.168, f32[2048]{0:T(1024)S(1)} %get-tuple-element.169, f32[2048,2048]{1,0:T(8,128)} %get-tuple-element.196, f32[2048]{0:T(1024)S(1)} %bitcast.373, ...), kind=kLoop, calls=%fused_computation.8 | loop fusion | flops 54525952 | bytes 33599488 | tf_op jit(solution)/shard_map/convert_element_type | solution.py:395
  422.9 18.7 %convolution_bitcast_fusion.p_ref = f32[1856,2048]{1,0:T(8,128)} fusion(bf16[2048,2048]{0,1:T(8,128)(2,1)S(1)} %multiply_convert_fusion.1, bf16[1856,2048]{1,0:T(8,128)(2,1)S(1)} %copy-done.9), kind=kOutput, calls=%fused_computation.14 | convolution fusion | flops 15569256448 | bytes 31195136 | tf_op jit(solution)/shard_map/dot_general | solution.py:397
  441.6 7.1 shard_map.342
  458.4 5.3 collective-permute-start.25
  475.0 29.7 %all_gather.22 = bf16[256,1280]{1,0:T(8,128)(2,1)S(1)} all-gather(bf16[64,1280]{1,0:T(8,128)(2,1)S(1)} %reshape.221), channel_id=1, replica_groups=mesh['dp'=8,'head'=4] {'head'}, dimensions={0}, use_global_device_ids=true | all-gather | bytes 819200 | tf_op jit(solution)/shard_map/all_gather | solution.py:324
  519.6 26.7 %reduce-scatter.5.cloned.1.call-done = bf16[256,512]{1,0:T(8,128)(2,1)} async-done(((bf16[256,2048]{1,0:T(8,128)(2,1)}), bf16[256,512]{1,0:T(8,128)(2,1)}) %reduce-scatter.5.cloned.1.call-update) | async-done | bytes 262160 | tf_op jit(solution)/shard_map/reduce_scatter | solution.py:422
  591.9 27.0 %all-gather.13.cloned.1.call-done = bf16[256,2048]{1,0:T(8,128)(2,1)} async-done(((bf16[256,512]{1,0:T(8,128)(2,1)}), bf16[256,2048]{1,0:T(8,128)(2,1)}) %all-gather.13.cloned.1.call-update) | async-done | bytes 1048592 | tf_op jit(solution)/shard_map/all_gather | solution.py:485
  653.7 41.6 %fusion.141 = (f32[2048]{0:T(1024)S(1)}, f32[2048]{0:T(1024)S(1)}, f32[2048,2048]{0,1:T(8,128)}) fusion(f32[2048]{0:T(1024)S(1)} %get-tuple-element.168, f32[2048]{0:T(1024)S(1)} %get-tuple-element.169, f32[2048,2048]{1,0:T(8,128)} %get-tuple-element.196, bf16[2048,2048]{0,1:T(8,128)(2,1)} %all-gather.11.cloned.1.call-done, ...), kind=kOutput, calls=%fused_computation.409 | convolution fusion | flops 15648944128 | bytes 57208832 | tf_op jit(solution)/shard_map/dot_general | solution.py:37
  695.3 5.4 collective-permute-start.55
  716.0 12.6 multiply_convert_fusion
  728.7 12.7 %fusion.143 = (f32[512]{0:T(512)S(1)}, f32[512]{0:T(512)S(1)}, f32[512,2048]{1,0:T(8,128)}) fusion(f32[512]{0:T(512)S(1)} %copy-done.71, f32[512]{0:T(512)S(1)} %copy-done.73, f32[2048,512,1]{0,1,2:T(8,128)} %get-tuple-element.195, f32[512]{0:T(512)S(1)} %bitcast.389, f32[512]{0:T(512)S(1)} %bitcast.381, f32[2048]{0:T(1024)S(1)} %fusion.118, ...), kind=kOutput, calls=%fused_computation.411 | convolution fusion | flops 4311743488 | bytes 18894848 | tf_op jit(solution)/shard_map/dot_general | solution.py:37
  763.9 4.7 fusion.4
  769.3 8.2 shard_map.344
  777.5 17.6 %fusion.142 = (f32[512]{0:T(512)S(1)}, f32[512]{0:T(512)S(1)}, f32[512,2048]{1,0:T(8,128)}) fusion(f32[512]{0:T(512)S(1)} %copy-done.50, f32[2048,512]{0,1:T(8,128)S(1)} %fusion.4, f32[512]{0:T(512)S(1)} %copy-done.52, f32[512]{0:T(512)S(1)} %bitcast.371, f32[512]{0:T(512)S(1)} %bitcast.365, f32[2048]{0:T(1024)S(1)} %fusion.118, ...), kind=kOutput, calls=%fused_computation.410 | convolution fusion | flops 9680453632 | bytes 32002048 | tf_op jit(solution)/shard_map/dot_general | solution.py:545
  801.7 11.3 convolution_convert_fusion.1
  819.9 14.4 %convolution_convert_fusion.2 = bf16[9,512,512]{2,1,0:T(8,128)(2,1)S(1)} fusion(bf16[9,512,2048]{2,1,0:T(8,128)(2,1)} %shard_map.344, bf16[512,512]{1,0:T(8,128)(2,1)S(1)} %copy-done.19, bf16[512,512]{1,0:T(8,128)(2,1)} %get-tuple-element.83, bf16[512,512]{1,0:T(8,128)(2,1)} %get-tuple-element.85, bf16[512,512]{1,0:T(8,128)(2,1)S(1)} %copy-done.33), kind=kOutput, calls=%fused_computation.51 | convolution fusion | flops 9674424320 | bytes 25690112 | tf_op jit(solution)/shard_map/dot_general | solution.py:37
  834.7 16.3 %copy.133 = bf16[1,4,1152,512]{3,1,2,0:T(4,128)(2,1)} copy(bf16[1,4,1152,512]{3,2,1,0:T(8,128)(2,1)S(1)} %bitcast.343) | data formatting | bytes 9437184
  851.1 6.6 fusion.15
  862.3 42.8 %maximum_bitcast_fusion = bf16[1,4,8704,128]{3,1,2,0:T(4,128)(2,1)S(1)} fusion(bf16[4,262144]{1,0:T(4,128)(2,1)S(1)} %reshape.239, bf16[4,589824]{1,0:T(4,128)(2,1)} %bitcast.344, bf16[4,262144]{1,0:T(4,128)(2,1)} %reshape.236), kind=kLoop, calls=%fused_computation.13 | loop fusion | flops 26738688 | bytes 17825792
  905.1 7.2 copy.137
  922.9 5.3 all-to-all-done
  928.9 21.8 %convolution_convert_fusion = bf16[1856,2048]{1,0:T(8,128)(2,1)} fusion(bf16[1856,2048]{1,0:T(8,128)(2,1)} %copy-done, bf16[2048,2048]{0,1:T(8,128)(2,1)} %copy-done.6), kind=kOutput, calls=%fused_computation.16 | convolution fusion | flops 15573057536 | bytes 23592960 | tf_op jit(solution)/shard_map/dot_general | solution.py:37
  950.7 7.8 pad_maximum_fusion
  958.5 12.9 %reshape.235 = bf16[30336,128]{1,0:T(8,128)(2,1)} reshape(bf16[1896,2048]{1,0:T(8,128)(2,1)} %pad_maximum_fusion) | data formatting | bytes 15532032 | tf_op jit(solution)/shard_map/reshape | solution.py:558
  971.6 14.8 %reduce-scatter.9.cloned.1.call-done = bf16[4,1088,128]{2,1,0:T(8,128)(2,1)} async-done(((bf16[4,8704,128]{2,1,0:T(8,128)(2,1)}), bf16[4,1088,128]{2,1,0:T(8,128)(2,1)}) %reduce-scatter.9.cloned.1.call-update) | async-done | bytes 1114128 | tf_op jit(solution)/shard_map/reduce_scatter | solution.py:568
  988.4 132.8 %all-reduce.2.cloned.1.call-done = f32[790,256]{1,0:T(8,128)} async-done(((f32[790,256]{1,0:T(8,128)}), f32[790,256]{1,0:T(8,128)}) %all-reduce.2.cloned.1.call-update) | async-done | bytes 808976 | tf_op jit(solution)/shard_map/psum | solution.py:463
  1123.3 13.5 %all_gather.27 = f32[2,4,4,64]{3,1,0,2:T(4,128)S(1)} all-gather(f32[2,4,1,64]{3,1,0,2:T(4,128)S(1)} %pad_maximum_fusion.25), channel_id=1, replica_groups=mesh['dp'=8,'head'=4] {'head'}, dimensions={2}, use_global_device_ids=true | all-gather | bytes 10240 | tf_op jit(solution)/shard_map/all_gather | solution.py:571
  1137.0 58.3 %reduce-scatter.7.cloned.1.call-done = bf16[3792,128]{1,0:T(8,128)(2,1)} async-done(((bf16[30336,128]{1,0:T(8,128)(2,1)}), bf16[3792,128]{1,0:T(8,128)(2,1)}) %reduce-scatter.7.cloned.1.call-update) | async-done | bytes 970768 | tf_op jit(solution)/shard_map/reduce_scatter | solution.py:559
  1197.6 28.0 %reduce-scatter.11.cloned.1.call-done = bf16[1,1088,128]{2,1,0:T(8,128)(2,1)} async-done(((bf16[4,1088,128]{2,1,0:T(8,128)(2,1)}), bf16[1,1088,128]{2,1,0:T(8,128)(2,1)}) %reduce-scatter.11.cloned.1.call-update) | async-done | bytes 278544 | tf_op jit(solution)/shard_map/reduce_scatter | solution.py:569
  1246.3 6.1 multiply_subtract_fusion
  (614 shorter events, 286.5 us)
Async XLA Ops:
  7.2 34.7 %all-gather.7.cloned.1.call-start = ((), (), s32[]{:S(2)}) async-start(), calls=%async_computation.5 | async-start | bytes 1392640 | tf_op jit(solution)/shard_map/all_gather | solution.py:308
  9.1 90.9 %all-gather.9.cloned.1.call-start = ((), (), s32[]{:S(2)}) async-start(), calls=%async_computation.6 | async-start | bytes 10027008 | tf_op jit(solution)/shard_map/all_gather | solution.py:309
  42.0 343.5 %all-gather.15.cloned.1.call-start = ((), (), s32[]{:S(2)}) async-start(), calls=%async_computation.14 | async-start | bytes 8736768 | tf_op jit(solution)/shard_map/all_gather | solution.py:320
  44.6 361.8 %all-gather.11.cloned.1.call-start = ((), (), s32[]{:S(2)}) async-start(), calls=%async_computation.7 | async-start | bytes 10485760 | tf_op jit(solution)/shard_map/all_gather | solution.py:319
  150.9 395.4 %reduce-scatter.5.cloned.1.call-start = ((), (), s32[]{:S(2)}) async-start(), calls=%async_computation.8 | async-start | bytes 1310720 | tf_op jit(solution)/shard_map/reduce_scatter | solution.py:422
  160.0 5.4 collective-permute-start.6
  167.1 40.0 %collective-permute-start.7 = (bf16[512,512]{1,0:T(8,128)(2,1)S(1)}, bf16[512,512]{1,0:T(8,128)(2,1)S(1)}, u32[]{:S(2)}, u32[]{:S(2)}) collective-permute-start(bf16[512,512]{1,0:T(8,128)(2,1)S(1)} %multiply_convert_fusion.6), channel_id=1, source_target_pairs={{1,0},{2,1},{3,2},{5,4},{6,5},{7,6},{9,8},{10,9},{11,10},{13,12},{... | collective-permute-start | bytes 1572872 | tf_op jit(solution)/shard_map/ppermute | solution.py:104
  207.9 36.5 %collective-permute-start.8 = (bf16[512,512]{1,0:T(8,128)(2,1)S(1)}, bf16[512,512]{1,0:T(8,128)(2,1)}, u32[]{:S(2)}, u32[]{:S(2)}) collective-permute-start(bf16[512,512]{1,0:T(8,128)(2,1)S(1)} %collective-permute-done.7), channel_id=1, source_target_pairs={{1,0},{2,1},{3,2},{5,4},{6,5},{7,6},{9,8},{10,9},{11,10},{13,12},{... | collective-permute-start | bytes 1572872 | tf_op jit(solution)/shard_map/ppermute | solution.py:104
  209.2 36.5 %collective-permute-start.11 = (bf16[512,512]{1,0:T(8,128)(2,1)S(1)}, bf16[512,512]{1,0:T(8,128)(2,1)}, u32[]{:S(2)}, u32[]{:S(2)}) collective-permute-start(bf16[512,512]{1,0:T(8,128)(2,1)S(1)} %multiply_convert_fusion.6), channel_id=1, source_target_pairs={{0,1},{1,2},{2,3},{4,5},{5,6},{6,7},{8,9},{9,10},{10,11},{12,13},{... | collective-permute-start | bytes 1572872 | tf_op jit(solution)/shard_map/ppermute | solution.py:104
  244.4 39.2 %collective-permute-start.9 = (bf16[512,512]{1,0:T(8,128)(2,1)}, bf16[512,512]{1,0:T(8,128)(2,1)}, u32[]{:S(2)}, u32[]{:S(2)}) collective-permute-start(bf16[512,512]{1,0:T(8,128)(2,1)} %collective-permute-done.8), channel_id=1, source_target_pairs={{1,0},{2,1},{3,2},{5,4},{6,5},{7,6},{9,8},{10,9},{11,10},{13,12},{... | collective-permute-start | bytes 1572872 | tf_op jit(solution)/shard_map/ppermute | solution.py:104
  245.7 41.2 %collective-permute-start.12 = (bf16[512,512]{1,0:T(8,128)(2,1)}, bf16[512,512]{1,0:T(8,128)(2,1)}, u32[]{:S(2)}, u32[]{:S(2)}) collective-permute-start(bf16[512,512]{1,0:T(8,128)(2,1)} %collective-permute-done.11), channel_id=1, source_target_pairs={{0,1},{1,2},{2,3},{4,5},{5,6},{6,7},{8,9},{9,10},{10,11},{12,13},{... | collective-permute-start | bytes 1572872 | tf_op jit(solution)/shard_map/ppermute | solution.py:104
  285.5 26.7 %collective-permute-start.10 = (bf16[512,512]{1,0:T(8,128)(2,1)S(1)}, bf16[512,512]{1,0:T(8,128)(2,1)S(1)}, u32[]{:S(2)}, u32[]{:S(2)}) collective-permute-start(bf16[512,512]{1,0:T(8,128)(2,1)S(1)} %select_select_fusion.3), channel_id=1, source_target_pairs={{0,4},{4,8},{8,12},{16,20},{20,24},{24,28},{1,5},{5,9},{9,13},{17,... | collective-permute-start | bytes 1572872 | tf_op jit(solution)/shard_map/ppermute | solution.py:99
  286.9 30.5 %collective-permute-start.13 = (bf16[512,512]{1,0:T(8,128)(2,1)}, bf16[512,512]{1,0:T(8,128)(2,1)S(1)}, u32[]{:S(2)}, u32[]{:S(2)}) collective-permute-start(bf16[512,512]{1,0:T(8,128)(2,1)} %collective-permute-done.12), channel_id=1, source_target_pairs={{0,1},{1,2},{2,3},{4,5},{5,6},{6,7},{8,9},{9,10},{10,11},{12,13},{... | collective-permute-start | bytes 1572872 | tf_op jit(solution)/shard_map/ppermute | solution.py:104
  318.7 6.5 collective-permute-start.14
  349.0 7.4 collective-permute-start.15
  356.5 6.9 collective-permute-start.17
  379.0 26.7 %collective-permute-start.21 = (f32[4096]{0:T(1024)S(1)}, f32[4096]{0:T(1024)S(1)}, u32[]{:S(2)}, u32[]{:S(2)}) collective-permute-start(f32[4096]{0:T(1024)S(1)} %fusion.136), channel_id=1, source_target_pairs={{0,16},{4,20},{8,24},{12,28},{16,0},{20,4},{24,8},{28,12},{1,17},{... | collective-permute-start | bytes 49160 | tf_op jit(solution)/shard_map/ppermute | solution.py:42
  380.6 25.1 %collective-permute-start.22 = (f32[4096]{0:T(1024)S(1)}, f32[4096]{0:T(1024)S(1)}, u32[]{:S(2)}, u32[]{:S(2)}) collective-permute-start(f32[4096]{0:T(1024)S(1)} %fusion.136), channel_id=1, source_target_pairs={{0,24},{4,28},{8,16},{12,20},{16,8},{20,12},{24,0},{28,4},{1,25},{... | collective-permute-start | bytes 49160 | tf_op jit(solution)/shard_map/ppermute | solution.py:42
  380.6 25.0 %collective-permute-start.20 = (f32[4096]{0:T(1024)S(1)}, f32[4096]{0:T(1024)S(1)}, u32[]{:S(2)}, u32[]{:S(2)}) collective-permute-start(f32[4096]{0:T(1024)S(1)} %fusion.136), channel_id=1, source_target_pairs={{0,8},{4,12},{8,0},{12,4},{16,24},{20,28},{24,16},{28,20},{1,9},{5... | collective-permute-start | bytes 49160 | tf_op jit(solution)/shard_map/ppermute | solution.py:42
  450.2 14.1 %collective-permute-start.23 = (bf16[5,64,512]{2,1,0:T(8,128)(2,1)}, bf16[5,64,512]{2,1,0:T(8,128)(2,1)}, u32[]{:S(2)}, u32[]{:S(2)}) collective-permute-start(bf16[5,64,512]{2,1,0:T(8,128)(2,1)} %pad_maximum_fusion.8), channel_id=1, source_target_pairs={{0,4},{4,8},{8,12},{16,20},{20,24},{24,28},{1,5},{5,9},{9,13},{17,... | collective-permute-start | bytes 983048 | tf_op jit(solution)/shard_map/ppermute | solution.py:99
  453.0 14.1 %collective-permute-start.24 = (bf16[5,64,512]{2,1,0:T(8,128)(2,1)}, bf16[5,64,512]{2,1,0:T(8,128)(2,1)}, u32[]{:S(2)}, u32[]{:S(2)}) collective-permute-start(bf16[5,64,512]{2,1,0:T(8,128)(2,1)} %pad_maximum_fusion.9), channel_id=1, source_target_pairs={{4,0},{8,4},{12,8},{20,16},{24,20},{28,24},{5,1},{9,5},{13,9},{21,... | collective-permute-start | bytes 983048 | tf_op jit(solution)/shard_map/ppermute | solution.py:99
  454.3 17.8 %collective-permute-start.28 = (bf16[1,64,512]{2,1,0:T(8,128)(2,1)}, bf16[1,64,512]{2,1,0:T(8,128)(2,1)}, u32[]{:S(2)}, u32[]{:S(2)}) collective-permute-start(bf16[1,64,512]{2,1,0:T(8,128)(2,1)} %get-tuple-element.98), channel_id=1, source_target_pairs={{12,0},{28,16},{13,1},{29,17},{14,2},{30,18},{15,3},{31,19}} | collective-permute-start | bytes 196616 | tf_op jit(solution)/shard_map/ppermute | solution.py:99
  456.3 13.5 %collective-permute-start.26 = (bf16[5,64,512]{2,1,0:T(8,128)(2,1)}, bf16[5,64,512]{2,1,0:T(8,128)(2,1)}, u32[]{:S(2)}, u32[]{:S(2)}) collective-permute-start(bf16[5,64,512]{2,1,0:T(8,128)(2,1)} %pad_maximum_fusion.11), channel_id=1, source_target_pairs={{8,0},{12,4},{24,16},{28,20},{9,1},{13,5},{25,17},{29,21},{10,2},{... | collective-permute-start | bytes 983048 | tf_op jit(solution)/shard_map/ppermute | solution.py:99
  458.4 13.6 %collective-permute-start.25 = (bf16[5,64,512]{2,1,0:T(8,128)(2,1)}, bf16[5,64,512]{2,1,0:T(8,128)(2,1)S(1)}, u32[]{:S(2)}, u32[]{:S(2)}) collective-permute-start(bf16[5,64,512]{2,1,0:T(8,128)(2,1)} %pad_maximum_fusion.10), channel_id=1, source_target_pairs={{0,8},{4,12},{16,24},{20,28},{1,9},{5,13},{17,25},{21,29},{2,10},{... | collective-permute-start | bytes 983048 | tf_op jit(solution)/shard_map/ppermute | solution.py:99
  464.4 8.3 collective-permute-start.27
  475.0 29.9 %collective-permute-start.29 = (f32[640]{0:T(1024)S(1)}, f32[640]{0:T(1024)S(1)}, u32[]{:S(2)}, u32[]{:S(2)}) collective-permute-start(f32[640]{0:T(1024)S(1)} %pad_maximum_fusion.21), channel_id=1, source_target_pairs={{0,4},{4,0},{8,12},{12,8},{16,20},{20,16},{24,28},{28,24},{1,5},{5... | collective-permute-start | bytes 7688 | tf_op jit(solution)/shard_map/ppermute | solution.py:42
  519.3 99.7 %all-gather.13.cloned.1.call-start = ((), (), s32[]{:S(2)}) async-start(), calls=%async_computation.9 | async-start | bytes 1310720 | tf_op jit(solution)/shard_map/all_gather | solution.py:485
  584.2 5.4 collective-permute-start.45
  591.9 394.5 %reduce-scatter.9.cloned.1.call-start = ((), (), s32[]{:S(2)}) async-start(), calls=%async_computation.11 | async-start | bytes 10027008 | tf_op jit(solution)/shard_map/reduce_scatter | solution.py:568
  633.7 8.9 collective-permute-start.52
  637.2 9.1 collective-permute-start.51
  638.5 7.9 collective-permute-start.50
  639.8 6.6 collective-permute-start.54
  641.3 5.7 collective-permute-start.53
  695.3 6.3 collective-permute-start.55
  709.7 5.5 collective-permute-start.61
  759.5 9.2 collective-permute-start.70
  760.8 7.9 collective-permute-start.69
  797.6 18.7 %collective-permute-start.73 = (f32[1024]{0:T(1024)S(1)}, f32[1024]{0:T(1024)S(1)}, u32[]{:S(2)}, u32[]{:S(2)}) collective-permute-start(f32[1024]{0:T(1024)S(1)} %fusion.130), channel_id=1, source_target_pairs={{0,16},{4,20},{8,24},{12,28},{16,0},{20,4},{24,8},{28,12},{1,17},{... | collective-permute-start | bytes 12296 | tf_op jit(solution)/shard_map/ppermute | solution.py:42
  798.5 17.8 %collective-permute-start.74 = (f32[1024]{0:T(1024)S(1)}, f32[1024]{0:T(1024)S(1)}, u32[]{:S(2)}, u32[]{:S(2)}) collective-permute-start(f32[1024]{0:T(1024)S(1)} %fusion.130), channel_id=1, source_target_pairs={{0,24},{4,28},{8,16},{12,20},{16,8},{20,12},{24,0},{28,4},{1,25},{... | collective-permute-start | bytes 12296 | tf_op jit(solution)/shard_map/ppermute | solution.py:42
  801.7 14.6 %collective-permute-start.72 = (f32[1024]{0:T(1024)S(1)}, f32[1024]{0:T(1024)S(1)}, u32[]{:S(2)}, u32[]{:S(2)}) collective-permute-start(f32[1024]{0:T(1024)S(1)} %fusion.130), channel_id=1, source_target_pairs={{0,8},{4,12},{8,0},{12,4},{16,24},{20,28},{24,16},{28,20},{1,9},{5... | collective-permute-start | bytes 12296 | tf_op jit(solution)/shard_map/ppermute | solution.py:42
  816.3 34.7 %collective-permute-start.76 = (f32[1024]{0:T(1024)S(1)}, f32[1024]{0:T(1024)S(1)}, u32[]{:S(2)}, u32[]{:S(2)}) collective-permute-start(f32[1024]{0:T(1024)S(1)} %add_add_fusion.6), channel_id=1, source_target_pairs={{0,2},{1,3},{2,0},{3,1},{4,6},{5,7},{6,4},{7,5},{8,10},{9,11},{10,... | collective-permute-start | bytes 12296 | tf_op jit(solution)/shard_map/ppermute | solution.py:42
  817.8 33.2 %collective-permute-start.77 = (f32[1024]{0:T(1024)S(1)}, f32[1024]{0:T(1024)S(1)}, u32[]{:S(2)}, u32[]{:S(2)}) collective-permute-start(f32[1024]{0:T(1024)S(1)} %add_add_fusion.6), channel_id=1, source_target_pairs={{0,3},{1,2},{2,1},{3,0},{4,7},{5,6},{6,5},{7,4},{8,11},{9,10},{10,... | collective-permute-start | bytes 12296 | tf_op jit(solution)/shard_map/ppermute | solution.py:42
  819.7 31.3 %collective-permute-start.75 = (f32[1024]{0:T(1024)S(1)}, f32[1024]{0:T(1024)S(1)}, u32[]{:S(2)}, u32[]{:S(2)}) collective-permute-start(f32[1024]{0:T(1024)S(1)} %add_add_fusion.6), channel_id=1, source_target_pairs={{0,1},{1,0},{2,3},{3,2},{4,5},{5,4},{6,7},{7,6},{8,9},{9,8},{10,11... | collective-permute-start | bytes 12296 | tf_op jit(solution)/shard_map/ppermute | solution.py:42
  918.1 10.1 all-to-all-start
  921.7 199.4 %all-reduce.2.cloned.1.call-start = ((), (), s32[]{:S(2)}) async-start(), calls=%async_computation.13 | async-start | bytes 1622016 | tf_op jit(solution)/shard_map/psum | solution.py:463
  922.8 272.5 %reduce-scatter.7.cloned.1.call-start = ((), (), s32[]{:S(2)}) async-start(), calls=%async_computation.10 | async-start | bytes 8736768 | tf_op jit(solution)/shard_map/reduce_scatter | solution.py:559
  971.5 254.1 %reduce-scatter.11.cloned.1.call-start = ((), (), s32[]{:S(2)}) async-start(), calls=%async_computation.12 | async-start | bytes 1392640 | tf_op jit(solution)/shard_map/reduce_scatter | solution.py:569
  (154 other events, 5177.7 us)
Sparse Core Ops, SparseCore 0:
  10.2 31.6 all-gather.6
  43.8 56.0 all-gather.8
  102.4 51.7 all-gather.14
  155.6 181.9 all-gather.10
  519.4 26.8 reduce-scatter.4
  592.0 26.8 all-gather.12
  912.6 73.7 reduce-scatter.8
  993.0 128.0 all-reduce.1
  1125.1 70.1 reduce-scatter.6
  1197.4 28.1 reduce-scatter.10

commit v2 on v1

--- a/solution.py
+++ b/solution.py
@@ -104,20 +104,68 @@
     return lax.ppermute(x, "head", [(i, i + by) for i in range(n) if 0 <= i + by < n])
 
 
-def gather_line(own, z):
-    n = lax.axis_size("head")
-    left, right = [own], [own]
-    for _ in range(n - 1):
-        left.append(line_shift(left[-1], 1))
-        right.append(line_shift(right[-1], -1))
-    blocks = []
-    for j in range(n):
-        block = None
-        for at in range(n):
-            source = own if at == j else (left[at - j] if at > j else right[j - at])
-            block = source if block is None else jnp.where(z == at, source, block)
-        blocks.append(block)
-    return blocks
+def exchange(own):
+    return [own] + [xor_move(own, "head", m) for m in range(1, lax.axis_size("head"))]
+
+
+def in_order(blocks, z):
+    stack = jnp.stack(blocks)
+    return [lax.dynamic_index_in_dim(stack, z ^ j, 0, False) for j in range(len(blocks))]
+
+
+def scatter_head(blocks, z):
+    n = blocks.shape[0]
+    total = lax.dynamic_index_in_dim(blocks, z, 0, False).astype(F32)
+    for m in range(1, n):
+        total = total + xor_move(lax.dynamic_index_in_dim(blocks, z ^ m, 0, False), "head", m).astype(F32)
+    return total
+
+
+def halve(t, axis, bits, bit, position):
+    at = bits.index(bit)
+    low = 1 << at
+    shape = t.shape
+    split = t.reshape(shape[:axis] + (shape[axis] // (2 * low), 2, low) + shape[axis + 1 :])
+    mine = (position >> (bit.bit_length() - 1)) & 1
+    keep = lax.dynamic_index_in_dim(split, mine, axis + 1, False)
+    send = lax.dynamic_index_in_dim(split, 1 - mine, axis + 1, False)
+    got = xor_move(send, "dp", bit)
+    out = (keep.astype(F32) + got.astype(F32)).astype(BF)
+    return out.reshape(shape[:axis] + (shape[axis] // 2,) + shape[axis + 1 :]), [x for x in bits if x != bit]
+
+
+def scatter_dp(t, axis):
+    n = lax.axis_size("dp")
+    position = lax.axis_index("dp")
+    bits = [1 << k for k in range(n.bit_length() - 1)]
+    t, bits = halve(t, axis, bits, 1, position)
+    t = yield (t,)
+    t = t[0]
+    half = t.shape[-1] // 2
+    parts = [(t[..., :half], bits), (t[..., half:], bits)]
+    order = [1 << k for k in range(1, n.bit_length() - 1)]
+    for k in range(0, len(order), 2):
+        pair = order[k : k + 2]
+        for step in range(len(pair)):
+            parts = [
+                halve(part, axis, left, pair[step if h == 0 else len(pair) - 1 - step], position)
+                for h, (part, left) in enumerate(parts)
+            ]
+            arrays = yield tuple(part for part, _ in parts)
+            parts = [(array, left) for array, (_, left) in zip(arrays, parts)]
+    return
+
+
+def tie(*trees):
+    return lax.optimization_barrier(trees)
+
+
+def last_step(steps, now):
+    while True:
+        try:
+            now = steps.send(now)
+        except StopIteration:
+            return jnp.concatenate(now, axis=-1) if len(now) > 1 else now[0]
 
 
 def shift_lanes(tile, by, lanes):
@@ -155,6 +203,49 @@
         compiler_params=pltpu.CompilerParams(vmem_limit_bytes=40 << 20),
         cost_estimate=pl.CostEstimate(flops=0, bytes_accessed=2 * 12 * rows * width, transcendentals=0),
     )(ext)
+
+
+def frames_of(own_rows, n_dp):
+    starts = [own_rows * s // 256 * 16 for s in range(n_dp)]
+    ends = [-(-own_rows * (s + 1) // 16) for s in range(n_dp)]
+    rows = max(end - start for start, end in zip(starts, ends))
+    return starts, -(-rows // 16) * 16
+
+
+def assemble_kernel(pieces, in_ref, out_ref):
+    for start, stop, sources in pieces:
+        total = None
+        for s, at in sources:
+            part = in_ref[s, at : at + stop - start, :]
+            total = part if total is None else total + part
+        out_ref[start:stop, :] = total
+
+
+def assemble(framed, own_rows, total_rows):
+    n_dp, frame_rows, width = framed.shape
+    starts, _ = frames_of(own_rows, n_dp)
+    rows = -(-total_rows // 16) * 16
+    pieces = []
+    for g in range(0, rows, 16):
+        sources = tuple(
+            (s, g - starts[s])
+            for s in range(n_dp)
+            if own_rows * s < (g + 16) * 16 and own_rows * (s + 1) > g * 16
+        )
+        if pieces and len(sources) == 1 and len(pieces[-1][2]) == 1 and pieces[-1][2][0][0] == sources[0][0]:
+            pieces[-1] = (pieces[-1][0], g + 16, pieces[-1][2])
+        else:
+            pieces.append((g, g + 16, sources))
+    block = 256
+    return pl.pallas_call(
+        functools.partial(assemble_kernel, pieces),
+        grid=(width // block,),
+        in_specs=[pl.BlockSpec((n_dp, frame_rows, block), lambda i: (0, 0, i))],
+        out_specs=pl.BlockSpec((rows, block), lambda i: (0, i)),
+        out_shape=jax.ShapeDtypeStruct((rows, width), BF),
+        compiler_params=pltpu.CompilerParams(vmem_limit_bytes=40 << 20),
+        cost_estimate=pl.CostEstimate(flops=0, bytes_accessed=4 * rows * width, transcendentals=0),
+    )(framed)
 
 
 def aspp_gather_kernel(p_ref, core_ref, side_ref, pool_ref):
@@ -305,26 +396,39 @@
     share = 1.0 / heads
     quarter = ASP // heads
 
-    neck_low = lax.all_gather(trunk_neck.astype(BF), "head", axis=0, tiled=True)
+    n_dp = lax.axis_size("dp")
+    neck_low = trunk_neck.reshape(1, -1, BOT).astype(BF)
+    neck_low = lax.all_gather(neck_low, "head", axis=0, tiled=True)
     neck_low = lax.all_gather(neck_low, "dp", axis=1, tiled=True)
-    line = neck_low.reshape(heads, -1)
-    first_end = BOT // heads * FEAT
-    second_end = first_end + 9 * BOT // heads * BOT
-    third_end = second_end + FEAT // heads * BOT
-    reduce_w = line[:, :first_end].reshape(BOT, FEAT)
-    middle = line[:, first_end:second_end].reshape(heads, 9, BOT // heads, BOT)
+    first_end = FEAT // heads
+    second_end = first_end + 9 * BOT // heads
+    reduce_w = neck_low[:, :first_end].reshape(BOT, FEAT)
+    middle = neck_low[:, first_end:second_end].reshape(heads, 9, BOT // heads, BOT)
     middle = jnp.moveaxis(middle, 0, 1).reshape(9, BOT, BOT)
-    expand_w = line[:, second_end:third_end].reshape(FEAT, BOT)
-
-    x_group = lax.all_gather(features, "head", axis=1, tiled=True)
-    aspp_low = lax.all_gather(trunk_aspp[0].astype(BF), "dp", axis=0, tiled=True)
-    aspp_rows = aspp_low.reshape(-1, FEAT)
+    expand_w = neck_low[:, second_end:].reshape(FEAT, BOT)
+
+    x_left, x_right = [features], [features]
+    for _ in range(heads // 2):
+        x_left.append(line_shift(x_left[-1], 1))
+        x_right.append(line_shift(x_right[-1], -1))
+
+    flat_total = trunk_aspp.shape[1] * n_dp // 16
+    own_rows = trunk_aspp.shape[1]
+    frames, frame_rows = frames_of(own_rows, n_dp)
+    inset = (group * own_rows) % 256
+    framed = lax.dynamic_update_slice_in_dim(
+        jnp.zeros((frame_rows * 16, 128), F32), trunk_aspp[0], inset, 0
+    )
+    framed = framed.reshape(frame_rows, FEAT).astype(BF)
+    aspp_rows = assemble(lax.all_gather(framed, "dp", axis=0), own_rows, flat_total)
     tap_w = aspp_rows[: 29 * quarter]
-    project_q = aspp_rows[29 * quarter :].reshape(quarter, 5 * ASP)
-    project_w = lax.all_gather(project_q, "head", axis=0, tiled=True)
-    project_own = lax.dynamic_slice_in_dim(
-        project_w.reshape(ASP, 5, heads, quarter), z, 1, 2
-    ).reshape(ASP, 5 * quarter)
+    project_q = aspp_rows[29 * quarter : flat_total].reshape(quarter, 5, heads, quarter)
+    project_q = jnp.moveaxis(project_q, 2, 0).reshape(heads, quarter, 5 * quarter)
+    received = [lax.dynamic_index_in_dim(project_q, z, 0, False)]
+    for m in range(1, heads):
+        received.append(xor_move(lax.dynamic_index_in_dim(project_q, z ^ m, 0, False), "head", m))
+    project_own = jnp.concatenate(in_order(received, z), axis=0)
+    tap_w, tap_wt, project_own = lax.optimization_barrier((tap_w, tap_w.T, project_own))
 
     place = jnp.arange(pixels, dtype=jnp.int32)
     row_place = group % CROP_DP * (pixels // WIDTH) + place // WIDTH
@@ -377,11 +481,15 @@
     lidar_n = lidar[0]
     mean_one, inv_one = coefficients(total, square)
     low_one = (jax.nn.silu(scaled(normed(pre_one, mean_one, inv_one), gain_one, shift_one)) * mask_own).astype(BF)
-    blocks = gather_line(low_one, z)
+    blocks = in_order(exchange(low_one), z)
     before = crop_shift(blocks[-1], 1)
     after = crop_shift(blocks[0], -1)
     h_one = jnp.concatenate(blocks, axis=1)
     columns = neck_columns(jnp.concatenate([before, h_one, after], axis=1), False)
+    columns, x_left[-1], x_right[-1] = tie(columns, x_left[-1], x_right[-1])
+    for _ in range(heads // 2, heads - 1):
+        x_left.append(line_shift(x_left[-1], 1))
+        x_right.append(line_shift(x_right[-1], -1))
     pre_two = lax.dot_general(middle, columns, (((0, 2), (0, 1)), ((), ())), preferred_element_type=F32)
     mean_two, inv_two = coefficients(*unpack(sum_dp(pack(moments(pre_two, mask))), (BOT, BOT)))
     hat_two = normed(pre_two, mean_two, inv_two)
@@ -389,6 +497,13 @@
     h_two = (jax.nn.silu(in_two) * mask).astype(BF)
     pre_three = jnp.dot(expand_w, h_two, preferred_element_type=F32)
     mean_three, inv_three = coefficients(*unpack(sum_dp(pack(moments(pre_three, mask))), (FEAT, FEAT)))
+    ring = [features]
+    for k in range(1, heads):
+        ring.append(jnp.where(z + k < heads, x_right[k], x_left[heads - k]))
+    ring = jnp.stack(ring)
+    x_group = jnp.concatenate(
+        [lax.dynamic_index_in_dim(ring, (a - z) % heads, 0, False) for a in range(heads)], axis=1
+    )
     x_group = x_group * mask.astype(BF)
     hat_three = normed(pre_three, mean_three, inv_three)
     in_three = scaled(hat_three, gain_three, shift_three) + x_group.astype(F32)
@@ -419,7 +534,7 @@
     joined = jnp.concatenate([act_aspp, jax.nn.silu(pool_pre)[:, None] * mask], axis=0).astype(BF)
 
     part_proj = jnp.dot(project_own, joined, preferred_element_type=F32)
-    pre_proj = lax.psum_scatter(part_proj.astype(BF), "head", scatter_dimension=1, tiled=True).astype(F32)
+    pre_proj = scatter_head(jnp.stack(quad_blocks(part_proj.astype(BF))), z)
     mean_proj, inv_proj = coefficients(*unpack(sum_all(pack(moments(pre_proj, mask_own))), (ASP, ASP)))
     hat_proj = normed(pre_proj, mean_proj, inv_proj)
     in_proj = scaled(hat_proj, gain_proj, shift_proj)
@@ -482,8 +597,8 @@
         * (gain_proj * inv_proj)[:, None]
         * (grad_act - (back_shift_proj / total_n)[:, None] - hat_proj * (back_gain_proj / total_n)[:, None])
     ).astype(BF)
-    grad_proj = lax.all_gather(grad_proj, "head", axis=1, tiled=True)
-    grad_project = dot(grad_proj, joined, (1,), (1,))
+    grad_proj = jnp.concatenate(in_order(exchange(grad_proj), z), axis=1)
+    grad_project = dot(grad_proj, joined, (1,), (1,)).astype(BF).reshape(heads, quarter, 5 * quarter)
     grad_joined = dot(project_own, grad_proj, (0,), (0,))
 
     grad_act = grad_joined[:ASP] * mask * silu_slope(in_aspp)
@@ -517,12 +632,32 @@
         jnp.broadcast_to(grad_pool[:, None], (quarter, WIDTH)),
         jnp.broadcast_to(mask, (8, pixels)),
     )
-    grad_y = dot(tap_w, spread, (0,), (0,))
-    grad_taps = dot(spread, y, (1,), (1,))
+    grad_y = dot(tap_wt, spread, (1,), (0,))
+    grad_taps = dot(spread, y, (1,), (1,)).astype(BF)
 
     grad_act = grad_y * mask * silu_slope(in_three)
-    sums = sum_all(pack((jnp.sum(grad_act, axis=-1), jnp.sum(grad_act * hat_three, axis=-1))))
-    back_shift_three, back_gain_three = unpack(sums, (FEAT, FEAT))
+    spread_norms = jnp.stack([back_gain_aspp, back_shift_aspp]).reshape(2, 4, 1, quarter)
+    own_place = (jnp.arange(heads) == z)[None, None, :, None] & (group == 0)
+    spread_norms = jnp.where(own_place, spread_norms, 0.0)
+    sums = sum_all(pack((jnp.sum(grad_act, axis=-1), jnp.sum(grad_act * hat_three, axis=-1), spread_norms)))
+
+    swapped = [
+        xor_move(lax.dynamic_index_in_dim(grad_project, z ^ m, 0, False), "head", m)
+        if m
+        else lax.dynamic_index_in_dim(grad_project, z, 0, False)
+        for m in range(heads)
+    ]
+    own_project = jnp.stack(in_order(swapped, z)).reshape(heads, quarter, 5, quarter)
+    own_project = jnp.moveaxis(own_project, 0, 2).reshape(-1, FEAT)
+    whole = jnp.concatenate(
+        [grad_taps, own_project, jnp.zeros((-flat_total % 16, FEAT), BF)], axis=0
+    )
+    framed = jnp.stack([whole[start : start + frame_rows] for start in frames])
+    sums, framed, dec_grad = tie(sums, framed, dec_grad)
+    aspp_steps = scatter_dp(framed, 0)
+    aspp_now = next(aspp_steps)
+    back_shift_three, back_gain_three, both = unpack(sums, (FEAT, FEAT, 8 * ASP))
+    both = both.reshape(2, 4 * ASP)
 
     def norm_back(grad_act, hat, gain, inv, back_shift, back_gain):
         scale = share / total_n
@@ -533,50 +668,63 @@
         ).astype(BF)
 
     grad_three = norm_back(grad_act, hat_three, gain_three, inv_three, back_shift_three, back_gain_three)
-    grad_expand = dot(grad_three, h_two, (1,), (1,))
     grad_act = dot(expand_w, grad_three, (0,), (0,)) * mask * silu_slope(in_two)
     sums = sum_all(pack((jnp.sum(grad_act, axis=-1), jnp.sum(grad_act * hat_two, axis=-1))))
+    grad_expand = dot(grad_three, h_two, (1,), (1,)).astype(BF).reshape(heads, n_dp, -1, BOT)
+    sums, grad_expand, aspp_now = tie(sums, grad_expand, aspp_now)
+    aspp_now = aspp_steps.send(aspp_now)
+    expand_steps = scatter_dp(grad_expand, 1)
+    expand_now = next(expand_steps)
     back_shift_two, back_gain_two = unpack(sums, (BOT, BOT))
     grad_two = norm_back(grad_act, hat_two, gain_two, inv_two, back_shift_two, back_gain_two)
     before = crop_shift(grad_two[:, -QUAD:], 1)
     after = crop_shift(grad_two[:, :QUAD], -1)
     columns = neck_columns(jnp.concatenate([before, grad_two, after], axis=1), True)
-    grad_middle = dot(columns, h_one, (2,), (1,))
     grad_h_one = lax.dot_general(middle, columns, (((0, 1), (0, 1)), ((), ())), preferred_element_type=F32)
     group_one = jnp.dot(reduce_w, x_group, preferred_element_type=F32)
     hat_one = normed(group_one, mean_one, inv_one)
     grad_act = grad_h_one * mask * silu_slope(scaled(hat_one, gain_one, shift_one))
     sums = sum_all(pack((jnp.sum(grad_act, axis=-1), jnp.sum(grad_act * hat_one, axis=-1))))
+    grad_middle = dot(columns, h_one, (2,), (1,)).astype(BF).reshape(9, heads, n_dp, -1, BOT)
+    sums, grad_middle, aspp_now, expand_now = tie(sums, grad_middle, aspp_now, expand_now)
+    aspp_block = last_step(aspp_steps, aspp_now)
+    expand_block = last_step(expand_steps, expand_now)
+    middle_steps = scatter_dp(grad_middle, 2)
+    middle_block = last_step(middle_steps, next(middle_steps))
     back_shift_one, back_gain_one = unpack(sums, (BOT, BOT))
     grad_one = norm_back(grad_act, hat_one, gain_one, inv_one, back_shift_one, back_gain_one)
-    grad_reduce = dot(grad_one, x_group, (1,), (1,))
-
-    swapped = lax.all_to_all(
-        grad_project.astype(BF).reshape(heads, quarter, 5 * quarter), "head", 0, 0, tiled=True
-    )
-    own_project = jnp.moveaxis(swapped.reshape(heads, quarter, 5, quarter), 0, 2).reshape(-1, FEAT)
-    flat_aspp = jnp.concatenate([grad_taps.astype(BF), own_project], axis=0).reshape(-1, 128)
-    shard_aspp = lax.psum_scatter(flat_aspp, "dp", scatter_dimension=0, tiled=True).astype(F32)[None]
-    flat_neck = jnp.concatenate(
-        [
-            grad_reduce.astype(BF).reshape(heads, -1),
-            jnp.moveaxis(grad_middle.astype(BF).reshape(9, heads, BOT // heads, BOT), 1, 0).reshape(heads, -1),
-            grad_expand.astype(BF).reshape(heads, -1),
-        ],
-        axis=1,
-    ).reshape(heads, -1, 128)
-    flat_neck = lax.psum_scatter(flat_neck, "dp", scatter_dimension=1, tiled=True)
-    shard_neck = lax.psum_scatter(flat_neck, "head", scatter_dimension=0, tiled=True).astype(F32)
-
-    both = lax.all_gather(jnp.stack([back_gain_aspp, back_shift_aspp]).reshape(2, 4, quarter), "head", axis=2)
-    both = both.reshape(2, 4 * ASP)
+    grad_reduce = dot(grad_one, x_group, (1,), (1,)).astype(BF).reshape(heads, n_dp, -1, FEAT)
+    reduce_steps = scatter_dp(grad_reduce, 1)
+    reduce_block = last_step(reduce_steps, next(reduce_steps))
+
+    shard_aspp = lax.dynamic_slice_in_dim(
+        aspp_block.astype(F32).reshape(frame_rows * 16, 128), inset, own_rows, 0
+    )[None]
+    expand_own = scatter_head(expand_block.reshape(heads, -1, BOT), z)
+    middle_own = scatter_head(jnp.moveaxis(middle_block.reshape(9, heads, -1, BOT), 1, 0), z)
+    reduce_own = scatter_head(reduce_block.reshape(heads, -1, FEAT), z)
+    expand_all = lax.all_gather(expand_own, "dp", axis=0, tiled=True)
+    middle_all = lax.all_gather(middle_own, "dp", axis=1, tiled=True)
+    reduce_all = lax.all_gather(reduce_own, "dp", axis=0, tiled=True)
+    neck_rows = jnp.concatenate(
+        [reduce_all.reshape(-1, BOT), middle_all.reshape(-1, BOT), expand_all], axis=0
+    )
+    shard_neck = lax.dynamic_slice_in_dim(
+        neck_rows, group * (neck_rows.shape[0] // n_dp), neck_rows.shape[0] // n_dp, 0
+    ).reshape(trunk_neck.shape)
+
     grad_norms = jnp.stack(
         [
             jnp.concatenate([back_gain_one, back_gain_two, back_gain_three, both[0], back_gain_proj]),
             jnp.concatenate([back_shift_one, back_shift_two, back_shift_three, both[1], back_shift_proj]),
         ]
     )
-    local_square = jnp.sum(shard_aspp * shard_aspp) + jnp.sum(shard_neck * shard_neck)
+    local_square = (
+        jnp.sum(shard_aspp * shard_aspp)
+        + jnp.sum(expand_own * expand_own)
+        + jnp.sum(middle_own * middle_own)
+        + jnp.sum(reduce_own * reduce_own)
+    )
     total_square = (
         sum_all(jnp.broadcast_to(local_square, (128,)))[0]
         + jnp.sum(grad_norms * grad_norms)

time: 1270 us -> 976 us (0.77)
  waiting for transfers between devices: 538 us -> 255 us
  starting transfers between devices: 146 us -> 199 us
  blocking collectives: 43.2 us -> 0 us
  local copies, waits for them, and re-layouts: 145 us -> 120 us
    psum x1, waiting for transfers between devices: 133 us -> 0.02 us  [shards(): lax.psum(jnp.concatenate([grad_hidden_w, *grad_out_w], axis=0), ('dp', 'h...]
    reduce_scatter x4 -> x0, waiting for transfers between devices: 128 us -> none  [the longest x1 58.3 us: shards(): lax.psum_scatter(flat_aspp, 'dp', scatter_dimension=0, tiled=True)]
    ppermute x63 -> x107, waiting for transfers between devices: 48.4 us -> 133 us  [xor_move(): return lax.ppermute(x, axis, [(i, i ^ mask) for i in range(n)])]
    ppermute x6, waiting for transfers between devices: 106 us -> 23.2 us  [line_shift(): lax.ppermute(x, 'head', [(i, i + by) for i in range(n) if 0 <= i + by < n])]
    ppermute x63 -> x107, starting transfers between devices: 78.2 us -> 143 us  [xor_move(): return lax.ppermute(x, axis, [(i, i ^ mask) for i in range(n)])]
    unnamed x223 -> x227, local copies, waits for them, and re-layouts: 75.3 us -> 21.8 us
    unnamed x10 -> x3, other arithmetic: 49.3 us -> 0.01 us
    all_gather x2 -> x0, blocking collectives: 43.2 us -> none  [the longest x1 29.7 us: shards(): project_w = lax.all_gather(project_q, 'head', axis=0, tiled=True)]
  transfers between devices with their start and end apart: 96 -> 136, of which waited for: 61 -> 53; matrix products, arithmetic and copies ran while one was open for 19% -> 34% of each run, Pallas kernels for 1% -> 3%
where the time goes in v2:
time: 976 us; the launch traced here: 966 us
  waiting for transfers between devices  255 us (26%)
  starting transfers between devices  199 us (20%)
  matrix products  198 us (20%)
  other arithmetic  137 us (14%)
  local copies, waits for them, and re-layouts  120 us (12%)
  Pallas kernels  31.7 us (3%)
  between operations  25.3 us (3%)
    ppermute x107, starting transfers between devices, xor_move(): return lax.ppermute(x, axis, [(i, i ^ mask) for i in range(n)])  143 us
    ppermute x107, waiting for transfers between devices, xor_move(): return lax.ppermute(x, axis, [(i, i ^ mask) for i in range(n)])  133 us
    dot_general x15, matrix products, dot(): lax.dot_general(a, b, ((ca, cb), ((), ())), preferred_element_type=F32)  113 us
    all_gather x1, waiting for transfers between devices, shards(): neck_low = lax.all_gather(neck_low, 'dp', axis=1, tiled=True)  45.9 us
    ppermute x16, starting transfers between devices, crop_shift(): return lax.ppermute(x, 'dp', pairs)  39.7 us
    all_gather x1, waiting for transfers between devices, shards(): neck_low = lax.all_gather(neck_low, 'head', axis=0, tiled=True)  32.5 us
    ppermute x6, waiting for transfers between devices, line_shift(): lax.ppermute(x, 'head', [(i, i + by) for i in range(n) if 0 <= i + by < n])  23.2 us
    unnamed x227, local copies, waits for them, and re-layouts  21.8 us
  transfers between devices with their start and end apart: 136, of which 53 were waited for; matrix products, arithmetic and copies ran while one was open for 34% of the time, Pallas kernels for 3%

profile of v2, /device:TPU:0, one launch (start us, length us, event | category | flops | bytes accessed | tf_op | source)
XLA Modules:
  0.0 966.0 jit_solution(890400662241971453)
XLA Ops:
  9.4 32.5 %all-gather.9.cloned.1.call-done = bf16[4,272,512]{2,1,0:T(8,128)(2,1)} async-done(((bf16[1,272,512]{2,1,0:T(8,128)(2,1)}), bf16[4,272,512]{2,1,0:T(8,128)(2,1)}) %all-gather.9.cloned.1.call-update) | async-done | bytes 1114128 | tf_op jit(solution)/shard_map/all_gather | solution.py:401
  43.6 4.6 collective-permute-start.15
  54.1 45.9 %all-gather.11.cloned.1.call-done = bf16[4,2176,512]{2,1,0:T(8,128)(2,1)} async-done(((bf16[4,272,512]{2,1,0:T(8,128)(2,1)}), bf16[4,2176,512]{2,1,0:T(8,128)(2,1)}) %all-gather.11.cloned.1.call-update) | async-done | bytes 8912912 | tf_op jit(solution)/shard_map/all_gather | solution.py:402
  99.9 4.1 fusion.203
  137.7 19.5 %all-gather.7.cloned.1.call-done.in_ref = bf16[8,256,2048]{2,1,0:T(8,128)(2,1)} async-done(((bf16[1,256,2048]{2,1,0:T(8,128)(2,1)}), bf16[8,256,2048]{2,1,0:T(8,128)(2,1)}) %all-gather.7.cloned.1.call-update) | async-done | bytes 8388624 | tf_op jit(solution)/shard_map/all_gather | solution.py:423
  157.2 6.3 shard_map.341
  163.9 5.2 collective-permute-done.11
  175.6 11.1 %slice_bitcast_fusion.66 = (bf16[2048,1856]{0,1:T(8,128)(2,1)}, bf16[1856,2048]{1,0:T(8,128)(2,1)}) fusion(bf16[1904,2048]{1,0:T(8,128)(2,1)} %copy-done), kind=kLoop, calls=%fused_computation.589 | loop fusion | bytes 22806528 | tf_op jit(solution)/shard_map/transpose | solution.py:431
  188.9 10.9 %collective-permute-start = (bf16[64,320]{0,1:T(8,128)(2,1)S(1)}, bf16[64,320]{0,1:T(8,128)(2,1)S(1)}, u32[]{:S(2)}, u32[]{:S(2)}) collective-permute-start(bf16[64,320]{0,1:T(8,128)(2,1)S(1)} %get-tuple-element.223), channel_id=1, source_target_pairs={{0,1},{1,0},{2,3},{3,2},{4,5},{5,4},{6,7},{7,6},{8,9},{9,8},{10,11... | collective-permute-start | bytes 122888 | tf_op jit(solution)/shard_map/ppermute | solution.py:42
  218.1 8.1 shard_map.342
  226.3 13.4 %multiply_reduce_fusion.2 = (f32[512]{0:T(512)S(1)}, f32[512]{0:T(512)S(1)}, f32[2048,512,1]{0,1,2:T(8,128)S(1)}) fusion(f32[2048]{0:T(1024)S(1)} %get-tuple-element.294, bf16[9,512,512]{2,1,0:T(8,128)(2,1)S(1)} %bitcast.625, bf16[9,512,2048]{2,1,0:T(8,128)(2,1)} %shard_map.342), kind=kOutput, calls=%fused_computation.17 | convolution fusion | flops 9667870720 | bytes 27799552 | tf_op jit(solution)/shard_map/dot_general | solution.py:493
  239.7 5.2 collective-permute-start.19
  250.5 4.7 collective-permute-start.27
  256.5 11.0 %multiply_reduce_fusion = (f32[2048]{0:T(1024)S(1)}, f32[2048]{0:T(1024)S(1)}, f32[2048,2048]{1,0:T(8,128)}) fusion(f32[2048]{0:T(1024)S(1)} %get-tuple-element.294, bf16[2048,512]{1,0:T(8,128)(2,1)S(1)} %bitcast.646, f32[2048,512,1]{0,1,2:T(8,128)S(1)} %get-tuple-element.286, f32[512]{0:T(512)S(1)} %bitcast.683, f32[512]{0:T(512)S(1)} %get-tuple-element.108, ...), kind=kOutput, calls=%fused_computation.1 | convolution fusion | flops 4322226176 | bytes 23101440 | tf_op jit(solution)/shard_map/dot_general | solution.py:498
  275.8 22.6 %collective-permute-done.28 = bf16[2048,512]{1,0:T(8,128)(2,1)S(1)} collective-permute-done((bf16[2048,512]{1,0:T(8,128)(2,1)}, bf16[2048,512]{1,0:T(8,128)(2,1)S(1)}, u32[]{:S(2)}, u32[]{:S(2)}) %collective-permute-start.28) | collective-permute-done | bytes 2097184 | tf_op jit(solution)/shard_map/ppermute | solution.py:104
  308.7 4.6 copy.134
  313.3 3.9 copy.135
  317.3 4.0 copy.136
  321.3 20.7 %multiply_convert_fusion.1 = bf16[2048,2048]{0,1:T(8,128)(2,1)S(1)} fusion(f32[2048]{0:T(1024)S(1)} %get-tuple-element.294, f32[2048]{0:T(1024)S(1)} %bitcast.668, f32[2048]{0:T(1024)S(1)} %get-tuple-element.263, f32[2048]{0:T(1024)S(1)} %get-tuple-element.264, f32[2048,2048]{1,0:T(8,128)} %get-tuple-element.287, f32[2048]{0:T(1024)S(1)} %bitcast.661, ...), kind=kLoop, calls=%fused_computation.8 | loop fusion | flops 88080384 | bytes 33599488 | tf_op jit(solution)/shard_map/convert_element_type | solution.py:510
  345.3 19.9 %fusion.217.p_ref = f32[1856,2048]{1,0:T(8,128)} fusion(bf16[1856,2048]{1,0:T(8,128)(2,1)} %get-tuple-element.38, bf16[2048,2048]{0,1:T(8,128)(2,1)S(1)} %multiply_convert_fusion.1), kind=kOutput, calls=%fused_computation.618 | convolution fusion | flops 15569256448 | bytes 31195136 | tf_op jit(solution)/shard_map/dot_general | solution.py:512
  365.2 7.1 shard_map.343
  384.7 5.6 collective-permute-start.33
  418.8 6.4 collective-permute-done.38
  425.2 12.0 %collective-permute-done.39 = bf16[256,512]{1,0:T(8,128)(2,1)} collective-permute-done((bf16[256,512]{1,0:T(8,128)(2,1)}, bf16[256,512]{1,0:T(8,128)(2,1)}, u32[]{:S(2)}, u32[]{:S(2)}) %collective-permute-start.39) | collective-permute-done | bytes 262176 | tf_op jit(solution)/shard_map/ppermute | solution.py:42
  448.0 4.0 collective-permute-start.45
  493.6 6.0 collective-permute-done.55
  499.6 8.8 collective-permute-done.56
  518.8 4.7 collective-permute-start.74
  544.4 5.3 collective-permute-start.64
  552.8 4.3 collective-permute-start.66
  567.6 16.3 %convolution_convert_fusion = bf16[1856,2048]{1,0:T(8,128)(2,1)S(1)} fusion(bf16[1856,2048]{1,0:T(8,128)(2,1)S(1)} %shard_map.344, bf16[2048,2048]{0,1:T(8,128)(2,1)S(1)} %bitcast.619), kind=kOutput, calls=%fused_computation.15 | convolution fusion | flops 15573057536 | bytes 23592960 | tf_op jit(solution)/shard_map/dot_general | solution.py:37
  589.8 42.4 %fusion.182 = (f32[2048]{0:T(1024)S(1)}, f32[2048]{0:T(1024)S(1)}, f32[2048,2048]{0,1:T(8,128)}) fusion(f32[2048]{0:T(1024)S(1)} %copy-done.57, f32[2048]{0:T(1024)S(1)} %copy-done.59, f32[2048,2048]{1,0:T(8,128)} %get-tuple-element.287, bf16[2048]{0:T(1024)(128)(2,1)S(1)} %copy-done.76, bf16[2048,512]{0,1:T(8,128)(2,1)} %bitcast.611, ...), kind=kOutput, calls=%fused_computation.593 | convolution fusion | flops 15682498560 | bytes 57208832 | tf_op jit(solution)/shard_map/dot_general | solution.py:37
  648.4 4.7 dynamic-slice_bitcast_fusion
  653.2 13.4 %multiply_convert_fusion = bf16[2048,2048]{0,1:T(8,128)(2,1)S(1)} fusion(f32[2048,2048]{0,1:T(8,128)} %get-tuple-element.291, f32[2048,2048]{1,0:T(8,128)} %get-tuple-element.287, f32[2048]{0:T(1024)S(1)} %get-tuple-element.261, f32[2048]{0:T(1024)S(1)} %get-tuple-element.260, f32[2048]{0:T(1024)S(1)} %copy-done.65, f32[2048]{0:T(1024)S(1)} %copy-done.57, ...), kind=kLoop, calls=%fused_computation.5 | loop fusion | flops 33554432 | bytes 41992192 | tf_op jit(solution)/shard_map/convert_element_type | solution.py:668
  666.7 10.5 %fusion.184 = (f32[512]{0:T(512)S(1)}, f32[512]{0:T(512)S(1)}, f32[512,2048]{1,0:T(8,128)}) fusion(f32[512]{0:T(512)S(1)} %copy-done.83, f32[512]{0:T(512)S(1)} %copy-done.85, f32[2048,512,1]{0,1,2:T(8,128)S(1)} %copy-done.22, f32[512]{0:T(512)S(1)} %bitcast.684, f32[512]{0:T(512)S(1)} %bitcast.676, f32[2048]{0:T(1024)S(1)} %get-tuple-element.294, ...), kind=kOutput, calls=%fused_computation.595 | convolution fusion | flops 4311743488 | bytes 18894848 | tf_op jit(solution)/shard_map/dot_general | solution.py:37
  690.3 11.4 %convolution_convert_fusion.2 = bf16[2048,512]{1,0:T(8,128)(2,1)} fusion(bf16[2048,2048]{0,1:T(8,128)(2,1)} %copy-done.18, f32[2048,512,1]{0,1,2:T(8,128)} %copy-done.21, f32[512]{0:T(512)S(1)} %bitcast.685, f32[512]{0:T(512)S(1)} %copy-done.83, f32[512]{0:T(512)S(1)} %copy-done.85, f32[2048]{0:T(1024)S(1)} %get-tuple-element.294, f32[512]{0:T(512)S(1)} %bitcast.677), kind=kOutput, calls=%fused_computation.49 | convolution fusion | flops 4306501632 | bytes 14696448 | tf_op jit(solution)/shard_map/dot_general | solution.py:37
  701.8 5.4 fusion.5
  707.2 4.9 multiply_convert_fusion.2
  715.0 14.5 %fusion.181 = f32[2048,512]{0,1:T(8,128)} fusion(bf16[512,2048]{1,0:T(8,128)(2,1)} %reshape.645, bf16[2048,512]{0,1:T(8,128)(2,1)S(1)} %bitcast.612, bf16[2048,512]{0,1:T(8,128)(2,1)S(1)} %bitcast.608, bf16[2048,512]{0,1:T(8,128)(2,1)S(1)} %bitcast.604, bf16[2048,512]{0,1:T(8,128)(2,1)S(1)} %bitcast.600, bf16[2048]{0:T(1024)(128)(2,1)S(1)} %copy-done.76), kind=kOutput, calls=%fused_computation.592 | convolution fusion | flops 4336910336 | bytes 14684160 | tf_op jit(solution)/shard_map/dot_general | solution.py:684
  736.4 7.8 shard_map.345
  744.2 19.0 %fusion.183 = (f32[512]{0:T(512)S(1)}, f32[512]{0:T(512)S(1)}, f32[512,2048]{1,0:T(8,128)}) fusion(f32[512]{0:T(512)S(1)} %copy-done.69, f32[2048,512]{0,1:T(8,128)} %fusion.181, f32[512]{0:T(512)S(1)} %copy-done.71, f32[512]{0:T(512)S(1)} %bitcast.672, f32[512]{0:T(512)S(1)} %bitcast.667, f32[2048]{0:T(1024)S(1)} %get-tuple-element.294, ...), kind=kOutput, calls=%fused_computation.594 | convolution fusion | flops 9680453632 | bytes 32002048 | tf_op jit(solution)/shard_map/dot_general | solution.py:683
  777.8 15.6 %convolution_convert_fusion.3 = bf16[9,512,512]{2,1,0:T(8,128)(2,1)} fusion(bf16[9,512,2048]{2,1,0:T(8,128)(2,1)} %shard_map.345, bf16[512,512]{1,0:T(8,128)(2,1)S(1)} %bitcast.634, bf16[512,512]{1,0:T(8,128)(2,1)S(1)} %bitcast.638, bf16[512,512]{1,0:T(8,128)(2,1)S(1)} %bitcast.637, bf16[512,512]{1,0:T(8,128)(2,1)S(1)} %bitcast.636), kind=kOutput, calls=%fused_computation.51 | convolution fusion | flops 9674424320 | bytes 25690112 | tf_op jit(solution)/shard_map/dot_general | solution.py:37
  799.6 8.8 convolution_convert_fusion.1
  825.4 12.4 %collective-permute-done.117 = bf16[4,1,2,16,1024]{4,3,2,0,1:T(8,128)(2,1)S(1)} collective-permute-done((bf16[4,1,2,16,1024]{4,3,2,0,1:T(8,128)(2,1)S(1)}, bf16[4,1,2,16,1024]{4,3,2,0,1:T(8,128)(2,1)S(1)}, u32[]{:S(2)}, u32[]{:S(2)}) %collective-permute-start.117) | collective-permute-done | bytes 262176 | tf_op jit(solution)/shard_map/ppermute | solution.py:42
  873.1 4.9 collective-permute-done.109
  879.5 19.1 %collective-permute-done.107 = bf16[9,4,2,1,16,256]{5,4,0,1,3,2:T(8,128)(2,1)} collective-permute-done((bf16[9,4,2,1,16,256]{5,4,0,1,3,2:T(8,128)(2,1)}, bf16[9,4,2,1,16,256]{5,4,0,1,3,2:T(8,128)(2,1)}, u32[]{:S(2)}, u32[]{:S(2)}) %collective-permute-start.107) | collective-permute-done | bytes 589856 | tf_op jit(solution)/shard_map/ppermute | solution.py:42
  903.3 5.7 collective-permute-done.108
  945.3 4.0 multiply_subtract_fusion.1
  (774 shorter events, 397.4 us)
Async XLA Ops:
  7.2 34.7 %all-gather.9.cloned.1.call-start = ((), (), s32[]{:S(2)}) async-start(), calls=%async_computation.1 | async-start | bytes 1392640 | tf_op jit(solution)/shard_map/all_gather | solution.py:401
  9.4 90.6 %all-gather.11.cloned.1.call-start = ((), (), s32[]{:S(2)}) async-start(), calls=%async_computation.2 | async-start | bytes 10027008 | tf_op jit(solution)/shard_map/all_gather | solution.py:402
  42.0 115.2 %all-gather.7.cloned.1.call-start = ((), (), s32[]{:S(2)}) async-start(), calls=%async_computation | async-start | bytes 9437184 | tf_op jit(solution)/shard_map/all_gather | solution.py:423
  43.6 604.8 %all-reduce.2.cloned.1.call-start = ((), (), s32[]{:S(2)}) async-start(), calls=%async_computation.3 | async-start | bytes 1622016 | tf_op jit(solution)/shard_map/psum | solution.py:578
  43.6 91.3 %collective-permute-start.15 = (bf16[2048,512]{1,0:T(8,128)(2,1)}, bf16[2048,512]{1,0:T(8,128)(2,1)}, u32[]{:S(2)}, u32[]{:S(2)}) collective-permute-start(bf16[2048,512]{1,0:T(8,128)(2,1)} %param.22), channel_id=1, source_target_pairs={{0,1},{1,2},{2,3},{4,5},{5,6},{6,7},{8,9},{9,10},{10,11},{12,13},{... | collective-permute-start | bytes 6291464 | tf_op jit(solution)/shard_map/ppermute | solution.py:104
  48.3 88.1 %collective-permute-start.17 = (bf16[2048,512]{1,0:T(8,128)(2,1)}, bf16[2048,512]{1,0:T(8,128)(2,1)}, u32[]{:S(2)}, u32[]{:S(2)}) collective-permute-start(bf16[2048,512]{1,0:T(8,128)(2,1)} %param.22), channel_id=1, source_target_pairs={{1,0},{2,1},{3,2},{5,4},{6,5},{7,6},{9,8},{10,9},{11,10},{13,12},{... | collective-permute-start | bytes 6291464 | tf_op jit(solution)/shard_map/ppermute | solution.py:104
  130.5 33.4 %collective-permute-start.10 = (bf16[512,512]{0,1:T(8,128)(2,1)}, bf16[512,512]{0,1:T(8,128)(2,1)}, u32[]{:S(2)}, u32[]{:S(2)}) collective-permute-start(bf16[512,512]{0,1:T(8,128)(2,1)} %multiply_convert_fusion.6), channel_id=1, source_target_pairs={{0,1},{1,0},{2,3},{3,2},{4,5},{5,4},{6,7},{7,6},{8,9},{9,8},{10,11... | collective-permute-start | bytes 1572872 | tf_op jit(solution)/shard_map/ppermute | solution.py:42
  130.5 38.6 %collective-permute-start.11 = (bf16[512,512]{0,1:T(8,128)(2,1)}, bf16[512,512]{0,1:T(8,128)(2,1)}, u32[]{:S(2)}, u32[]{:S(2)}) collective-permute-start(bf16[512,512]{0,1:T(8,128)(2,1)} %multiply_convert_fusion.6), channel_id=1, source_target_pairs={{0,2},{1,3},{2,0},{3,1},{4,6},{5,7},{6,4},{7,5},{8,10},{9,11},{10,... | collective-permute-start | bytes 1572872 | tf_op jit(solution)/shard_map/ppermute | solution.py:42
  131.6 37.5 %collective-permute-start.12 = (bf16[512,512]{0,1:T(8,128)(2,1)}, bf16[512,512]{0,1:T(8,128)(2,1)}, u32[]{:S(2)}, u32[]{:S(2)}) collective-permute-start(bf16[512,512]{0,1:T(8,128)(2,1)} %multiply_convert_fusion.6), channel_id=1, source_target_pairs={{0,3},{1,2},{2,1},{3,0},{4,7},{5,6},{6,5},{7,4},{8,11},{9,10},{10,... | collective-permute-start | bytes 1572872 | tf_op jit(solution)/shard_map/ppermute | solution.py:42
  135.0 91.3 %collective-permute-start.16 = (bf16[2048,512]{1,0:T(8,128)(2,1)}, bf16[2048,512]{1,0:T(8,128)(2,1)S(1)}, u32[]{:S(2)}, u32[]{:S(2)}) collective-permute-start(bf16[2048,512]{1,0:T(8,128)(2,1)} %collective-permute-done.15), channel_id=1, source_target_pairs={{0,1},{1,2},{2,3},{4,5},{5,6},{6,7},{8,9},{9,10},{10,11},{12,13},{... | collective-permute-start | bytes 6291464 | tf_op jit(solution)/shard_map/ppermute | solution.py:104
  136.4 89.8 %collective-permute-start.18 = (bf16[2048,512]{1,0:T(8,128)(2,1)}, bf16[2048,512]{1,0:T(8,128)(2,1)}, u32[]{:S(2)}, u32[]{:S(2)}) collective-permute-start(bf16[2048,512]{1,0:T(8,128)(2,1)} %collective-permute-done.17), channel_id=1, source_target_pairs={{1,0},{2,1},{3,2},{5,4},{6,5},{7,6},{9,8},{10,9},{11,10},{13,12},{... | collective-permute-start | bytes 6291464 | tf_op jit(solution)/shard_map/ppermute | solution.py:104
  173.4 35.1 %collective-permute-start.13 = (bf16[512,512]{1,0:T(8,128)(2,1)S(1)}, bf16[512,512]{1,0:T(8,128)(2,1)}, u32[]{:S(2)}, u32[]{:S(2)}) collective-permute-start(bf16[512,512]{1,0:T(8,128)(2,1)S(1)} %bitcast.633), channel_id=1, source_target_pairs={{0,4},{4,8},{8,12},{16,20},{20,24},{24,28},{1,5},{5,9},{9,13},{17,... | collective-permute-start | bytes 1572872 | tf_op jit(solution)/shard_map/ppermute | solution.py:99
  187.4 57.5 %collective-permute-start.2 = (bf16[64,320]{0,1:T(8,128)(2,1)S(1)}, bf16[64,320]{0,1:T(8,128)(2,1)S(1)}, u32[]{:S(2)}, u32[]{:S(2)}) collective-permute-start(bf16[64,320]{0,1:T(8,128)(2,1)S(1)} %get-tuple-element.221), channel_id=1, source_target_pairs={{0,3},{1,2},{2,1},{3,0},{4,7},{5,6},{6,5},{7,4},{8,11},{9,10},{10,... | collective-permute-start | bytes 122888 | tf_op jit(solution)/shard_map/ppermute | solution.py:42
  188.9 56.0 %collective-permute-start = (bf16[64,320]{0,1:T(8,128)(2,1)S(1)}, bf16[64,320]{0,1:T(8,128)(2,1)S(1)}, u32[]{:S(2)}, u32[]{:S(2)}) collective-permute-start(bf16[64,320]{0,1:T(8,128)(2,1)S(1)} %get-tuple-element.223), channel_id=1, source_target_pairs={{0,1},{1,0},{2,3},{3,2},{4,5},{5,4},{6,7},{7,6},{8,9},{9,8},{10,11... | collective-permute-start | bytes 122888 | tf_op jit(solution)/shard_map/ppermute | solution.py:42
  214.8 30.1 %collective-permute-start.1 = (bf16[64,320]{0,1:T(8,128)(2,1)S(1)}, bf16[64,320]{0,1:T(8,128)(2,1)S(1)}, u32[]{:S(2)}, u32[]{:S(2)}) collective-permute-start(bf16[64,320]{0,1:T(8,128)(2,1)S(1)} %get-tuple-element.222), channel_id=1, source_target_pairs={{0,2},{1,3},{2,0},{3,1},{4,6},{5,7},{6,4},{7,5},{8,10},{9,11},{10,... | collective-permute-start | bytes 122888 | tf_op jit(solution)/shard_map/ppermute | solution.py:42
  249.2 49.1 %collective-permute-start.28 = (bf16[2048,512]{1,0:T(8,128)(2,1)}, bf16[2048,512]{1,0:T(8,128)(2,1)S(1)}, u32[]{:S(2)}, u32[]{:S(2)}) collective-permute-start(bf16[2048,512]{1,0:T(8,128)(2,1)} %collective-permute-done.18), channel_id=1, source_target_pairs={{1,0},{2,1},{3,2},{5,4},{6,5},{7,6},{9,8},{10,9},{11,10},{13,12},{... | collective-permute-start | bytes 6291464 | tf_op jit(solution)/shard_map/ppermute | solution.py:104
  250.5 48.8 %collective-permute-start.27 = (bf16[2048,512]{1,0:T(8,128)(2,1)S(1)}, bf16[2048,512]{1,0:T(8,128)(2,1)S(1)}, u32[]{:S(2)}, u32[]{:S(2)}) collective-permute-start(bf16[2048,512]{1,0:T(8,128)(2,1)S(1)} %collective-permute-done.16), channel_id=1, source_target_pairs={{0,1},{1,2},{2,3},{4,5},{5,6},{6,7},{8,9},{9,10},{10,11},{12,13},{... | collective-permute-start | bytes 6291464 | tf_op jit(solution)/shard_map/ppermute | solution.py:104
  373.8 16.7 %collective-permute-start.31 = (bf16[5,64,512]{2,1,0:T(8,128)(2,1)}, bf16[5,64,512]{2,1,0:T(8,128)(2,1)}, u32[]{:S(2)}, u32[]{:S(2)}) collective-permute-start(bf16[5,64,512]{2,1,0:T(8,128)(2,1)} %pad_maximum_fusion.16), channel_id=1, source_target_pairs={{0,8},{4,12},{16,24},{20,28},{1,9},{5,13},{17,25},{21,29},{2,10},{... | collective-permute-start | bytes 983048 | tf_op jit(solution)/shard_map/ppermute | solution.py:99
  415.7 21.6 %collective-permute-start.39 = (bf16[256,512]{1,0:T(8,128)(2,1)}, bf16[256,512]{1,0:T(8,128)(2,1)}, u32[]{:S(2)}, u32[]{:S(2)}) collective-permute-start(bf16[256,512]{1,0:T(8,128)(2,1)} %get-tuple-element.184), channel_id=1, source_target_pairs={{0,2},{1,3},{2,0},{3,1},{4,6},{5,7},{6,4},{7,5},{8,10},{9,11},{10,... | collective-permute-start | bytes 786440 | tf_op jit(solution)/shard_map/ppermute | solution.py:42
  415.7 21.6 %collective-permute-start.40 = (bf16[256,512]{1,0:T(8,128)(2,1)S(1)}, bf16[256,512]{1,0:T(8,128)(2,1)}, u32[]{:S(2)}, u32[]{:S(2)}) collective-permute-start(bf16[256,512]{1,0:T(8,128)(2,1)S(1)} %get-tuple-element.183), channel_id=1, source_target_pairs={{0,3},{1,2},{2,1},{3,0},{4,7},{5,6},{6,5},{7,4},{8,11},{9,10},{10,... | collective-permute-start | bytes 786440 | tf_op jit(solution)/shard_map/ppermute | solution.py:42
  487.6 20.8 %collective-permute-start.56 = (bf16[256,512]{1,0:T(8,128)(2,1)S(1)}, bf16[256,512]{1,0:T(8,128)(2,1)S(1)}, u32[]{:S(2)}, u32[]{:S(2)}) collective-permute-start(bf16[256,512]{1,0:T(8,128)(2,1)S(1)} %multiply_convert_fusion.7), channel_id=1, source_target_pairs={{0,2},{1,3},{2,0},{3,1},{4,6},{5,7},{6,4},{7,5},{8,10},{9,11},{10,... | collective-permute-start | bytes 786440 | tf_op jit(solution)/shard_map/ppermute | solution.py:42
  489.6 18.8 %collective-permute-start.57 = (bf16[256,512]{1,0:T(8,128)(2,1)S(1)}, bf16[256,512]{1,0:T(8,128)(2,1)S(1)}, u32[]{:S(2)}, u32[]{:S(2)}) collective-permute-start(bf16[256,512]{1,0:T(8,128)(2,1)S(1)} %multiply_convert_fusion.7), channel_id=1, source_target_pairs={{0,3},{1,2},{2,1},{3,0},{4,7},{5,6},{6,5},{7,4},{8,11},{9,10},{10,... | collective-permute-start | bytes 786440 | tf_op jit(solution)/shard_map/ppermute | solution.py:42
  493.1 446.8 %all-gather.13.cloned.1.call-start = ((), (), s32[]{:S(2)}) async-start(), calls=%async_computation.4 | async-start | bytes 1179648 | tf_op jit(solution)/shard_map/all_gather | solution.py:708
  518.8 24.2 %collective-permute-start.74 = (bf16[64,320]{1,0:T(8,128)(2,1)}, bf16[64,320]{1,0:T(8,128)(2,1)}, u32[]{:S(2)}, u32[]{:S(2)}) collective-permute-start(bf16[64,320]{1,0:T(8,128)(2,1)} %get-tuple-element.247), channel_id=1, source_target_pairs={{0,1},{1,0},{2,3},{3,2},{4,5},{5,4},{6,7},{7,6},{8,9},{9,8},{10,11... | collective-permute-start | bytes 122888 | tf_op jit(solution)/shard_map/ppermute | solution.py:42
  523.6 20.8 %collective-permute-start.75 = (bf16[64,320]{1,0:T(8,128)(2,1)}, bf16[64,320]{1,0:T(8,128)(2,1)}, u32[]{:S(2)}, u32[]{:S(2)}) collective-permute-start(bf16[64,320]{1,0:T(8,128)(2,1)} %get-tuple-element.246), channel_id=1, source_target_pairs={{0,2},{1,3},{2,0},{3,1},{4,6},{5,7},{6,4},{7,5},{8,10},{9,11},{10,... | collective-permute-start | bytes 122888 | tf_op jit(solution)/shard_map/ppermute | solution.py:42
  523.6 26.1 %collective-permute-start.76 = (bf16[64,320]{1,0:T(8,128)(2,1)}, bf16[64,320]{1,0:T(8,128)(2,1)}, u32[]{:S(2)}, u32[]{:S(2)}) collective-permute-start(bf16[64,320]{1,0:T(8,128)(2,1)} %get-tuple-element.245), channel_id=1, source_target_pairs={{0,3},{1,2},{2,1},{3,0},{4,7},{5,6},{6,5},{7,4},{8,11},{9,10},{10,... | collective-permute-start | bytes 122888 | tf_op jit(solution)/shard_map/ppermute | solution.py:42
  535.6 17.2 %collective-permute-start.61 = (bf16[5,64,512]{2,1,0:T(8,128)(2,1)}, bf16[5,64,512]{2,1,0:T(8,128)(2,1)}, u32[]{:S(2)}, u32[]{:S(2)}) collective-permute-start(bf16[5,64,512]{2,1,0:T(8,128)(2,1)} %get-tuple-element.248), channel_id=1, source_target_pairs={{4,0},{8,4},{12,8},{20,16},{24,20},{28,24},{5,1},{9,5},{13,9},{21,... | collective-permute-start | bytes 983048 | tf_op jit(solution)/shard_map/ppermute | solution.py:99
  536.9 22.0 %collective-permute-start.62 = (bf16[5,64,512]{2,1,0:T(8,128)(2,1)S(1)}, bf16[5,64,512]{2,1,0:T(8,128)(2,1)}, u32[]{:S(2)}, u32[]{:S(2)}) collective-permute-start(bf16[5,64,512]{2,1,0:T(8,128)(2,1)S(1)} %get-tuple-element.250), channel_id=1, source_target_pairs={{0,4},{4,8},{8,12},{16,20},{20,24},{24,28},{1,5},{5,9},{9,13},{17,... | collective-permute-start | bytes 983048 | tf_op jit(solution)/shard_map/ppermute | solution.py:99
  543.1 18.6 %collective-permute-start.63 = (bf16[5,64,512]{2,1,0:T(8,128)(2,1)S(1)}, bf16[5,64,512]{2,1,0:T(8,128)(2,1)S(1)}, u32[]{:S(2)}, u32[]{:S(2)}) collective-permute-start(bf16[5,64,512]{2,1,0:T(8,128)(2,1)S(1)} %get-tuple-element.251), channel_id=1, source_target_pairs={{8,0},{12,4},{24,16},{28,20},{9,1},{13,5},{25,17},{29,21},{10,2},{... | collective-permute-start | bytes 983048 | tf_op jit(solution)/shard_map/ppermute | solution.py:99
  544.4 17.5 %collective-permute-start.64 = (bf16[5,64,512]{2,1,0:T(8,128)(2,1)S(1)}, bf16[5,64,512]{2,1,0:T(8,128)(2,1)}, u32[]{:S(2)}, u32[]{:S(2)}) collective-permute-start(bf16[5,64,512]{2,1,0:T(8,128)(2,1)S(1)} %get-tuple-element.249), channel_id=1, source_target_pairs={{0,8},{4,12},{16,24},{20,28},{1,9},{5,13},{17,25},{21,29},{2,10},{... | collective-permute-start | bytes 983048 | tf_op jit(solution)/shard_map/ppermute | solution.py:99
  653.1 48.6 %collective-permute-start.84 = (bf16[4,1,256,2048]{3,2,0,1:T(8,128)(2,1)}, bf16[4,1,256,2048]{3,2,0,1:T(8,128)(2,1)}, u32[]{:S(2)}, u32[]{:S(2)}) collective-permute-start(bf16[4,1,256,2048]{3,2,0,1:T(8,128)(2,1)} %dynamic-slice_bitcast_fusion), channel_id=1, source_target_pairs={{0,4},{4,0},{8,12},{12,8},{16,20},{20,16},{24,28},{28,24},{1,5},{5... | collective-permute-start | bytes 12582920 | tf_op jit(solution)/shard_map/ppermute | solution.py:42
  685.9 15.8 %collective-permute-start.81 = (f32[1024]{0:T(1024)S(1)}, f32[1024]{0:T(1024)S(1)}, u32[]{:S(2)}, u32[]{:S(2)}) collective-permute-start(f32[1024]{0:T(1024)S(1)} %add_add_fusion.8), channel_id=1, source_target_pairs={{0,1},{1,0},{2,3},{3,2},{4,5},{5,4},{6,7},{7,6},{8,9},{9,8},{10,11... | collective-permute-start | bytes 12296 | tf_op jit(solution)/shard_map/ppermute | solution.py:42
  685.9 15.8 %collective-permute-start.82 = (f32[1024]{0:T(1024)S(1)}, f32[1024]{0:T(1024)S(1)}, u32[]{:S(2)}, u32[]{:S(2)}) collective-permute-start(f32[1024]{0:T(1024)S(1)} %add_add_fusion.8), channel_id=1, source_target_pairs={{0,2},{1,3},{2,0},{3,1},{4,6},{5,7},{6,4},{7,5},{8,10},{9,11},{10,... | collective-permute-start | bytes 12296 | tf_op jit(solution)/shard_map/ppermute | solution.py:42
  712.2 23.8 %collective-permute-start.85 = (bf16[512,512]{1,0:T(8,128)(2,1)S(1)}, bf16[512,512]{1,0:T(8,128)(2,1)S(1)}, u32[]{:S(2)}, u32[]{:S(2)}) collective-permute-start(bf16[512,512]{1,0:T(8,128)(2,1)S(1)} %get-tuple-element.138), channel_id=1, source_target_pairs={{0,4},{4,8},{8,12},{16,20},{20,24},{24,28},{1,5},{5,9},{9,13},{17,... | collective-permute-start | bytes 1572872 | tf_op jit(solution)/shard_map/ppermute | solution.py:99
  713.6 22.4 %collective-permute-start.86 = (bf16[512,512]{1,0:T(8,128)(2,1)S(1)}, bf16[512,512]{1,0:T(8,128)(2,1)S(1)}, u32[]{:S(2)}, u32[]{:S(2)}) collective-permute-start(bf16[512,512]{1,0:T(8,128)(2,1)S(1)} %get-tuple-element.139), channel_id=1, source_target_pairs={{4,0},{8,4},{12,8},{20,16},{24,20},{28,24},{5,1},{9,5},{13,9},{21,... | collective-permute-start | bytes 1572872 | tf_op jit(solution)/shard_map/ppermute | solution.py:99
  734.3 59.1 %collective-permute-start.96 = (bf16[4,4,1,64,512]{4,3,1,0,2:T(8,128)(2,1)S(1)}, bf16[4,4,1,64,512]{4,3,1,0,2:T(8,128)(2,1)}, u32[]{:S(2)}, u32[]{:S(2)}) collective-permute-start(bf16[4,4,1,64,512]{4,3,1,0,2:T(8,128)(2,1)S(1)} %dynamic-slice_bitcast_fusion.3), channel_id=1, source_target_pairs={{0,4},{4,0},{8,12},{12,8},{16,20},{20,16},{24,28},{28,24},{1,5},{5... | collective-permute-start | bytes 3145736 | tf_op jit(solution)/shard_map/ppermute | solution.py:42
  768.0 27.5 %collective-permute-start.95 = (bf16[1,2,256,1024]{3,2,1,0:T(8,128)(2,1)S(1)}, bf16[1,2,256,1024]{3,2,1,0:T(8,128)(2,1)}, u32[]{:S(2)}, u32[]{:S(2)}) collective-permute-start(bf16[1,2,256,1024]{3,2,1,0:T(8,128)(2,1)S(1)} %dynamic-slice_bitcast_fusion.4), channel_id=1, source_target_pairs={{0,16},{4,20},{8,24},{12,28},{16,0},{20,4},{24,8},{28,12},{1,17},{... | collective-permute-start | bytes 3145736 | tf_op jit(solution)/shard_map/ppermute | solution.py:42
  772.9 25.0 %collective-permute-start.94 = (bf16[2,1,256,1024]{3,2,0,1:T(8,128)(2,1)}, bf16[2,1,256,1024]{3,2,0,1:T(8,128)(2,1)}, u32[]{:S(2)}, u32[]{:S(2)}) collective-permute-start(bf16[2,1,256,1024]{3,2,0,1:T(8,128)(2,1)} %dynamic-slice_bitcast_fusion.5), channel_id=1, source_target_pairs={{0,8},{4,12},{8,0},{12,4},{16,24},{20,28},{24,16},{28,20},{1,9},{5... | collective-permute-start | bytes 3145736 | tf_op jit(solution)/shard_map/ppermute | solution.py:42
  773.0 20.4 %collective-permute-start.92 = (f32[1024]{0:T(1024)S(1)}, f32[1024]{0:T(1024)S(1)}, u32[]{:S(2)}, u32[]{:S(2)}) collective-permute-start(f32[1024]{0:T(1024)S(1)} %add_add_fusion.6), channel_id=1, source_target_pairs={{0,2},{1,3},{2,0},{3,1},{4,6},{5,7},{6,4},{7,5},{8,10},{9,11},{10,... | collective-permute-start | bytes 12296 | tf_op jit(solution)/shard_map/ppermute | solution.py:42
  775.9 17.5 %collective-permute-start.93 = (f32[1024]{0:T(1024)S(1)}, f32[1024]{0:T(1024)S(1)}, u32[]{:S(2)}, u32[]{:S(2)}) collective-permute-start(f32[1024]{0:T(1024)S(1)} %add_add_fusion.6), channel_id=1, source_target_pairs={{0,3},{1,2},{2,1},{3,0},{4,7},{5,6},{6,5},{7,4},{8,11},{9,10},{10,... | collective-permute-start | bytes 12296 | tf_op jit(solution)/shard_map/ppermute | solution.py:42
  812.0 44.3 %collective-permute-start.106 = (bf16[9,4,4,1,16,512]{5,4,2,1,0,3:T(8,128)(2,1)}, bf16[9,4,4,1,16,512]{5,4,2,1,0,3:T(8,128)(2,1)}, u32[]{:S(2)}, u32[]{:S(2)}) collective-permute-start(bf16[9,4,4,1,16,512]{5,4,2,1,0,3:T(8,128)(2,1)} %dynamic-slice_bitcast_fusion.1), channel_id=1, source_target_pairs={{0,4},{4,0},{8,12},{12,8},{16,20},{20,16},{24,28},{28,24},{1,5},{5... | collective-permute-start | bytes 7077896 | tf_op jit(solution)/shard_map/ppermute | solution.py:42
  816.3 84.9 %collective-permute-start.97 = (bf16[1,1,256,1024]{3,2,1,0:T(8,128)(2,1)}, bf16[1,1,256,1024]{3,2,1,0:T(8,128)(2,1)}, u32[]{:S(2)}, u32[]{:S(2)}) collective-permute-start(bf16[1,1,256,1024]{3,2,1,0:T(8,128)(2,1)} %dynamic-slice_bitcast_fusion.7), channel_id=1, source_target_pairs={{0,16},{4,20},{8,24},{12,28},{16,0},{20,4},{24,8},{28,12},{1,17},{... | collective-permute-start | bytes 1572872 | tf_op jit(solution)/shard_map/ppermute | solution.py:42
  855.1 98.7 %all-gather.17.cloned.1.call-start = ((), (), s32[]{:S(2)}) async-start(), calls=%async_computation.6 | async-start | bytes 1179648 | tf_op jit(solution)/shard_map/all_gather | solution.py:706
  862.1 15.9 %collective-permute-start.109 = (bf16[9,4,1,2,16,256]{5,4,0,1,3,2:T(8,128)(2,1)}, bf16[9,4,1,2,16,256]{5,4,0,1,3,2:T(8,128)(2,1)}, u32[]{:S(2)}, u32[]{:S(2)}) collective-permute-start(bf16[9,4,1,2,16,256]{5,4,0,1,3,2:T(8,128)(2,1)} %bitcast.592), channel_id=1, source_target_pairs={{0,16},{4,20},{8,24},{12,28},{16,0},{20,4},{24,8},{28,12},{1,17},{... | collective-permute-start | bytes 1769480 | tf_op jit(solution)/shard_map/ppermute | solution.py:42
  869.4 44.2 %collective-permute-start.98 = (bf16[1,1,256,1024]{3,2,1,0:T(8,128)(2,1)}, bf16[1,1,256,1024]{3,2,1,0:T(8,128)(2,1)}, u32[]{:S(2)}, u32[]{:S(2)}) collective-permute-start(bf16[1,1,256,1024]{3,2,1,0:T(8,128)(2,1)} %dynamic-slice_bitcast_fusion.6), channel_id=1, source_target_pairs={{0,8},{4,12},{8,0},{12,4},{16,24},{20,28},{24,16},{28,20},{1,9},{5... | collective-permute-start | bytes 1572872 | tf_op jit(solution)/shard_map/ppermute | solution.py:42
  869.6 29.0 %collective-permute-start.107 = (bf16[9,4,2,1,16,256]{5,4,0,1,3,2:T(8,128)(2,1)}, bf16[9,4,2,1,16,256]{5,4,0,1,3,2:T(8,128)(2,1)}, u32[]{:S(2)}, u32[]{:S(2)}) collective-permute-start(bf16[9,4,2,1,16,256]{5,4,0,1,3,2:T(8,128)(2,1)} %bitcast.593), channel_id=1, source_target_pairs={{0,8},{4,12},{8,0},{12,4},{16,24},{20,28},{24,16},{28,20},{1,9},{5... | collective-permute-start | bytes 1769480 | tf_op jit(solution)/shard_map/ppermute | solution.py:42
  872.8 81.1 %all-gather.15.cloned.1.call-start = ((), (), s32[]{:S(2)}) async-start(), calls=%async_computation.5 | async-start | bytes 2654208 | tf_op jit(solution)/shard_map/all_gather | solution.py:707
  879.5 23.7 %collective-permute-start.110 = (bf16[9,4,1,1,16,256]{5,4,0,1,3,2:T(8,128)(2,1)S(1)}, bf16[9,4,1,1,16,256]{5,4,0,1,3,2:T(8,128)(2,1)S(1)}, u32[]{:S(2)}, u32[]{:S(2)}) collective-permute-start(bf16[9,4,1,1,16,256]{5,4,0,1,3,2:T(8,128)(2,1)S(1)} %constant_dynamic-slice_fusion.4), channel_id=1, source_target_pairs={{0,8},{4,12},{8,0},{12,4},{16,24},{20,28},{24,16},{28,20},{1,9},{5... | collective-permute-start | bytes 884744 | tf_op jit(solution)/shard_map/ppermute | solution.py:42
  (197 other events, 2821.9 us)
Sparse Core Ops, SparseCore 0:
  10.2 31.6 all-gather.8
  43.8 56.0 all-gather.10
  102.4 54.7 all-gather.6
  493.2 128.4 all-reduce.1
  855.2 25.4 all-gather.12
  883.0 25.6 all-gather.16
  920.7 27.6 all-gather.14

commit v3 on v2

--- a/solution.py
+++ b/solution.py
@@ -2,6 +2,7 @@
 
 import jax
 import jax.numpy as jnp
+import numpy as np
 from jax import lax
 from jax.experimental import pallas as pl
 from jax.experimental.pallas import tpu as pltpu
@@ -138,11 +139,16 @@
     n = lax.axis_size("dp")
     position = lax.axis_index("dp")
     bits = [1 << k for k in range(n.bit_length() - 1)]
-    t, bits = halve(t, axis, bits, 1, position)
-    t = yield (t,)
-    t = t[0]
-    half = t.shape[-1] // 2
-    parts = [(t[..., :half], bits), (t[..., half:], bits)]
+    if not isinstance(t, tuple):
+        t, bits = halve(t, axis, bits, 1, position)
+        t = yield (t,)
+        t = t[0]
+        half = t.shape[-1] // 2
+        parts = [(t[..., :half], bits), (t[..., half:], bits)]
+    else:
+        parts = [halve(part, axis, bits, 1, position) for part in t]
+        arrays = yield tuple(part for part, _ in parts)
+        parts = [(array, left) for array, (_, left) in zip(arrays, parts)]
     order = [1 << k for k in range(1, n.bit_length() - 1)]
     for k in range(0, len(order), 2):
         pair = order[k : k + 2]
@@ -158,6 +164,10 @@
 
 def tie(*trees):
     return lax.optimization_barrier(trees)
+
+
+def held_until(value, *others):
+    return lax.optimization_barrier((value, others))[0]
 
 
 def last_step(steps, now):
@@ -205,6 +215,9 @@
     )(ext)
 
 
+TAP_STEP = 240
+
+
 def frames_of(own_rows, n_dp):
     starts = [own_rows * s // 256 * 16 for s in range(n_dp)]
     ends = [-(-own_rows * (s + 1) // 16) for s in range(n_dp)]
@@ -219,14 +232,17 @@
             part = in_ref[s, at : at + stop - start, :]
             total = part if total is None else total + part
         out_ref[start:stop, :] = total
+    end = pieces[-1][1]
+    if end < out_ref.shape[0]:
+        out_ref[end:, :] = jnp.zeros((out_ref.shape[0] - end, out_ref.shape[1]), BF)
 
 
 def assemble(framed, own_rows, total_rows):
     n_dp, frame_rows, width = framed.shape
     starts, _ = frames_of(own_rows, n_dp)
-    rows = -(-total_rows // 16) * 16
+    rows = -(-total_rows // TAP_STEP) * TAP_STEP
     pieces = []
-    for g in range(0, rows, 16):
+    for g in range(0, -(-total_rows // 16) * 16, 16):
         sources = tuple(
             (s, g - starts[s])
             for s in range(n_dp)
@@ -248,55 +264,270 @@
     )(framed)
 
 
-def aspp_gather_kernel(p_ref, core_ref, side_ref, pool_ref):
-    lanes = lax.broadcasted_iota(jnp.int32, (64, WIDTH), 1)
-    core_ref[0] = p_ref[0:64, :]
-    pool_sum = jnp.zeros((64, WIDTH), F32)
-    for t in range(4):
-        part = slice(t * WIDTH, (t + 1) * WIDTH)
-        pool_sum = pool_sum + p_ref[64 * 28 : 64 * 29, part]
-        for br, rate in enumerate(RATES):
-            for i in range(3):
-                total = None
-                for j in range(3):
-                    at = 64 * (1 + 9 * br + 3 * i + j)
-                    moved = shift_lanes(p_ref[at : at + 64, part], (j - 1) * rate, lanes)
-                    total = moved if total is None else total + moved
-                if i == 1:
-                    core_ref[1 + br, :, part] = total
-                else:
-                    side_ref[2 * br + i // 2, 0, :, part] = total.astype(BF)
-    pool_ref[0] = pool_sum
-
-
-def aspp_gather(products):
-    rows, width = products.shape
+def whole(shape):
+    return pl.BlockSpec(shape, lambda *_: (0,) * len(shape), pipeline_mode=pl.Buffered(1))
+
+
+def lane_parts(value):
+    total = value[:, :WIDTH]
+    for t in range(1, value.shape[1] // WIDTH):
+        total = total + value[:, t * WIDTH : (t + 1) * WIDTH]
+    return total
+
+
+def sigmoid_of(value):
+    return 0.5 * jnp.tanh(0.5 * value) + 0.5
+
+
+def shift_quad(value, by, lanes):
+    return jnp.concatenate(
+        [shift_lanes(value[:, t * WIDTH : (t + 1) * WIDTH], by, lanes) for t in range(4)], axis=1
+    )
+
+
+def neck_conv_kernel(z_ref, s0, s1, s2, s3, before, after, w_ref, mask_ref, out_ref, own_ref, one_ref, two_ref, ext):
+    a = pl.program_id(0)
+
+    @pl.when(a == 0)
+    def _():
+        z = z_ref[0]
+        ext[0] = before[...]
+        ext[5] = after[...]
+        for m, slot in enumerate((s0, s1, s2, s3)):
+            ext[1 + jnp.bitwise_xor(z, m)] = slot[...]
+        one_ref[...] = jnp.zeros_like(one_ref)
+        two_ref[...] = jnp.zeros_like(two_ref)
+
+    own_ref[...] = ext[a + 1]
+    rows = out_ref.shape[0]
+    lanes = lax.broadcasted_iota(jnp.int32, (rows, WIDTH), 1)
+    for j in (1, 0, 2):
+        total = None
+        for i in range(3):
+            part = jnp.dot(w_ref[3 * i + j], ext[a + i], preferred_element_type=F32)
+            total = part if total is None else total + part
+        if j == 1:
+            out_ref[...] = total
+        else:
+            out_ref[...] += shift_quad(total, (j - 1) * 4, lanes)
+    value = out_ref[...]
+    masked = value * mask_ref[0:1, :]
+    one_ref[...] += lane_parts(masked)
+    two_ref[...] += lane_parts(masked * value)
+
+
+def neck_conv(z, slots, before, after, weights, mask8):
+    rows = weights.shape[1]
+    width = mask8.shape[1]
+    block = lambda a, z_ref: (0, a)
+    return pl.pallas_call(
+        neck_conv_kernel,
+        grid_spec=pltpu.PrefetchScalarGridSpec(
+            num_scalar_prefetch=1,
+            grid=(width // QUAD,),
+            in_specs=[whole(before.shape)] * 6
+            + [whole(weights.shape), pl.BlockSpec((8, QUAD), block)],
+            out_specs=[
+                pl.BlockSpec((rows, QUAD), block),
+                pl.BlockSpec((rows, QUAD), block),
+                pl.BlockSpec((rows, WIDTH), lambda a, z_ref: (0, 0)),
+                pl.BlockSpec((rows, WIDTH), lambda a, z_ref: (0, 0)),
+            ],
+            scratch_shapes=[pltpu.VMEM((6, rows, QUAD), BF)],
+        ),
+        out_shape=[
+            jax.ShapeDtypeStruct((rows, width), F32),
+            jax.ShapeDtypeStruct((rows, width), BF),
+            jax.ShapeDtypeStruct((rows, WIDTH), F32),
+            jax.ShapeDtypeStruct((rows, WIDTH), F32),
+        ],
+        compiler_params=pltpu.CompilerParams(vmem_limit_bytes=48 << 20),
+        cost_estimate=pl.CostEstimate(flops=18 * rows * rows * width, bytes_accessed=16 << 20, transcendentals=0),
+    )(z.reshape(1), *slots, before, after, weights, mask8)
+
+
+CHUNK = 256
+
+
+def fetch_quad(away, sources, buffer, sem):
+    for k, source in zip((0, 1, 2, 3, -1, -2, -3), sources):
+
+        @pl.when(away == k)
+        def _():
+            pltpu.make_async_copy(source, buffer, sem).start()
+
+
+def feature_group_kernel(z_ref, mask_ref, x0, x1, x2, x3, x4, x5, x6, out_ref, xbuf, sem):
+    sources = (x0, x1, x2, x3, x4, x5, x6)
+    fetch_quad(pl.program_id(0) - z_ref[0], sources, xbuf, sem)
+    pltpu.make_async_copy(x0, xbuf, sem).wait()
+    mask = mask_ref[0:1, :]
+
+    def place(i, carry):
+        at = pl.ds(pl.multiple_of(i * CHUNK, CHUNK), CHUNK)
+        out_ref[at, :] = (xbuf[at, :].astype(F32) * mask).astype(BF)
+        return carry
+
+    lax.fori_loop(0, out_ref.shape[0] // CHUNK, place, 0)
+
+
+def feature_group(z, mask8, sources):
+    rows = sources[0].shape[0]
+    width = mask8.shape[1]
+    block = lambda a, z_ref: (0, a)
+    return pl.pallas_call(
+        feature_group_kernel,
+        grid_spec=pltpu.PrefetchScalarGridSpec(
+            num_scalar_prefetch=1,
+            grid=(width // QUAD,),
+            in_specs=[pl.BlockSpec((8, QUAD), block)] + [pl.BlockSpec(memory_space=pl.ANY)] * 7,
+            out_specs=pl.BlockSpec((rows, QUAD), block),
+            scratch_shapes=[pltpu.VMEM((rows, QUAD), BF), pltpu.SemaphoreType.DMA],
+        ),
+        out_shape=jax.ShapeDtypeStruct((rows, width), BF),
+        compiler_params=pltpu.CompilerParams(vmem_limit_bytes=32 << 20),
+        cost_estimate=pl.CostEstimate(flops=0, bytes_accessed=4 * rows * width, transcendentals=0),
+    )(z.reshape(1), mask8, *sources)
+
+
+def aspp_forward_kernel(
+    z_ref, pre_ref, coef_ref, mask_ref, w_ref, x0, x1, x2, x3, x4, x5, x6,
+    y_ref, slope_ref, core_ref, side_ref, pool_ref, xbuf, held, products, sem
+):
+    a = pl.program_id(0)
+    quads = pl.num_programs(0) - 1
+    sources = (x0, x1, x2, x3, x4, x5, x6)
+    slot = a % 2
+    channels = y_ref.shape[0]
+    steps = w_ref.shape[0] // TAP_STEP
+    chunk = channels // steps
+
+    @pl.when(a == 0)
+    def _():
+        fetch_quad(-z_ref[0], sources, xbuf.at[0], sem.at[0])
+
+    @pl.when(a < quads)
+    def _():
+        pltpu.make_async_copy(x0, xbuf.at[slot], sem.at[slot]).wait()
+
+    @pl.when(a + 1 < quads)
+    def _():
+        fetch_quad(a + 1 - z_ref[0], sources, xbuf.at[1 - slot], sem.at[1 - slot])
+
+    mask = mask_ref[0:1, :]
+
+    def activate(i):
+        at = pl.ds(pl.multiple_of(i * chunk, chunk), chunk)
+        x = xbuf[slot, at, :].astype(F32) * mask
+        value = pre_ref[at, :].astype(F32) * coef_ref[at, 0:1] + coef_ref[at, 1:2] + x
+        sig = sigmoid_of(value)
+        y_ref[at, :] = (value * sig * mask).astype(BF)
+        slope_ref[at, :] = (sig * (1.0 + value * (1.0 - sig)) * mask).astype(BF)
+
+    def multiply(i):
+        at = pl.ds(pl.multiple_of(i * TAP_STEP, 16), TAP_STEP)
+        products[at, :] = jnp.dot(w_ref[at, :], held[...], preferred_element_type=F32)
+
+    @pl.when(a == 0)
+    def _():
+        lax.fori_loop(0, steps, lambda i, c: (activate(i), c)[1], 0)
+
+    @pl.when((a > 0) & (a < quads))
+    def _():
+        def both(i, carry):
+            multiply(i)
+            activate(i)
+            return carry
+
+        lax.fori_loop(0, steps, both, 0)
+
+    @pl.when(a == quads)
+    def _():
+        lax.fori_loop(0, steps, lambda i, c: (multiply(i), c)[1], 0)
+
+    held[...] = y_ref[...]
+
+    @pl.when(a > 0)
+    def _():
+        lanes = lax.broadcasted_iota(jnp.int32, (64, WIDTH), 1)
+        core_ref[0] = products[0:64, :]
+        pool_ref[0] = lane_parts(products[64 * 28 : 64 * 29, :])
+        for t in range(4):
+            part = slice(t * WIDTH, (t + 1) * WIDTH)
+            for br, rate in enumerate(RATES):
+                for i in range(3):
+                    total = None
+                    for j in range(3):
+                        row = 64 * (1 + 9 * br + 3 * i + j)
+                        moved = shift_lanes(products[row : row + 64, part], (j - 1) * rate, lanes)
+                        total = moved if total is None else total + moved
+                    if i == 1:
+                        core_ref[1 + br, :, part] = total
+                    else:
+                        side_ref[2 * br + i // 2, 0, :, part] = total.astype(BF)
+
+
+def aspp_forward(z, pre, coef, mask8, weights, sources):
+    rows, width = pre.shape
     quads = width // QUAD
+    now = lambda a: jnp.minimum(a, quads - 1)
+    done = lambda a: jnp.maximum(a - 1, 0)
+    wide = pl.BlockSpec((rows, QUAD), lambda a, z_ref: (0, now(a)))
     return pl.pallas_call(
-        aspp_gather_kernel,
-        grid=(quads,),
-        in_specs=[pl.BlockSpec((rows, QUAD), lambda a: (0, a))],
-        out_specs=[
-            pl.BlockSpec((4, 64, QUAD), lambda a: (0, 0, a)),
-            pl.BlockSpec((6, 1, 64, QUAD), lambda a: (0, a, 0, 0)),
-            pl.BlockSpec((1, 64, WIDTH), lambda a: (a, 0, 0)),
-        ],
+        aspp_forward_kernel,
+        grid_spec=pltpu.PrefetchScalarGridSpec(
+            num_scalar_prefetch=1,
+            grid=(quads + 1,),
+            in_specs=[
+                wide,
+                whole(coef.shape),
+                pl.BlockSpec((8, QUAD), lambda a, z_ref: (0, now(a))),
+                whole(weights.shape),
+            ]
+            + [pl.BlockSpec(memory_space=pl.ANY)] * 7,
+            out_specs=[
+                wide,
+                wide,
+                pl.BlockSpec((4, 64, QUAD), lambda a, z_ref: (0, 0, done(a))),
+                pl.BlockSpec((6, 1, 64, QUAD), lambda a, z_ref: (0, done(a), 0, 0)),
+                pl.BlockSpec((1, 64, WIDTH), lambda a, z_ref: (done(a), 0, 0)),
+            ],
+            scratch_shapes=[
+                pltpu.VMEM((2, rows, QUAD), BF),
+                pltpu.VMEM((rows, QUAD), BF),
+                pltpu.VMEM((weights.shape[0], QUAD), F32),
+                pltpu.SemaphoreType.DMA((2,)),
+            ],
+        ),
         out_shape=[
+            jax.ShapeDtypeStruct((rows, width), BF),
+            jax.ShapeDtypeStruct((rows, width), BF),
             jax.ShapeDtypeStruct((4, 64, width), F32),
             jax.ShapeDtypeStruct((6, quads, 64, QUAD), BF),
             jax.ShapeDtypeStruct((quads, 64, WIDTH), F32),
         ],
-        compiler_params=pltpu.CompilerParams(vmem_limit_bytes=40 << 20),
-        cost_estimate=pl.CostEstimate(flops=0, bytes_accessed=5 * rows * width, transcendentals=0),
-    )(products)
-
-
-def aspp_spread_kernel(one_ref, rows_ref, pool_ref, mask_ref, out_ref):
+        compiler_params=pltpu.CompilerParams(vmem_limit_bytes=58 << 20),
+        cost_estimate=pl.CostEstimate(
+            flops=2 * 29 * 64 * rows * width, bytes_accessed=48 << 20, transcendentals=rows * width
+        ),
+    )(z.reshape(1), pre, coef, mask8, weights, *sources)
+
+
+def aspp_backward_kernel(
+    one_ref, rows_ref, pool_in, mask_ref, w_ref, slope_ref, pre_ref,
+    out_ref, act_ref, sum_ref, dot_ref
+):
+    @pl.when(pl.program_id(0) == 0)
+    def _():
+        sum_ref[...] = jnp.zeros_like(sum_ref)
+        dot_ref[...] = jnp.zeros_like(dot_ref)
+
     lanes = lax.broadcasted_iota(jnp.int32, (64, WIDTH), 1)
     out_ref[0:64, :] = one_ref[...].astype(BF)
+    out_ref[64 * 29 :, :] = jnp.zeros((out_ref.shape[0] - 64 * 29, QUAD), BF)
     for t in range(4):
         part = slice(t * WIDTH, (t + 1) * WIDTH)
-        out_ref[64 * 28 : 64 * 29, part] = (pool_ref[...] * mask_ref[0:1, part]).astype(BF)
+        out_ref[64 * 28 : 64 * 29, part] = (pool_in[...] * mask_ref[0:1, part]).astype(BF)
         for br, rate in enumerate(RATES):
             for i in range(3):
                 tile = rows_ref[br, i, 0, :, part].astype(F32)
@@ -304,37 +535,101 @@
                     at = 64 * (1 + 9 * br + 3 * i + j)
                     out_ref[at : at + 64, part] = shift_lanes(tile, (1 - j) * rate, lanes).astype(BF)
 
-
-def aspp_spread(one, rows, pool, mask):
-    width = one.shape[1]
+    def multiply(i, carry):
+        at = pl.ds(pl.multiple_of(i * CHUNK, CHUNK), CHUNK)
+        grad = jnp.dot(w_ref[at, :], out_ref[...], preferred_element_type=F32)
+        act = grad * slope_ref[at, :].astype(F32)
+        act_ref[at, :] = act.astype(BF)
+        sum_ref[at, :] += lane_parts(act)
+        dot_ref[at, :] += lane_parts(act * pre_ref[at, :].astype(F32))
+        return carry
+
+    lax.fori_loop(0, act_ref.shape[0] // CHUNK, multiply, 0)
+
+
+def aspp_backward(one, rows, pool, mask8, weights_t, slope, pre):
+    channels, width = pre.shape
     quads = width // QUAD
-    count = 64 * 29
+    count = weights_t.shape[1]
+    block = lambda a: (0, a)
+    wide = pl.BlockSpec((channels, QUAD), block)
     return pl.pallas_call(
-        aspp_spread_kernel,
+        aspp_backward_kernel,
         grid=(quads,),
         in_specs=[
-            pl.BlockSpec((64, QUAD), lambda a: (0, a)),
+            pl.BlockSpec((64, QUAD), block),
             pl.BlockSpec((3, 3, 1, 64, QUAD), lambda a: (0, 0, a, 0, 0)),
-            pl.BlockSpec((64, WIDTH), lambda a: (0, 0)),
-            pl.BlockSpec((8, QUAD), lambda a: (0, a)),
+            whole((64, WIDTH)),
+            pl.BlockSpec((8, QUAD), block),
+            whole(weights_t.shape),
+            wide,
+            wide,
         ],
-        out_specs=pl.BlockSpec((count, QUAD), lambda a: (0, a)),
-        out_shape=jax.ShapeDtypeStruct((count, width), BF),
-        compiler_params=pltpu.CompilerParams(vmem_limit_bytes=40 << 20),
-        cost_estimate=pl.CostEstimate(flops=0, bytes_accessed=3 * count * width, transcendentals=0),
-    )(one, rows, pool, mask)
+        out_specs=[
+            pl.BlockSpec((count, QUAD), block),
+            wide,
+            pl.BlockSpec((channels, WIDTH), lambda a: (0, 0)),
+            pl.BlockSpec((channels, WIDTH), lambda a: (0, 0)),
+        ],
+        out_shape=[
+            jax.ShapeDtypeStruct((count, width), BF),
+            jax.ShapeDtypeStruct((channels, width), BF),
+            jax.ShapeDtypeStruct((channels, WIDTH), F32),
+            jax.ShapeDtypeStruct((channels, WIDTH), F32),
+        ],
+        compiler_params=pltpu.CompilerParams(vmem_limit_bytes=58 << 20),
+        cost_estimate=pl.CostEstimate(
+            flops=2 * count * channels * width, bytes_accessed=48 << 20, transcendentals=0
+        ),
+    )(one, rows, pool, mask8, weights_t, slope, pre)
+
+
+def taps_grad_kernel(starts, spread_ref, y_ref, project_ref, out_ref, total):
+    total[...] = dot(spread_ref[...], y_ref[...], (1,), (1,)).astype(BF)
+    low = 29 * 64
+    total[low : low + project_ref.shape[0], :] = project_ref[...]
+    for s, start in enumerate(starts):
+        out_ref[s] = total[start : start + out_ref.shape[1], :]
+
+
+def taps_grad(starts, frame_rows, spread, y, project, part, parts):
+    rows, pixels = spread.shape
+    width = y.shape[0] // parts
+    block = 256
+    first = part * width // block
+    return pl.pallas_call(
+        functools.partial(taps_grad_kernel, starts),
+        grid=(width // block,),
+        in_specs=[
+            whole((rows, pixels)),
+            pl.BlockSpec((block, pixels), lambda i: (first + i, 0)),
+            pl.BlockSpec((project.shape[0], block), lambda i: (0, first + i)),
+        ],
+        out_specs=pl.BlockSpec((len(starts), frame_rows, block), lambda i: (0, 0, i)),
+        out_shape=jax.ShapeDtypeStruct((len(starts), frame_rows, width), BF),
+        scratch_shapes=[pltpu.VMEM((rows, block), BF)],
+        compiler_params=pltpu.CompilerParams(vmem_limit_bytes=48 << 20),
+        cost_estimate=pl.CostEstimate(
+            flops=2 * rows * pixels * width, bytes_accessed=20 << 20, transcendentals=0
+        ),
+    )(spread, y, project)
 
 
 def side_rows(side):
-    zero = jnp.zeros_like(side[0, :1])
     result = []
+    at = lax.axis_index("dp") % CROP_DP
+    n = lax.axis_size("dp")
     from_one = crop_shift(jnp.concatenate([side[0, 1:4], side[2, 0:2]]), 1)
-    from_two = crop_shift(jnp.concatenate([side[2, 2:4], side[4, 0:3]]), 2)
-    from_three = crop_shift(side[4, 3:4], 3)
     to_one = crop_shift(jnp.concatenate([side[1, 0:3], side[3, 2:4]]), -1)
-    to_two = crop_shift(jnp.concatenate([side[3, 0:2], side[5, 1:4]]), -2)
-    to_three = crop_shift(side[5, 0:1], -3)
-    del zero
+    up = jnp.concatenate([side[2, 2:4], side[4, 0:3]])
+    down = jnp.concatenate([side[3, 0:2], side[5, 1:4]])
+    two = xor_move(jnp.where(at < 2, up, down), "dp", 2)
+    from_two = jnp.where(at < 2, jnp.zeros_like(two), two)
+    to_two = jnp.where(at < 2, two, jnp.zeros_like(two))
+    ends = [(i, i + 3 - 2 * (i % CROP_DP)) for i in range(n) if i % CROP_DP in (0, CROP_DP - 1)]
+    three = lax.ppermute(jnp.where(at == 0, side[4, 3:4], side[5, 0:1]), "dp", ends)
+    from_three = jnp.where(at == 0, jnp.zeros_like(three), three)
+    to_three = jnp.where(at == 0, three, jnp.zeros_like(three))
     result.append(jnp.concatenate([from_one[0:3], side[0, 0:1]]))
     result.append(jnp.concatenate([side[1, 3:4], to_one[0:3]]))
     result.append(jnp.concatenate([from_two[0:2], from_one[3:5]]))
@@ -362,6 +657,30 @@
 
 def quad_blocks(flat):
     return [flat[..., a * QUAD : (a + 1) * QUAD] for a in range(flat.shape[-1] // QUAD)]
+
+
+def owner_tables(n_dp, share_rows, wide, heads):
+    quarter = BOT // heads
+    places = []
+    for p in range(n_dp):
+        rows = []
+        for k in range(wide):
+            rows += [(share_rows * p + r) * wide + k for r in range(share_rows)]
+        for tap in range(9):
+            rows += [quarter * (wide + tap) + share_rows * p + r for r in range(share_rows)]
+        rows += [quarter * (wide + 9) + share_rows * wide * p + r for r in range(share_rows * wide)]
+        places.append(np.array(rows))
+    own = len(places[0])
+    lists = [[np.nonzero(place // own == s)[0] for s in range(n_dp)] for place in places]
+    count = -(-max(len(x) for row in lists for x in row) // 16) * 16
+    send = np.full((n_dp, n_dp, count), -1, np.int32)
+    take = np.zeros((n_dp, own), np.int32)
+    for p in range(n_dp):
+        for s in range(n_dp):
+            rows = lists[p][s]
+            send[p, s, : len(rows)] = rows
+            take[s, places[p][rows] - own * s] = p * count + np.arange(len(rows))
+    return send, take
 
 
 def shards(
@@ -400,6 +719,8 @@
     neck_low = trunk_neck.reshape(1, -1, BOT).astype(BF)
     neck_low = lax.all_gather(neck_low, "head", axis=0, tiled=True)
     neck_low = lax.all_gather(neck_low, "dp", axis=1, tiled=True)
+    x_left, x_right = [features, line_shift(features, 1)], [features, line_shift(features, -1)]
+    neck_low, x_left[1], x_right[1] = tie(neck_low, x_left[1], x_right[1])
     first_end = FEAT // heads
     second_end = first_end + 9 * BOT // heads
     reduce_w = neck_low[:, :first_end].reshape(BOT, FEAT)
@@ -407,10 +728,6 @@
     middle = jnp.moveaxis(middle, 0, 1).reshape(9, BOT, BOT)
     expand_w = neck_low[:, second_end:].reshape(FEAT, BOT)
 
-    x_left, x_right = [features], [features]
-    for _ in range(heads // 2):
-        x_left.append(line_shift(x_left[-1], 1))
-        x_right.append(line_shift(x_right[-1], -1))
 
     flat_total = trunk_aspp.shape[1] * n_dp // 16
     own_rows = trunk_aspp.shape[1]
@@ -420,15 +737,7 @@
         jnp.zeros((frame_rows * 16, 128), F32), trunk_aspp[0], inset, 0
     )
     framed = framed.reshape(frame_rows, FEAT).astype(BF)
-    aspp_rows = assemble(lax.all_gather(framed, "dp", axis=0), own_rows, flat_total)
-    tap_w = aspp_rows[: 29 * quarter]
-    project_q = aspp_rows[29 * quarter : flat_total].reshape(quarter, 5, heads, quarter)
-    project_q = jnp.moveaxis(project_q, 2, 0).reshape(heads, quarter, 5 * quarter)
-    received = [lax.dynamic_index_in_dim(project_q, z, 0, False)]
-    for m in range(1, heads):
-        received.append(xor_move(lax.dynamic_index_in_dim(project_q, z ^ m, 0, False), "head", m))
-    project_own = jnp.concatenate(in_order(received, z), axis=0)
-    tap_w, tap_wt, project_own = lax.optimization_barrier((tap_w, tap_w.T, project_own))
+    gathered = lax.all_gather(framed, "dp", axis=0)
 
     place = jnp.arange(pixels, dtype=jnp.int32)
     row_place = group % CROP_DP * (pixels // WIDTH) + place // WIDTH
@@ -481,36 +790,46 @@
     lidar_n = lidar[0]
     mean_one, inv_one = coefficients(total, square)
     low_one = (jax.nn.silu(scaled(normed(pre_one, mean_one, inv_one), gain_one, shift_one)) * mask_own).astype(BF)
-    blocks = in_order(exchange(low_one), z)
-    before = crop_shift(blocks[-1], 1)
-    after = crop_shift(blocks[0], -1)
-    h_one = jnp.concatenate(blocks, axis=1)
-    columns = neck_columns(jnp.concatenate([before, h_one, after], axis=1), False)
-    columns, x_left[-1], x_right[-1] = tie(columns, x_left[-1], x_right[-1])
-    for _ in range(heads // 2, heads - 1):
+    slots = exchange(low_one)
+    aspp_rows = assemble(held_until(gathered, low_one), own_rows, flat_total)
+    project_q = aspp_rows[29 * quarter : flat_total].reshape(quarter, 5, heads, quarter)
+    project_q = jnp.moveaxis(project_q, 2, 0).reshape(heads, quarter, 5 * quarter)
+    received = [lax.dynamic_index_in_dim(project_q, z, 0, False)]
+    for m in range(1, heads):
+        received.append(xor_move(lax.dynamic_index_in_dim(project_q, z ^ m, 0, False), "head", m))
+    project_own = jnp.concatenate(in_order(received, z), axis=0)
+    tap_wt = aspp_rows.T
+    slots, tap_wt, project_own = tie(slots, tap_wt, project_own)
+    x_left[1], x_right[1] = held_until((x_left[1], x_right[1]), slots)
+    for _ in range(1, heads - 1):
         x_left.append(line_shift(x_left[-1], 1))
         x_right.append(line_shift(x_right[-1], -1))
-    pre_two = lax.dot_general(middle, columns, (((0, 2), (0, 1)), ((), ())), preferred_element_type=F32)
-    mean_two, inv_two = coefficients(*unpack(sum_dp(pack(moments(pre_two, mask))), (BOT, BOT)))
+
+    def block_of(j):
+        block = slots[0]
+        for m in range(1, heads):
+            block = jnp.where((z ^ m) == j, slots[m], block)
+        return block
+
+    before = crop_shift(block_of(heads - 1), 1)
+    after = crop_shift(block_of(0), -1)
+    mask8 = jnp.broadcast_to(mask, (8, pixels))
+    pre_two, h_one, one_part, two_part = neck_conv(z, slots, before, after, middle, mask8)
+    sums = sum_dp(pack((jnp.sum(one_part, axis=1), jnp.sum(two_part, axis=1))))
+    mean_two, inv_two = coefficients(*unpack(sums, (BOT, BOT)))
     hat_two = normed(pre_two, mean_two, inv_two)
     in_two = scaled(hat_two, gain_two, shift_two)
     h_two = (jax.nn.silu(in_two) * mask).astype(BF)
     pre_three = jnp.dot(expand_w, h_two, preferred_element_type=F32)
     mean_three, inv_three = coefficients(*unpack(sum_dp(pack(moments(pre_three, mask))), (FEAT, FEAT)))
-    ring = [features]
-    for k in range(1, heads):
-        ring.append(jnp.where(z + k < heads, x_right[k], x_left[heads - k]))
-    ring = jnp.stack(ring)
-    x_group = jnp.concatenate(
-        [lax.dynamic_index_in_dim(ring, (a - z) % heads, 0, False) for a in range(heads)], axis=1
-    )
-    x_group = x_group * mask.astype(BF)
-    hat_three = normed(pre_three, mean_three, inv_three)
-    in_three = scaled(hat_three, gain_three, shift_three) + x_group.astype(F32)
-    y = (jax.nn.silu(in_three) * mask).astype(BF)
-
-    products = jnp.dot(tap_w, y, preferred_element_type=F32)
-    middle_rows, side, pool_part = aspp_gather(products)
+    pre_three = pre_three.astype(BF)
+    scale_three = gain_three * inv_three
+    coef = jnp.stack([scale_three, shift_three - scale_three * mean_three], axis=1)
+    sources = [features, *x_right[1:], *x_left[1:]]
+    y, slope_three, middle_rows, side, pool_part = aspp_forward(
+        z, pre_three, coef, mask8, aspp_rows, sources
+    )
+
     moved = side_rows(side)
     branches = [middle_rows[0]]
     for br in range(3):
@@ -535,6 +854,8 @@
 
     part_proj = jnp.dot(project_own, joined, preferred_element_type=F32)
     pre_proj = scatter_head(jnp.stack(quad_blocks(part_proj.astype(BF))), z)
+    x_group = feature_group(z, held_until(mask8, part_proj), sources)
+    pre_proj, x_group = tie(pre_proj, x_group)
     mean_proj, inv_proj = coefficients(*unpack(sum_all(pack(moments(pre_proj, mask_own))), (ASP, ASP)))
     hat_proj = normed(pre_proj, mean_proj, inv_proj)
     in_proj = scaled(hat_proj, gain_proj, shift_proj)
@@ -626,20 +947,25 @@
     rows = jnp.stack(
         [jnp.stack([moved[2 * br + 1], parts[br], moved[2 * br]]) for br in range(3)]
     )
-    spread = aspp_spread(
+    spread, act_three, sum_part, dot_part = aspp_backward(
         grad_aspp[:quarter],
         rows,
         jnp.broadcast_to(grad_pool[:, None], (quarter, WIDTH)),
-        jnp.broadcast_to(mask, (8, pixels)),
-    )
-    grad_y = dot(tap_wt, spread, (1,), (0,))
-    grad_taps = dot(spread, y, (1,), (1,)).astype(BF)
-
-    grad_act = grad_y * mask * silu_slope(in_three)
+        mask8,
+        tap_wt,
+        slope_three,
+        pre_three,
+    )
+
     spread_norms = jnp.stack([back_gain_aspp, back_shift_aspp]).reshape(2, 4, 1, quarter)
     own_place = (jnp.arange(heads) == z)[None, None, :, None] & (group == 0)
     spread_norms = jnp.where(own_place, spread_norms, 0.0)
-    sums = sum_all(pack((jnp.sum(grad_act, axis=-1), jnp.sum(grad_act * hat_three, axis=-1), spread_norms)))
+    sum_three = jnp.sum(sum_part, axis=1)
+    sums = xor_round(
+        pack((sum_three, (jnp.sum(dot_part, axis=1) - mean_three * sum_three) * inv_three, spread_norms)),
+        "dp",
+        (1,),
+    )
 
     swapped = [
         xor_move(lax.dynamic_index_in_dim(grad_project, z ^ m, 0, False), "head", m)
@@ -649,12 +975,16 @@
     ]
     own_project = jnp.stack(in_order(swapped, z)).reshape(heads, quarter, 5, quarter)
     own_project = jnp.moveaxis(own_project, 0, 2).reshape(-1, FEAT)
-    whole = jnp.concatenate(
-        [grad_taps, own_project, jnp.zeros((-flat_total % 16, FEAT), BF)], axis=0
-    )
-    framed = jnp.stack([whole[start : start + frame_rows] for start in frames])
-    sums, framed, dec_grad = tie(sums, framed, dec_grad)
-    aspp_steps = scatter_dp(framed, 0)
+    own_project = jnp.concatenate([own_project, jnp.zeros((-flat_total % 16, FEAT), BF)], axis=0)
+    sums, spread, own_project = tie(sums, spread, own_project)
+    first_half = taps_grad(frames, frame_rows, spread, y, own_project, 0, 2)
+    for bits in rounds_of(2, n_dp):
+        sums = xor_round(sums, "dp", bits)
+    sums, first_half, spread = tie(sums, first_half, spread)
+    second_half = taps_grad(frames, frame_rows, spread, y, own_project, 1, 2)
+    sums = sum_head(sums)
+    sums, first_half, second_half, dec_grad = tie(sums, first_half, second_half, dec_grad)
+    aspp_steps = scatter_dp((first_half, second_half), 0)
     aspp_now = next(aspp_steps)
     back_shift_three, back_gain_three, both = unpack(sums, (FEAT, FEAT, 8 * ASP))
     both = both.reshape(2, 4 * ASP)
@@ -667,51 +997,77 @@
             * (grad_act - (back_shift * scale)[:, None] - hat * (back_gain * scale)[:, None])
         ).astype(BF)
 
-    grad_three = norm_back(grad_act, hat_three, gain_three, inv_three, back_shift_three, back_gain_three)
-    grad_act = dot(expand_w, grad_three, (0,), (0,)) * mask * silu_slope(in_two)
-    sums = sum_all(pack((jnp.sum(grad_act, axis=-1), jnp.sum(grad_act * hat_two, axis=-1))))
+    hat_three = normed(pre_three.astype(F32), mean_three, inv_three)
+    grad_three = norm_back(
+        act_three.astype(F32), hat_three, gain_three, inv_three, back_shift_three, back_gain_three
+    )
+    grad_h_two = dot(expand_w, grad_three, (0,), (0,))
+    grad_act = grad_h_two * mask * silu_slope(in_two)
+    sums = pack((jnp.sum(grad_act, axis=-1), jnp.sum(grad_act * hat_two, axis=-1)))
+    sums = xor_round(sums, "dp", (1,))
+    sums, grad_three = tie(sums, grad_three)
     grad_expand = dot(grad_three, h_two, (1,), (1,)).astype(BF).reshape(heads, n_dp, -1, BOT)
+    for bits in rounds_of(2, n_dp):
+        sums = xor_round(sums, "dp", bits)
+    sums = sum_head(sums)
     sums, grad_expand, aspp_now = tie(sums, grad_expand, aspp_now)
-    aspp_now = aspp_steps.send(aspp_now)
-    expand_steps = scatter_dp(grad_expand, 1)
-    expand_now = next(expand_steps)
     back_shift_two, back_gain_two = unpack(sums, (BOT, BOT))
     grad_two = norm_back(grad_act, hat_two, gain_two, inv_two, back_shift_two, back_gain_two)
     before = crop_shift(grad_two[:, -QUAD:], 1)
     after = crop_shift(grad_two[:, :QUAD], -1)
+    before, after, aspp_now, grad_expand = tie(before, after, aspp_now, grad_expand)
+    aspp_now = aspp_steps.send(aspp_now)
+    expand_steps = scatter_dp(grad_expand, 1)
+    expand_now = next(expand_steps)
     columns = neck_columns(jnp.concatenate([before, grad_two, after], axis=1), True)
     grad_h_one = lax.dot_general(middle, columns, (((0, 1), (0, 1)), ((), ())), preferred_element_type=F32)
     group_one = jnp.dot(reduce_w, x_group, preferred_element_type=F32)
     hat_one = normed(group_one, mean_one, inv_one)
     grad_act = grad_h_one * mask * silu_slope(scaled(hat_one, gain_one, shift_one))
-    sums = sum_all(pack((jnp.sum(grad_act, axis=-1), jnp.sum(grad_act * hat_one, axis=-1))))
+    sums = pack((jnp.sum(grad_act, axis=-1), jnp.sum(grad_act * hat_one, axis=-1)))
+    sums, aspp_now, expand_now = tie(sums, aspp_now, expand_now)
+    sums = xor_round(sums, "dp", (1,))
+    sums, columns = tie(sums, columns)
     grad_middle = dot(columns, h_one, (2,), (1,)).astype(BF).reshape(9, heads, n_dp, -1, BOT)
+    for bits in rounds_of(2, n_dp):
+        sums = xor_round(sums, "dp", bits)
+    sums = sum_head(sums)
     sums, grad_middle, aspp_now, expand_now = tie(sums, grad_middle, aspp_now, expand_now)
+    middle_steps = scatter_dp(grad_middle, 2)
+    middle_now = next(middle_steps)
     aspp_block = last_step(aspp_steps, aspp_now)
     expand_block = last_step(expand_steps, expand_now)
-    middle_steps = scatter_dp(grad_middle, 2)
-    middle_block = last_step(middle_steps, next(middle_steps))
     back_shift_one, back_gain_one = unpack(sums, (BOT, BOT))
     grad_one = norm_back(grad_act, hat_one, gain_one, inv_one, back_shift_one, back_gain_one)
-    grad_reduce = dot(grad_one, x_group, (1,), (1,)).astype(BF).reshape(heads, n_dp, -1, FEAT)
-    reduce_steps = scatter_dp(grad_reduce, 1)
-    reduce_block = last_step(reduce_steps, next(reduce_steps))
+    grad_reduce = dot(grad_one, x_group, (1,), (1,)).astype(BF)
+    wide = FEAT // BOT
+    grad_reduce = jnp.stack([grad_reduce[:, k * BOT : (k + 1) * BOT] for k in range(wide)])
+    reduce_steps = scatter_dp(grad_reduce.reshape(wide, heads, n_dp, -1, BOT), 2)
+    reduce_now, middle_now, aspp_block, expand_block = tie(
+        next(reduce_steps), middle_now, aspp_block, expand_block
+    )
+    expand_own = scatter_head(expand_block.reshape(heads, -1, BOT), z)
+    both_now = jnp.concatenate([reduce_now[0], middle_now[0]], axis=0)
+    both_block = last_step(reduce_steps, reduce_steps.send((both_now,)))
 
     shard_aspp = lax.dynamic_slice_in_dim(
         aspp_block.astype(F32).reshape(frame_rows * 16, 128), inset, own_rows, 0
     )[None]
-    expand_own = scatter_head(expand_block.reshape(heads, -1, BOT), z)
-    middle_own = scatter_head(jnp.moveaxis(middle_block.reshape(9, heads, -1, BOT), 1, 0), z)
-    reduce_own = scatter_head(reduce_block.reshape(heads, -1, FEAT), z)
-    expand_all = lax.all_gather(expand_own, "dp", axis=0, tiled=True)
-    middle_all = lax.all_gather(middle_own, "dp", axis=1, tiled=True)
-    reduce_all = lax.all_gather(reduce_own, "dp", axis=0, tiled=True)
-    neck_rows = jnp.concatenate(
-        [reduce_all.reshape(-1, BOT), middle_all.reshape(-1, BOT), expand_all], axis=0
-    )
-    shard_neck = lax.dynamic_slice_in_dim(
-        neck_rows, group * (neck_rows.shape[0] // n_dp), neck_rows.shape[0] // n_dp, 0
-    ).reshape(trunk_neck.shape)
+    share_rows = BOT // heads // n_dp
+    both_block = both_block.reshape(wide + 9, heads, share_rows, BOT)
+    both_own = scatter_head(jnp.moveaxis(both_block, 1, 0), z)
+    pieces = jnp.concatenate([both_own, expand_own.reshape(wide, share_rows, BOT)], axis=0).astype(BF)
+    pieces = pieces.reshape(-1, BOT)
+    send_rows, take_rows = owner_tables(n_dp, share_rows, wide, heads)
+    count = send_rows.shape[2]
+    chosen = lax.dynamic_index_in_dim(jnp.asarray(send_rows), group, 0, False).reshape(-1)
+    pick = (chosen[:, None] == jnp.arange(pieces.shape[0], dtype=jnp.int32)[None, :]).astype(BF)
+    sent = jnp.dot(pick, pieces, preferred_element_type=F32).astype(BF).reshape(n_dp, count, BOT)
+    got = lax.all_to_all(sent, "dp", 0, 0, tiled=True).reshape(n_dp * count, BOT)
+    chosen = lax.dynamic_index_in_dim(jnp.asarray(take_rows), group, 0, False)
+    pick = (chosen[:, None] == jnp.arange(n_dp * count, dtype=jnp.int32)[None, :]).astype(BF)
+    shard_neck = jnp.dot(pick, got, preferred_element_type=F32)
+    shard_neck = shard_neck.reshape(trunk_neck.shape)
 
     grad_norms = jnp.stack(
         [
@@ -722,8 +1078,7 @@
     local_square = (
         jnp.sum(shard_aspp * shard_aspp)
         + jnp.sum(expand_own * expand_own)
-        + jnp.sum(middle_own * middle_own)
-        + jnp.sum(reduce_own * reduce_own)
+        + jnp.sum(both_own * both_own)
     )
     total_square = (
         sum_all(jnp.broadcast_to(local_square, (128,)))[0]

time: 976 us -> 841 us (0.86)
  matrix products: 198 us -> 91.5 us
  Pallas kernels: 31.7 us -> 137 us
  local copies, waits for them, and re-layouts: 120 us -> 77.7 us
  other arithmetic: 137 us -> 96.9 us
  starting transfers between devices: 199 us -> 171 us
  waiting for transfers between devices: 255 us -> 232 us
    pallas_call x2 -> x6, Pallas kernels: 9.43 us -> 122 us  [the longest x1 39.2 us: aspp_forward(): pl.pallas_call(aspp_forward_kernel, grid_spec=pltpu.PrefetchScalarGridSpe...]
    dot_general x15 -> x13, matrix products: 113 us -> 47.9 us  [dot(): lax.dot_general(a, b, ((ca, cb), ((), ())), preferred_element_type=F32)]
    ppermute x6, waiting for transfers between devices: 23.2 us -> 70.5 us  [line_shift(): lax.ppermute(x, 'head', [(i, i + by) for i in range(n) if 0 <= i + by < n])]
    all_gather x1, waiting for transfers between devices: 45.9 us -> 2.16 us  [shards(): neck_low = lax.all_gather(neck_low, 'dp', axis=1, tiled=True)]
    ppermute x107 -> x103, waiting for transfers between devices: 133 us -> 97.9 us  [xor_move(): return lax.ppermute(x, axis, [(i, i ^ mask) for i in range(n)])]
    dot_general x2, matrix products: 33.3 us -> 1.63 us  [the longest x1 1.27 us: shards(): jnp.dot(pick, pieces, preferred_element_type=F32).astype(BF)]
    ppermute x16 -> x8, starting transfers between devices: 39.7 us -> 14.9 us  [crop_shift(): return lax.ppermute(x, 'dp', pairs)]
    convert_element_type x2 -> x0, other arithmetic: 22.2 us -> none  [the longest x1 20.7 us: shards(): y = (jax.nn.silu(in_three) * mask).astype(BF)]
  transfers between devices with their start and end apart: 136 -> 124, of which waited for: 53 -> 51; matrix products, arithmetic and copies ran while one was open for 34% -> 23% of each run, Pallas kernels for 3% -> 12%
where the time goes in v3:
time: 841 us; the launch traced here: 830 us
  waiting for transfers between devices  232 us (28%)
  starting transfers between devices  171 us (20%)
  Pallas kernels  137 us (16%)
  other arithmetic  96.9 us (12%)
  matrix products  91.5 us (11%)
  local copies, waits for them, and re-layouts  77.7 us (9%)
  between operations  24.2 us (3%)
    ppermute x103, starting transfers between devices, xor_move(): return lax.ppermute(x, axis, [(i, i ^ mask) for i in range(n)])  127 us
    ppermute x103, waiting for transfers between devices, xor_move(): return lax.ppermute(x, axis, [(i, i ^ mask) for i in range(n)])  97.9 us
    ppermute x6, waiting for transfers between devices, line_shift(): lax.ppermute(x, 'head', [(i, i + by) for i in range(n) if 0 <= i + by < n])  70.5 us
    dot_general x13, matrix products, dot(): lax.dot_general(a, b, ((ca, cb), ((), ())), preferred_element_type=F32)  47.9 us
    pallas_call x1, Pallas kernels, aspp_forward(): pl.pallas_call(aspp_forward_kernel, grid_spec=pltpu.PrefetchScalarGridSpe...  39.2 us
    pallas_call x1, Pallas kernels, aspp_backward(): pl.pallas_call(aspp_backward_kernel, grid=(quads,), in_specs=[pl.BlockSpe...  33.7 us
    all_gather x1, waiting for transfers between devices, shards(): neck_low = lax.all_gather(neck_low, 'head', axis=0, tiled=True)  32.5 us
    pallas_call x2, Pallas kernels, taps_grad(): pl.pallas_call(functools.partial(taps_grad_kernel, starts), grid=(width /...  26.3 us
  transfers between devices with their start and end apart: 124, of which 51 were waited for; matrix products, arithmetic and copies ran while one was open for 23% of the time, Pallas kernels for 12%

profile of v3, /device:TPU:0, one launch (start us, length us, event | category | flops | bytes accessed | tf_op | source)
XLA Modules:
  0.0 830.3 jit_solution(1388717222298689255)
XLA Ops:
  9.4 32.5 %all-gather.4.cloned.1.call-done = bf16[4,272,512]{2,1,0:T(8,128)(2,1)} async-done(((bf16[1,272,512]{2,1,0:T(8,128)(2,1)}), bf16[4,272,512]{2,1,0:T(8,128)(2,1)}) %all-gather.4.cloned.1.call-update) | async-done | bytes 1114128 | tf_op jit(solution)/shard_map/all_gather | solution.py:720
  44.2 4.7 collective-permute-start
  54.1 38.1 %collective-permute-done.x4 = bf16[2048,512]{1,0:T(8,128)(2,1)} collective-permute-done((bf16[2048,512]{1,0:T(8,128)(2,1)S(1)}, bf16[2048,512]{1,0:T(8,128)(2,1)}, u32[]{:S(2)}, u32[]{:S(2)}) %collective-permute-start) | collective-permute-done | bytes 2097184 | tf_op jit(solution)/shard_map/ppermute | solution.py:105
  92.2 5.6 collective-permute-done.1.x1
  99.9 4.5 fusion.153
  104.4 4.3 reshape.656
  108.8 4.1 multiply_reduce_fusion.6
  127.4 3.2 collective-permute-done.8
  137.3 19.9 %all-gather.8.cloned.1.call-done.in_ref = bf16[8,256,2048]{2,1,0:T(8,128)(2,1)} async-done(((bf16[1,256,2048]{2,1,0:T(8,128)(2,1)}), bf16[8,256,2048]{2,1,0:T(8,128)(2,1)}) %all-gather.8.cloned.1.call-update) | async-done | bytes 8388624 | tf_op jit(solution)/shard_map/all_gather | solution.py:740
  157.2 6.3 shard_map.359.w_ref
  163.5 3.1 copy-done
  172.0 3.3 collective-permute-start.14
  175.3 10.4 %copy.83 = bf16[1920,2048]{0,1:T(8,128)(2,1)} copy(bf16[1920,2048]{1,0:T(8,128)(2,1)} %copy-done) | data formatting | bytes 15728640 | tf_op jit(solution)/shard_map/pallas_call | solution.py:256
  190.8 5.9 collective-permute-start.27
  201.8 15.1 %shard_map.360 = (f32[512,2048]{1,0:T(8,128)}, bf16[512,2048]{1,0:T(8,128)(2,1)S(1)}, f32[512,128]{1,0:T(8,128)S(1)}, f32[512,128]{1,0:T(8,128)S(1)}) custom-call(s32[1]{0:T(128)} %bitcast.20.z_ref, bf16[512,512]{1,0:T(8,128)(2,1)S(1)} %multiply_convert_fusion.7.s0, bf16[512,512]{1,0:T(8,128)(2,1)S(1)} %copy-done.12, ...), custom_call_target="tpu_custom_call" | custom-call | flops 9663676416 | bytes 16777216 | tf_op jit(solution)/shard_map/pallas_call | solution.py:323
  232.2 6.0 collective-permute-done.25.x2
  240.0 6.2 collective-permute-start.28
  246.3 10.6 %multiply_reduce_fusion = (f32[2048]{0:T(1024)S(1)}, f32[2048]{0:T(1024)S(1)}, bf16[2048,2048]{1,0:T(8,128)(2,1)}) fusion(f32[2048]{0:T(1024)S(1)} %fusion.111, bf16[2048,512]{1,0:T(8,128)(2,1)} %bitcast.485, f32[512,2048]{1,0:T(8,128)} %get-tuple-element.88, f32[512]{0:T(512)S(1)} %bitcast.523, f32[512]{0:T(512)S(1)} %get-tuple-element.188, ...), kind=kOutput, calls=%fused_computation.1 | convolution fusion | flops 4326420480 | bytes 14712832 | tf_op jit(solution)/shard_map/dot_general | solution.py:823
  269.7 18.2 %collective-permute-done.26.x3 = bf16[2048,512]{1,0:T(8,128)(2,1)} collective-permute-done((bf16[2048,512]{1,0:T(8,128)(2,1)S(1)}, bf16[2048,512]{1,0:T(8,128)(2,1)}, u32[]{:S(2)}, u32[]{:S(2)}) %collective-permute-start.26) | collective-permute-done | bytes 2097184 | tf_op jit(solution)/shard_map/ppermute | solution.py:105
  290.0 39.2 %shard_map.361 = (bf16[2048,2048]{1,0:T(8,128)(2,1)}, bf16[2048,2048]{1,0:T(8,128)(2,1)}, f32[4,64,2048]{2,1,0:T(8,128)}, bf16[6,4,64,512]{3,2,1,0:T(8,128)(2,1)}, f32[4,64,128]{2,1,0:T(8,128)}) custom-call(s32[1]{0:T(128)} %bitcast.20.z_ref, bf16[2048,2048]{1,0:T(8,128)(2,1)} %get-tuple-element.209.pre_ref, f32[2048,2]{1,0:T(8,128)} %copy.89.coef_ref, ...), custom_call_target="tpu_custom_call" | custom-call | flops 15569256448 | bytes 50331648 | tf_op jit(solution)/shard_map/pallas_call | solution.py:476
  336.6 3.8 collective-permute-start.29
  373.9 8.2 shard_map.362
  382.1 6.3 collective-permute-done.37
  402.6 3.6 collective-permute-start.43
  445.8 5.6 collective-permute-done.53
  451.4 10.9 %collective-permute-done.54 = bf16[256,512]{1,0:T(8,128)(2,1)S(1)} collective-permute-done((bf16[256,512]{1,0:T(8,128)(2,1)S(1)}, bf16[256,512]{1,0:T(8,128)(2,1)S(1)}, u32[]{:S(2)}, u32[]{:S(2)}) %collective-permute-start.54) | collective-permute-done | bytes 262176 | tf_op jit(solution)/shard_map/ppermute | solution.py:43
  470.5 4.6 collective-permute-start.64
  486.7 3.1 collective-permute-start.60
  492.1 2.8 collective-permute-start.62
  495.9 6.3 collective-permute-done.62
  505.3 33.7 %shard_map.363 = (bf16[1920,2048]{1,0:T(8,128)(2,1)}, bf16[2048,2048]{1,0:T(8,128)(2,1)}, f32[2048,128]{1,0:T(8,128)}, f32[2048,128]{1,0:T(8,128)}) custom-call(bf16[64,2048]{1,0:T(8,128)(2,1)} %slice.682.one_ref, bf16[3,3,4,64,512]{4,3,2,1,0:T(8,128)(2,1)} %pad_maximum_fusion.1.rows_ref, f32[64,128]{1,0:T(8,128)} %broadcast_in_dim.31.pool_in, ...), custom_call_target="tpu_custom_call" | custom-call | flops 16106127360 | bytes 50331648 | tf_op jit(solution)/shard_map/pallas_call | solution.py:556
  547.3 13.1 %shard_map.364 = bf16[8,256,1024]{2,1,0:T(8,128)(2,1)S(1)} custom-call(bf16[1920,2048]{1,0:T(8,128)(2,1)} %get-tuple-element.112.spread_ref, bf16[2048,2048]{1,0:T(8,128)(2,1)} %get-tuple-element.108.y_ref, bf16[48,2048]{1,0:T(8,128)(2,1)S(1)} %concatenate.173.project_ref), custom_call_target="tpu_custom_call" | custom-call | flops 8053063680 | bytes 20971520 | tf_op jit(solution)/shard_map/pallas_call | solution.py:600
  567.0 13.1 %shard_map.365 = bf16[8,256,1024]{2,1,0:T(8,128)(2,1)S(1)} custom-call(bf16[1920,2048]{1,0:T(8,128)(2,1)} %get-tuple-element.112.spread_ref, bf16[2048,2048]{1,0:T(8,128)(2,1)} %get-tuple-element.108.y_ref, bf16[48,2048]{1,0:T(8,128)(2,1)S(1)} %concatenate.173.project_ref), custom_call_target="tpu_custom_call" | custom-call | flops 8053063680 | bytes 20971520 | tf_op jit(solution)/shard_map/pallas_call | solution.py:600
  582.2 9.9 %multiply_convert_fusion = bf16[2048,2048]{1,0:T(8,128)(2,1)S(1)} fusion(bf16[2048,2048]{1,0:T(8,128)(2,1)} %get-tuple-element.209.pre_ref, bf16[2048,2048]{1,0:T(8,128)(2,1)} %get-tuple-element.102, f32[2048]{0:T(1024)S(1)} %get-tuple-element.336, f32[2048]{0:T(1024)S(1)} %copy-done.60, f32[2048]{0:T(1024)S(1)} %copy-done.61, ...), kind=kLoop, calls=%fused_computation.3 | loop fusion | flops 41943040 | bytes 25214976 | tf_op jit(solution)/shard_map/convert_element_type | solution.py:998
  592.1 8.5 %fusion.135 = (f32[512]{0:T(512)S(1)}, f32[512]{0:T(512)S(1)}, f32[512,2048]{1,0:T(8,128)}) fusion(f32[512]{0:T(512)S(1)} %copy-done.82, f32[512,2048]{1,0:T(8,128)S(1)} %copy-done.24, f32[512]{0:T(512)S(1)} %copy-done.84, f32[512]{0:T(512)S(1)} %bitcast.524, f32[512]{0:T(512)S(1)} %bitcast.516, f32[2048]{0:T(1024)S(1)} %fusion.111, ...), kind=kOutput, calls=%fused_computation.496 | convolution fusion | flops 4311743488 | bytes 18894848 | tf_op jit(solution)/shard_map/dot_general | solution.py:38
  613.6 6.9 convolution_convert_fusion.1
  628.3 6.3 fusion.166
  634.8 3.7 collective-permute-start.86
  640.2 7.9 shard_map.366
  648.1 18.8 %fusion.134 = (f32[512]{0:T(512)S(1)}, f32[512]{0:T(512)S(1)}, f32[512,2048]{1,0:T(8,128)}) fusion(f32[512]{0:T(512)S(1)} %copy-done.72, f32[512,2048]{1,0:T(8,128)} %fusion.166, f32[512]{0:T(512)S(1)} %copy-done.74, f32[512]{0:T(512)S(1)} %bitcast.512, f32[512]{0:T(512)S(1)} %bitcast.510, f32[2048]{0:T(1024)S(1)} %fusion.111, ...), kind=kOutput, calls=%fused_computation.495 | convolution fusion | flops 9680453632 | bytes 32002048 | tf_op jit(solution)/shard_map/dot_general | solution.py:1023
  684.9 15.6 %convolution_convert_fusion.2 = bf16[9,512,512]{2,1,0:T(8,128)(2,1)} fusion(bf16[9,512,2048]{2,1,0:T(8,128)(2,1)} %shard_map.366, bf16[512,2048]{1,0:T(8,128)(2,1)S(1)} %copy-done.17), kind=kOutput, calls=%fused_computation.28 | convolution fusion | flops 9666035712 | bytes 25690112 | tf_op jit(solution)/shard_map/dot_general | solution.py:38
  709.5 8.3 convolution_convert_fusion
  722.6 3.0 collective-permute-done.99
  725.7 4.9 collective-permute-done.101
  739.3 17.1 %collective-permute-done.107 = bf16[13,4,1,2,16,256]{5,4,3,1,0,2:T(8,128)(2,1)S(1)} collective-permute-done((bf16[13,4,1,2,16,256]{5,4,3,1,0,2:T(8,128)(2,1)S(1)}, bf16[13,4,1,2,16,256]{5,4,3,1,0,2:T(8,128)(2,1)S(1)}, u32[]{:S(2)}, u32[]{:S(2)}) %collective-permute-start.107) | collective-permute-done | bytes 852000 | tf_op jit(solution)/shard_map/ppermute | solution.py:43
  780.0 6.2 collective-permute-done.110
  803.3 3.5 all-to-all-start
  809.8 6.3 multiply_subtract_fusion
  (715 shorter events, 323.0 us)
Async XLA Ops:
  7.2 34.7 %all-gather.4.cloned.1.call-start = ((), (), s32[]{:S(2)}) async-start(), calls=%async_computation.1 | async-start | bytes 1392640 | tf_op jit(solution)/shard_map/all_gather | solution.py:720
  9.4 90.6 %all-gather.6.cloned.1.call-start = ((), (), s32[]{:S(2)}) async-start(), calls=%async_computation.2 | async-start | bytes 10027008 | tf_op jit(solution)/shard_map/all_gather | solution.py:721
  41.9 115.2 %all-gather.8.cloned.1.call-start = ((), (), s32[]{:S(2)}) async-start(), calls=%async_computation.3 | async-start | bytes 9437184 | tf_op jit(solution)/shard_map/all_gather | solution.py:740
  43.6 538.5 %all-reduce.3.cloned.1.call-start = ((), (), s32[]{:S(2)}) async-start(), calls=%async_computation.4 | async-start | bytes 1622016 | tf_op jit(solution)/shard_map/psum | solution.py:899
  44.2 47.9 %collective-permute-start = (bf16[2048,512]{1,0:T(8,128)(2,1)S(1)}, bf16[2048,512]{1,0:T(8,128)(2,1)}, u32[]{:S(2)}, u32[]{:S(2)}) collective-permute-start(bf16[2048,512]{1,0:T(8,128)(2,1)S(1)} %copy-done.5), channel_id=1, source_target_pairs={{0,1},{1,2},{2,3},{4,5},{5,6},{6,7},{8,9},{9,10},{10,11},{12,13},{... | collective-permute-start | bytes 6291464 | tf_op jit(solution)/shard_map/ppermute | solution.py:105
  48.9 48.9 %collective-permute-start.1 = (bf16[2048,512]{1,0:T(8,128)(2,1)S(1)}, bf16[2048,512]{1,0:T(8,128)(2,1)}, u32[]{:S(2)}, u32[]{:S(2)}) collective-permute-start(bf16[2048,512]{1,0:T(8,128)(2,1)S(1)} %copy-done.5), channel_id=1, source_target_pairs={{1,0},{2,1},{3,2},{5,4},{6,5},{7,6},{9,8},{10,9},{11,10},{13,12},{... | collective-permute-start | bytes 6291464 | tf_op jit(solution)/shard_map/ppermute | solution.py:105
  133.8 52.9 %collective-permute-start.10 = (bf16[512,512]{1,0:T(8,128)(2,1)S(1)}, bf16[512,512]{1,0:T(8,128)(2,1)S(1)}, u32[]{:S(2)}, u32[]{:S(2)}) collective-permute-start(bf16[512,512]{1,0:T(8,128)(2,1)S(1)} %multiply_convert_fusion.7.s0), channel_id=1, source_target_pairs={{0,2},{1,3},{2,0},{3,1},{4,6},{5,7},{6,4},{7,5},{8,10},{9,11},{10,... | collective-permute-start | bytes 1572872 | tf_op jit(solution)/shard_map/ppermute | solution.py:43
  133.9 52.8 %collective-permute-start.11 = (bf16[512,512]{1,0:T(8,128)(2,1)S(1)}, bf16[512,512]{1,0:T(8,128)(2,1)S(1)}, u32[]{:S(2)}, u32[]{:S(2)}) collective-permute-start(bf16[512,512]{1,0:T(8,128)(2,1)S(1)} %multiply_convert_fusion.7.s0), channel_id=1, source_target_pairs={{0,3},{1,2},{2,1},{3,0},{4,7},{5,6},{6,5},{7,4},{8,11},{9,10},{10,... | collective-permute-start | bytes 1572872 | tf_op jit(solution)/shard_map/ppermute | solution.py:43
  134.9 51.7 %collective-permute-start.9 = (bf16[512,512]{1,0:T(8,128)(2,1)S(1)}, bf16[512,512]{1,0:T(8,128)(2,1)S(1)}, u32[]{:S(2)}, u32[]{:S(2)}) collective-permute-start(bf16[512,512]{1,0:T(8,128)(2,1)S(1)} %multiply_convert_fusion.7.s0), channel_id=1, source_target_pairs={{0,1},{1,0},{2,3},{3,2},{4,5},{5,4},{6,7},{7,6},{8,9},{9,8},{10,11... | collective-permute-start | bytes 1572872 | tf_op jit(solution)/shard_map/ppermute | solution.py:43
  168.9 16.8 %collective-permute-start.13 = (bf16[64,320]{0,1:T(8,128)(2,1)S(1)}, bf16[64,320]{0,1:T(8,128)(2,1)S(1)}, u32[]{:S(2)}, u32[]{:S(2)}) collective-permute-start(bf16[64,320]{0,1:T(8,128)(2,1)S(1)} %get-tuple-element.299), channel_id=1, source_target_pairs={{0,2},{1,3},{2,0},{3,1},{4,6},{5,7},{6,4},{7,5},{8,10},{9,11},{10,... | collective-permute-start | bytes 122888 | tf_op jit(solution)/shard_map/ppermute | solution.py:43
  189.5 48.7 %collective-permute-start.25 = (bf16[2048,512]{1,0:T(8,128)(2,1)}, bf16[2048,512]{1,0:T(8,128)(2,1)S(1)}, u32[]{:S(2)}, u32[]{:S(2)}) collective-permute-start(bf16[2048,512]{1,0:T(8,128)(2,1)} %collective-permute-done.1.x1), channel_id=1, source_target_pairs={{1,0},{2,1},{3,2},{5,4},{6,5},{7,6},{9,8},{10,9},{11,10},{13,12},{... | collective-permute-start | bytes 6291464 | tf_op jit(solution)/shard_map/ppermute | solution.py:105
  190.8 49.3 %collective-permute-start.27 = (bf16[2048,512]{1,0:T(8,128)(2,1)}, bf16[2048,512]{1,0:T(8,128)(2,1)}, u32[]{:S(2)}, u32[]{:S(2)}) collective-permute-start(bf16[2048,512]{1,0:T(8,128)(2,1)} %collective-permute-done.x4), channel_id=1, source_target_pairs={{0,1},{1,2},{2,3},{4,5},{5,6},{6,7},{8,9},{9,10},{10,11},{12,13},{... | collective-permute-start | bytes 6291464 | tf_op jit(solution)/shard_map/ppermute | solution.py:105
  238.2 49.8 %collective-permute-start.26 = (bf16[2048,512]{1,0:T(8,128)(2,1)S(1)}, bf16[2048,512]{1,0:T(8,128)(2,1)}, u32[]{:S(2)}, u32[]{:S(2)}) collective-permute-start(bf16[2048,512]{1,0:T(8,128)(2,1)S(1)} %collective-permute-done.25.x2), channel_id=1, source_target_pairs={{1,0},{2,1},{3,2},{5,4},{6,5},{7,6},{9,8},{10,9},{11,10},{13,12},{... | collective-permute-start | bytes 6291464 | tf_op jit(solution)/shard_map/ppermute | solution.py:105
  240.0 50.0 %collective-permute-start.28 = (bf16[2048,512]{1,0:T(8,128)(2,1)}, bf16[2048,512]{1,0:T(8,128)(2,1)}, u32[]{:S(2)}, u32[]{:S(2)}) collective-permute-start(bf16[2048,512]{1,0:T(8,128)(2,1)} %collective-permute-done.27.x5), channel_id=1, source_target_pairs={{0,1},{1,2},{2,3},{4,5},{5,6},{6,7},{8,9},{9,10},{10,11},{12,13},{... | collective-permute-start | bytes 6291464 | tf_op jit(solution)/shard_map/ppermute | solution.py:105
  365.1 17.0 %collective-permute-start.36 = (bf16[256,512]{1,0:T(8,128)(2,1)}, bf16[256,512]{1,0:T(8,128)(2,1)}, u32[]{:S(2)}, u32[]{:S(2)}) collective-permute-start(bf16[256,512]{1,0:T(8,128)(2,1)} %get-tuple-element.255), channel_id=1, source_target_pairs={{0,1},{1,0},{2,3},{3,2},{4,5},{5,4},{6,7},{7,6},{8,9},{9,8},{10,11... | collective-permute-start | bytes 786440 | tf_op jit(solution)/shard_map/ppermute | solution.py:43
  367.3 21.2 %collective-permute-start.37 = (bf16[256,512]{1,0:T(8,128)(2,1)}, bf16[256,512]{1,0:T(8,128)(2,1)}, u32[]{:S(2)}, u32[]{:S(2)}) collective-permute-start(bf16[256,512]{1,0:T(8,128)(2,1)} %get-tuple-element.257), channel_id=1, source_target_pairs={{0,2},{1,3},{2,0},{3,1},{4,6},{5,7},{6,4},{7,5},{8,10},{9,11},{10,... | collective-permute-start | bytes 786440 | tf_op jit(solution)/shard_map/ppermute | solution.py:43
  368.9 19.6 %collective-permute-start.38 = (bf16[256,512]{1,0:T(8,128)(2,1)}, bf16[256,512]{1,0:T(8,128)(2,1)}, u32[]{:S(2)}, u32[]{:S(2)}) collective-permute-start(bf16[256,512]{1,0:T(8,128)(2,1)} %get-tuple-element.256), channel_id=1, source_target_pairs={{0,3},{1,2},{2,1},{3,0},{4,7},{5,6},{6,5},{7,4},{8,11},{9,10},{10,... | collective-permute-start | bytes 786440 | tf_op jit(solution)/shard_map/ppermute | solution.py:43
  440.3 22.0 %collective-permute-start.54 = (bf16[256,512]{1,0:T(8,128)(2,1)S(1)}, bf16[256,512]{1,0:T(8,128)(2,1)S(1)}, u32[]{:S(2)}, u32[]{:S(2)}) collective-permute-start(bf16[256,512]{1,0:T(8,128)(2,1)S(1)} %multiply_convert_fusion.8), channel_id=1, source_target_pairs={{0,2},{1,3},{2,0},{3,1},{4,6},{5,7},{6,4},{7,5},{8,10},{9,11},{10,... | collective-permute-start | bytes 786440 | tf_op jit(solution)/shard_map/ppermute | solution.py:43
  442.6 19.7 %collective-permute-start.55 = (bf16[256,512]{1,0:T(8,128)(2,1)S(1)}, bf16[256,512]{1,0:T(8,128)(2,1)S(1)}, u32[]{:S(2)}, u32[]{:S(2)}) collective-permute-start(bf16[256,512]{1,0:T(8,128)(2,1)S(1)} %multiply_convert_fusion.8), channel_id=1, source_target_pairs={{0,3},{1,2},{2,1},{3,0},{4,7},{5,6},{6,5},{7,4},{8,11},{9,10},{10,... | collective-permute-start | bytes 786440 | tf_op jit(solution)/shard_map/ppermute | solution.py:43
  470.5 20.2 %collective-permute-start.64 = (bf16[64,320]{1,0:T(8,128)(2,1)}, bf16[64,320]{1,0:T(8,128)(2,1)}, u32[]{:S(2)}, u32[]{:S(2)}) collective-permute-start(bf16[64,320]{1,0:T(8,128)(2,1)} %get-tuple-element.319), channel_id=1, source_target_pairs={{0,1},{1,0},{2,3},{3,2},{4,5},{5,4},{6,7},{7,6},{8,9},{9,8},{10,11... | collective-permute-start | bytes 122888 | tf_op jit(solution)/shard_map/ppermute | solution.py:43
  475.1 16.9 %collective-permute-start.65 = (bf16[64,320]{1,0:T(8,128)(2,1)}, bf16[64,320]{1,0:T(8,128)(2,1)}, u32[]{:S(2)}, u32[]{:S(2)}) collective-permute-start(bf16[64,320]{1,0:T(8,128)(2,1)} %get-tuple-element.318), channel_id=1, source_target_pairs={{0,2},{1,3},{2,0},{3,1},{4,6},{5,7},{6,4},{7,5},{8,10},{9,11},{10,... | collective-permute-start | bytes 122888 | tf_op jit(solution)/shard_map/ppermute | solution.py:43
  475.1 19.8 %collective-permute-start.66 = (bf16[64,320]{1,0:T(8,128)(2,1)}, bf16[64,320]{1,0:T(8,128)(2,1)}, u32[]{:S(2)}, u32[]{:S(2)}) collective-permute-start(bf16[64,320]{1,0:T(8,128)(2,1)} %get-tuple-element.317), channel_id=1, source_target_pairs={{0,3},{1,2},{2,1},{3,0},{4,7},{5,6},{6,5},{7,4},{8,11},{9,10},{10,... | collective-permute-start | bytes 122888 | tf_op jit(solution)/shard_map/ppermute | solution.py:43
  485.4 17.0 %collective-permute-start.59 = (bf16[5,64,512]{2,1,0:T(8,128)(2,1)S(1)}, bf16[5,64,512]{2,1,0:T(8,128)(2,1)S(1)}, u32[]{:S(2)}, u32[]{:S(2)}) collective-permute-start(bf16[5,64,512]{2,1,0:T(8,128)(2,1)S(1)} %get-tuple-element.320), channel_id=1, source_target_pairs={{4,0},{8,4},{12,8},{20,16},{24,20},{28,24},{5,1},{9,5},{13,9},{21,... | collective-permute-start | bytes 983048 | tf_op jit(solution)/shard_map/ppermute | solution.py:100
  486.7 15.8 %collective-permute-start.60 = (bf16[5,64,512]{2,1,0:T(8,128)(2,1)S(1)}, bf16[5,64,512]{2,1,0:T(8,128)(2,1)S(1)}, u32[]{:S(2)}, u32[]{:S(2)}) collective-permute-start(bf16[5,64,512]{2,1,0:T(8,128)(2,1)S(1)} %get-tuple-element.322), channel_id=1, source_target_pairs={{0,4},{4,8},{8,12},{16,20},{20,24},{24,28},{1,5},{5,9},{9,13},{17,... | collective-permute-start | bytes 983048 | tf_op jit(solution)/shard_map/ppermute | solution.py:100
  543.5 19.0 %collective-permute-start.67 = (f32[6144]{0:T(1024)S(1)}, f32[6144]{0:T(1024)S(1)}, u32[]{:S(2)}, u32[]{:S(2)}) collective-permute-start(f32[6144]{0:T(1024)S(1)} %fusion.131), channel_id=1, source_target_pairs={{0,8},{4,12},{8,0},{12,4},{16,24},{20,28},{24,16},{28,20},{1,9},{5... | collective-permute-start | bytes 73736 | tf_op jit(solution)/shard_map/ppermute | solution.py:43
  545.8 16.7 %collective-permute-start.68 = (f32[6144]{0:T(1024)S(1)}, f32[6144]{0:T(1024)S(1)}, u32[]{:S(2)}, u32[]{:S(2)}) collective-permute-start(f32[6144]{0:T(1024)S(1)} %fusion.131), channel_id=1, source_target_pairs={{0,16},{4,20},{8,24},{12,28},{16,0},{20,4},{24,8},{28,12},{1,17},{... | collective-permute-start | bytes 73736 | tf_op jit(solution)/shard_map/ppermute | solution.py:43
  546.6 15.9 %collective-permute-start.69 = (f32[6144]{0:T(1024)S(1)}, f32[6144]{0:T(1024)S(1)}, u32[]{:S(2)}, u32[]{:S(2)}) collective-permute-start(f32[6144]{0:T(1024)S(1)} %fusion.131), channel_id=1, source_target_pairs={{0,24},{4,28},{8,16},{12,20},{16,8},{20,12},{24,0},{28,4},{1,25},{... | collective-permute-start | bytes 73736 | tf_op jit(solution)/shard_map/ppermute | solution.py:43
  562.5 19.5 %collective-permute-start.70 = (f32[6144]{0:T(1024)S(1)}, f32[6144]{0:T(1024)S(1)}, u32[]{:S(2)}, u32[]{:S(2)}) collective-permute-start(f32[6144]{0:T(1024)S(1)} %add_add_fusion.1), channel_id=1, source_target_pairs={{0,1},{1,0},{2,3},{3,2},{4,5},{5,4},{6,7},{7,6},{8,9},{9,8},{10,11... | collective-permute-start | bytes 73736 | tf_op jit(solution)/shard_map/ppermute | solution.py:43
  563.7 18.3 %collective-permute-start.71 = (f32[6144]{0:T(1024)S(1)}, f32[6144]{0:T(1024)S(1)}, u32[]{:S(2)}, u32[]{:S(2)}) collective-permute-start(f32[6144]{0:T(1024)S(1)} %add_add_fusion.1), channel_id=1, source_target_pairs={{0,2},{1,3},{2,0},{3,1},{4,6},{5,7},{6,4},{7,5},{8,10},{9,11},{10,... | collective-permute-start | bytes 73736 | tf_op jit(solution)/shard_map/ppermute | solution.py:43
  565.0 17.1 %collective-permute-start.72 = (f32[6144]{0:T(1024)S(1)}, f32[6144]{0:T(1024)S(1)}, u32[]{:S(2)}, u32[]{:S(2)}) collective-permute-start(f32[6144]{0:T(1024)S(1)} %add_add_fusion.1), channel_id=1, source_target_pairs={{0,3},{1,2},{2,1},{3,0},{4,7},{5,6},{6,5},{7,4},{8,11},{9,10},{10,... | collective-permute-start | bytes 73736 | tf_op jit(solution)/shard_map/ppermute | solution.py:43
  600.9 19.6 %collective-permute-start.81 = (bf16[4,1,256,1024]{3,2,0,1:T(8,128)(2,1)S(1)}, bf16[4,1,256,1024]{3,2,0,1:T(8,128)(2,1)S(1)}, u32[]{:S(2)}, u32[]{:S(2)}) collective-permute-start(bf16[4,1,256,1024]{3,2,0,1:T(8,128)(2,1)S(1)} %dynamic-slice_bitcast_fusion.1), channel_id=1, source_target_pairs={{0,4},{4,0},{8,12},{12,8},{16,20},{20,16},{24,28},{28,24},{1,5},{5... | collective-permute-start | bytes 6291464 | tf_op jit(solution)/shard_map/ppermute | solution.py:43
  605.5 16.0 %collective-permute-start.80 = (bf16[4,1,256,1024]{3,2,0,1:T(8,128)(2,1)S(1)}, bf16[4,1,256,1024]{3,2,0,1:T(8,128)(2,1)S(1)}, u32[]{:S(2)}, u32[]{:S(2)}) collective-permute-start(bf16[4,1,256,1024]{3,2,0,1:T(8,128)(2,1)S(1)} %dynamic-slice_bitcast_fusion.2), channel_id=1, source_target_pairs={{0,4},{4,0},{8,12},{12,8},{16,20},{20,16},{24,28},{28,24},{1,5},{5... | collective-permute-start | bytes 6291464 | tf_op jit(solution)/shard_map/ppermute | solution.py:43
  634.8 32.2 %collective-permute-start.86 = (bf16[4,4,1,64,512]{4,3,1,0,2:T(8,128)(2,1)S(1)}, bf16[4,4,1,64,512]{4,3,1,0,2:T(8,128)(2,1)}, u32[]{:S(2)}, u32[]{:S(2)}) collective-permute-start(bf16[4,4,1,64,512]{4,3,1,0,2:T(8,128)(2,1)S(1)} %dynamic-slice_bitcast_fusion.4), channel_id=1, source_target_pairs={{0,4},{4,0},{8,12},{12,8},{16,20},{20,16},{24,28},{28,24},{1,5},{5... | collective-permute-start | bytes 3145736 | tf_op jit(solution)/shard_map/ppermute | solution.py:43
  638.5 30.1 %collective-permute-start.85 = (bf16[1,2,256,1024]{3,2,1,0:T(8,128)(2,1)S(1)}, bf16[1,2,256,1024]{3,2,1,0:T(8,128)(2,1)}, u32[]{:S(2)}, u32[]{:S(2)}) collective-permute-start(bf16[1,2,256,1024]{3,2,1,0:T(8,128)(2,1)S(1)} %dynamic-slice_bitcast_fusion.5), channel_id=1, source_target_pairs={{0,16},{4,20},{8,24},{12,28},{16,0},{20,4},{24,8},{28,12},{1,17},{... | collective-permute-start | bytes 3145736 | tf_op jit(solution)/shard_map/ppermute | solution.py:43
  639.8 30.4 %collective-permute-start.84 = (bf16[2,1,256,1024]{3,2,0,1:T(8,128)(2,1)S(1)}, bf16[2,1,256,1024]{3,2,0,1:T(8,128)(2,1)S(1)}, u32[]{:S(2)}, u32[]{:S(2)}) collective-permute-start(bf16[2,1,256,1024]{3,2,0,1:T(8,128)(2,1)S(1)} %dynamic-slice_bitcast_fusion.6), channel_id=1, source_target_pairs={{0,8},{4,12},{8,0},{12,4},{16,24},{20,28},{24,16},{28,20},{1,9},{5... | collective-permute-start | bytes 3145736 | tf_op jit(solution)/shard_map/ppermute | solution.py:43
  680.5 20.0 %collective-permute-start.91 = (f32[1024]{0:T(1024)S(1)}, f32[1024]{0:T(1024)S(1)}, u32[]{:S(2)}, u32[]{:S(2)}) collective-permute-start(f32[1024]{0:T(1024)S(1)} %add_add_fusion.6), channel_id=1, source_target_pairs={{0,1},{1,0},{2,3},{3,2},{4,5},{5,4},{6,7},{7,6},{8,9},{9,8},{10,11... | collective-permute-start | bytes 12296 | tf_op jit(solution)/shard_map/ppermute | solution.py:43
  680.5 20.0 %collective-permute-start.92 = (f32[1024]{0:T(1024)S(1)}, f32[1024]{0:T(1024)S(1)}, u32[]{:S(2)}, u32[]{:S(2)}) collective-permute-start(f32[1024]{0:T(1024)S(1)} %add_add_fusion.6), channel_id=1, source_target_pairs={{0,2},{1,3},{2,0},{3,1},{4,6},{5,7},{6,4},{7,5},{8,10},{9,11},{10,... | collective-permute-start | bytes 12296 | tf_op jit(solution)/shard_map/ppermute | solution.py:43
  682.6 17.9 %collective-permute-start.93 = (f32[1024]{0:T(1024)S(1)}, f32[1024]{0:T(1024)S(1)}, u32[]{:S(2)}, u32[]{:S(2)}) collective-permute-start(f32[1024]{0:T(1024)S(1)} %add_add_fusion.6), channel_id=1, source_target_pairs={{0,3},{1,2},{2,1},{3,0},{4,7},{5,6},{6,5},{7,4},{8,11},{9,10},{10,... | collective-permute-start | bytes 12296 | tf_op jit(solution)/shard_map/ppermute | solution.py:43
  701.4 17.0 %collective-permute-start.98 = (bf16[4,2,1,64,256]{4,3,0,2,1:T(8,128)(2,1)}, bf16[4,2,1,64,256]{4,3,0,2,1:T(8,128)(2,1)}, u32[]{:S(2)}, u32[]{:S(2)}) collective-permute-start(bf16[4,2,1,64,256]{4,3,0,2,1:T(8,128)(2,1)} %bitcast.456), channel_id=1, source_target_pairs={{0,8},{4,12},{8,0},{12,4},{16,24},{20,28},{24,16},{28,20},{1,9},{5... | collective-permute-start | bytes 786440 | tf_op jit(solution)/shard_map/ppermute | solution.py:43
  702.2 18.1 %collective-permute-start.100 = (bf16[4,1,2,64,256]{4,3,2,0,1:T(8,128)(2,1)}, bf16[4,1,2,64,256]{4,3,2,0,1:T(8,128)(2,1)}, u32[]{:S(2)}, u32[]{:S(2)}) collective-permute-start(bf16[4,1,2,64,256]{4,3,2,0,1:T(8,128)(2,1)} %dynamic-slice_bitcast_fusion.10), channel_id=1, source_target_pairs={{0,16},{4,20},{8,24},{12,28},{16,0},{20,4},{24,8},{28,12},{1,17},{... | collective-permute-start | bytes 786440 | tf_op jit(solution)/shard_map/ppermute | solution.py:43
  704.2 26.5 %collective-permute-start.96 = (bf16[1,1,256,1024]{3,2,1,0:T(8,128)(2,1)}, bf16[1,1,256,1024]{3,2,1,0:T(8,128)(2,1)}, u32[]{:S(2)}, u32[]{:S(2)}) collective-permute-start(bf16[1,1,256,1024]{3,2,1,0:T(8,128)(2,1)} %dynamic-slice_bitcast_fusion.9), channel_id=1, source_target_pairs={{0,16},{4,20},{8,24},{12,28},{16,0},{20,4},{24,8},{28,12},{1,17},{... | collective-permute-start | bytes 1572872 | tf_op jit(solution)/shard_map/ppermute | solution.py:43
  705.9 26.1 %collective-permute-start.97 = (bf16[1,1,256,1024]{3,2,1,0:T(8,128)(2,1)}, bf16[1,1,256,1024]{3,2,1,0:T(8,128)(2,1)}, u32[]{:S(2)}, u32[]{:S(2)}) collective-permute-start(bf16[1,1,256,1024]{3,2,1,0:T(8,128)(2,1)} %dynamic-slice_bitcast_fusion.8), channel_id=1, source_target_pairs={{0,8},{4,12},{8,0},{12,4},{16,24},{20,28},{24,16},{28,20},{1,9},{5... | collective-permute-start | bytes 1572872 | tf_op jit(solution)/shard_map/ppermute | solution.py:43
  709.5 24.3 %collective-permute-start.95 = (bf16[9,4,4,1,16,512]{5,4,2,1,0,3:T(8,128)(2,1)}, bf16[9,4,4,1,16,512]{5,4,2,1,0,3:T(8,128)(2,1)}, u32[]{:S(2)}, u32[]{:S(2)}) collective-permute-start(bf16[9,4,4,1,16,512]{5,4,2,1,0,3:T(8,128)(2,1)} %dynamic-slice_bitcast_fusion), channel_id=1, source_target_pairs={{0,4},{4,0},{8,12},{12,8},{16,20},{20,16},{24,28},{28,24},{1,5},{5... | collective-permute-start | bytes 7077896 | tf_op jit(solution)/shard_map/ppermute | solution.py:43
  718.4 15.0 %collective-permute-start.94 = (bf16[4,4,4,1,16,512]{5,4,2,1,0,3:T(8,128)(2,1)S(1)}, bf16[4,4,4,1,16,512]{5,4,2,1,0,3:T(8,128)(2,1)S(1)}, u32[]{:S(2)}, u32[]{:S(2)}) collective-permute-start(bf16[4,4,4,1,16,512]{5,4,2,1,0,3:T(8,128)(2,1)S(1)} %dynamic-slice_bitcast_fusion.3), channel_id=1, source_target_pairs={{0,4},{4,0},{8,12},{12,8},{16,20},{20,16},{24,28},{28,24},{1,5},{5... | collective-permute-start | bytes 3145736 | tf_op jit(solution)/shard_map/ppermute | solution.py:43
  737.6 18.8 %collective-permute-start.107 = (bf16[13,4,1,2,16,256]{5,4,3,1,0,2:T(8,128)(2,1)S(1)}, bf16[13,4,1,2,16,256]{5,4,3,1,0,2:T(8,128)(2,1)S(1)}, u32[]{:S(2)}, u32[]{:S(2)}) collective-permute-start(bf16[13,4,1,2,16,256]{5,4,3,1,0,2:T(8,128)(2,1)S(1)} %dynamic-slice_bitcast_fusion.7), channel_id=1, source_target_pairs={{0,16},{4,20},{8,24},{12,28},{16,0},{20,4},{24,8},{28,12},{1,17},{... | collective-permute-start | bytes 2555912 | tf_op jit(solution)/shard_map/ppermute | solution.py:43
  739.1 18.8 %collective-permute-start.105 = (bf16[13,4,2,1,16,256]{5,4,1,0,3,2:T(8,128)(2,1)S(1)}, bf16[13,4,2,1,16,256]{5,4,1,0,3,2:T(8,128)(2,1)S(1)}, u32[]{:S(2)}, u32[]{:S(2)}) collective-permute-start(bf16[13,4,2,1,16,256]{5,4,1,0,3,2:T(8,128)(2,1)S(1)} %bitcast.494), channel_id=1, source_target_pairs={{0,8},{4,12},{8,0},{12,4},{16,24},{20,28},{24,16},{28,20},{1,9},{5... | collective-permute-start | bytes 2555912 | tf_op jit(solution)/shard_map/ppermute | solution.py:43
  770.3 15.8 %collective-permute-start.110 = (bf16[13,16,512]{2,1,0:T(8,128)(2,1)}, bf16[13,16,512]{2,1,0:T(8,128)(2,1)}, u32[]{:S(2)}, u32[]{:S(2)}) collective-permute-start(bf16[13,16,512]{2,1,0:T(8,128)(2,1)} %get-tuple-element.263), channel_id=1, source_target_pairs={{0,2},{1,3},{2,0},{3,1},{4,6},{5,7},{6,4},{7,5},{8,10},{9,11},{10,... | collective-permute-start | bytes 638984 | tf_op jit(solution)/shard_map/ppermute | solution.py:43
  803.3 15.2 %all-to-all-start = ((bf16[8,64,512]{2,1,0:T(8,128)(2,1)}), bf16[8,64,512]{2,1,0:T(8,128)(2,1)S(1)}, u32[]{:S(2)}, u32[]{:S(2)}) async-start(bf16[8,64,512]{2,1,0:T(8,128)(2,1)} %bitcast.216), calls=%async_computation | async-start | bytes 1048576 | tf_op jit(solution)/shard_map/all_to_all | solution.py:1066
  (181 other events, 1786.7 us)
Sparse Core Ops, SparseCore 0:
  10.2 31.6 all-gather.3
  43.8 56.0 all-gather.5
  102.4 54.7 all-gather.7
  445.9 130.7 all-reduce.2

commit v4 on v3

--- a/solution.py
+++ b/solution.py
@@ -544,7 +544,7 @@
         dot_ref[at, :] += lane_parts(act * pre_ref[at, :].astype(F32))
         return carry
 
-    lax.fori_loop(0, act_ref.shape[0] // CHUNK, multiply, 0)
+    lax.fori_loop(0, act_ref.shape[0] // CHUNK, multiply, 0, unroll=4)
 
 
 def aspp_backward(one, rows, pool, mask8, weights_t, slope, pre):
@@ -659,6 +659,31 @@
     return [flat[..., a * QUAD : (a + 1) * QUAD] for a in range(flat.shape[-1] // QUAD)]
 
 
+def reduce_weights(trunk_neck, z, group):
+    heads, n_dp = lax.axis_size("head"), lax.axis_size("dp")
+    each = BOT // heads
+    rows = trunk_neck.shape[1] // 16
+    if trunk_neck.shape[1] % 16 or 2 * rows < each or n_dp < 4:
+        return None, ()
+    room = -(-rows // 8) * 8
+    mine = trunk_neck[0].reshape(rows, FEAT).astype(BF)
+    mine = jnp.concatenate([mine, jnp.zeros((room - rows, FEAT), BF)], axis=0)
+    mine = lax.optimization_barrier(mine)
+    held = mine
+    for m in range(2, n_dp, 2):
+        got = lax.ppermute(mine, "dp", [(c, c ^ m) for c in range(2)])
+        held = jnp.where((group ^ m) < 2, got, held)
+    slots = exchange(held)
+    stack = jnp.stack(slots)
+    stack = jnp.concatenate([stack, xor_move(stack, "dp", 1)], axis=0).reshape(-1, FEAT)
+    channel = jnp.arange(BOT, dtype=jnp.int32)
+    place = channel % each
+    source = ((place // rows) ^ (group & 1)) * heads + ((channel // each) ^ z)
+    source = source * room + place % rows
+    pick = (source[:, None] == jnp.arange(stack.shape[0], dtype=jnp.int32)[None, :]).astype(BF)
+    return jnp.dot(pick, stack, preferred_element_type=F32).astype(BF), slots
+
+
 def owner_tables(n_dp, share_rows, wide, heads):
     quarter = BOT // heads
     places = []
@@ -716,20 +741,15 @@
     quarter = ASP // heads
 
     n_dp = lax.axis_size("dp")
-    neck_low = trunk_neck.reshape(1, -1, BOT).astype(BF)
+    reduce_w, first = reduce_weights(trunk_neck, z, group)
+    neck_low = held_until(trunk_neck, *first).reshape(1, -1, BOT).astype(BF)
     neck_low = lax.all_gather(neck_low, "head", axis=0, tiled=True)
-    neck_low = lax.all_gather(neck_low, "dp", axis=1, tiled=True)
-    x_left, x_right = [features, line_shift(features, 1)], [features, line_shift(features, -1)]
-    neck_low, x_left[1], x_right[1] = tie(neck_low, x_left[1], x_right[1])
-    first_end = FEAT // heads
-    second_end = first_end + 9 * BOT // heads
-    reduce_w = neck_low[:, :first_end].reshape(BOT, FEAT)
-    middle = neck_low[:, first_end:second_end].reshape(heads, 9, BOT // heads, BOT)
-    middle = jnp.moveaxis(middle, 0, 1).reshape(9, BOT, BOT)
-    expand_w = neck_low[:, second_end:].reshape(FEAT, BOT)
-
-
-    flat_total = trunk_aspp.shape[1] * n_dp // 16
+    held_features = held_until(features, *first)
+    x_left = [features, line_shift(held_features, 1)]
+    x_right = [features, line_shift(held_features, -1)]
+    if reduce_w is None:
+        neck_low = lax.all_gather(neck_low, "dp", axis=1, tiled=True)
+        reduce_w = neck_low[:, : FEAT // heads].reshape(BOT, FEAT)
     own_rows = trunk_aspp.shape[1]
     frames, frame_rows = frames_of(own_rows, n_dp)
     inset = (group * own_rows) % 256
@@ -790,17 +810,19 @@
     lidar_n = lidar[0]
     mean_one, inv_one = coefficients(total, square)
     low_one = (jax.nn.silu(scaled(normed(pre_one, mean_one, inv_one), gain_one, shift_one)) * mask_own).astype(BF)
+    low_one, x_left[1], x_right[1] = tie(low_one, x_left[1], x_right[1])
     slots = exchange(low_one)
-    aspp_rows = assemble(held_until(gathered, low_one), own_rows, flat_total)
-    project_q = aspp_rows[29 * quarter : flat_total].reshape(quarter, 5, heads, quarter)
-    project_q = jnp.moveaxis(project_q, 2, 0).reshape(heads, quarter, 5 * quarter)
-    received = [lax.dynamic_index_in_dim(project_q, z, 0, False)]
-    for m in range(1, heads):
-        received.append(xor_move(lax.dynamic_index_in_dim(project_q, z ^ m, 0, False), "head", m))
-    project_own = jnp.concatenate(in_order(received, z), axis=0)
-    tap_wt = aspp_rows.T
-    slots, tap_wt, project_own = tie(slots, tap_wt, project_own)
-    x_left[1], x_right[1] = held_until((x_left[1], x_right[1]), slots)
+    if first:
+        neck_low = lax.all_gather(held_until(neck_low, low_one), "dp", axis=1, tiled=True)
+    first_end = FEAT // heads
+    second_end = first_end + 9 * BOT // heads
+    middle = neck_low[:, first_end:second_end].reshape(heads, 9, BOT // heads, BOT)
+    middle = jnp.moveaxis(middle, 0, 1).reshape(9, BOT, BOT)
+    expand_w = neck_low[:, second_end:].reshape(FEAT, BOT)
+
+
+    flat_total = trunk_aspp.shape[1] * n_dp // 16
+    x_left[-1], x_right[-1] = held_until((x_left[-1], x_right[-1]), slots)
     for _ in range(1, heads - 1):
         x_left.append(line_shift(x_left[-1], 1))
         x_right.append(line_shift(x_right[-1], -1))
@@ -820,6 +842,7 @@
     hat_two = normed(pre_two, mean_two, inv_two)
     in_two = scaled(hat_two, gain_two, shift_two)
     h_two = (jax.nn.silu(in_two) * mask).astype(BF)
+    aspp_rows = assemble(held_until(gathered, pre_two), own_rows, flat_total)
     pre_three = jnp.dot(expand_w, h_two, preferred_element_type=F32)
     mean_three, inv_three = coefficients(*unpack(sum_dp(pack(moments(pre_three, mask))), (FEAT, FEAT)))
     pre_three = pre_three.astype(BF)
@@ -831,6 +854,12 @@
     )
 
     moved = side_rows(side)
+    project_q = held_until(aspp_rows, side)[29 * quarter : flat_total].reshape(quarter, 5, heads, quarter)
+    project_q = jnp.moveaxis(project_q, 2, 0).reshape(heads, quarter, 5 * quarter)
+    received = [lax.dynamic_index_in_dim(project_q, z, 0, False)]
+    for m in range(1, heads):
+        received.append(xor_move(lax.dynamic_index_in_dim(project_q, z ^ m, 0, False), "head", m))
+    project_own = jnp.concatenate(in_order(received, z), axis=0)
     branches = [middle_rows[0]]
     for br in range(3):
         branches.append(
@@ -918,7 +947,9 @@
         * (gain_proj * inv_proj)[:, None]
         * (grad_act - (back_shift_proj / total_n)[:, None] - hat_proj * (back_gain_proj / total_n)[:, None])
     ).astype(BF)
-    grad_proj = jnp.concatenate(in_order(exchange(grad_proj), z), axis=1)
+    tap_wt = held_until(aspp_rows, grad_proj).T
+    grad_blocks, tap_wt = tie(exchange(grad_proj), tap_wt)
+    grad_proj = jnp.concatenate(in_order(grad_blocks, z), axis=1)
     grad_project = dot(grad_proj, joined, (1,), (1,)).astype(BF).reshape(heads, quarter, 5 * quarter)
     grad_joined = dot(project_own, grad_proj, (0,), (0,))
 

time: 841 us -> 837 us (level)
  waiting for transfers between devices: 232 us -> 192 us
  starting transfers between devices: 171 us -> 209 us
    ppermute x103 -> x107, waiting for transfers between devices: 97.9 us -> 165 us  [xor_move(): return lax.ppermute(x, axis, [(i, i ^ mask) for i in range(n)])]
    ppermute x6, waiting for transfers between devices: 70.5 us -> 11.8 us  [line_shift(): lax.ppermute(x, 'head', [(i, i + by) for i in range(n) if 0 <= i + by < n])]
    all_gather x1, waiting for transfers between devices: 32.5 us -> 0.02 us  [shards(): neck_low = lax.all_gather(neck_low, 'head', axis=0, tiled=True)]
    all_gather x1, waiting for transfers between devices: 19.9 us -> 0.01 us  [shards(): gathered = lax.all_gather(framed, 'dp', axis=0)]
    ppermute x103 -> x107, starting transfers between devices: 127 us -> 147 us  [xor_move(): return lax.ppermute(x, axis, [(i, i ^ mask) for i in range(n)])]
    optimization_barrier x0 -> x1, local copies, waits for them, and re-layouts: none -> 10.5 us  [held_until(): return lax.optimization_barrier((value, others))[0]]
    pallas_call x1 -> x0, local copies, waits for them, and re-layouts: 10.4 us -> none  [assemble(): pl.pallas_call(functools.partial(assemble_kernel, pieces), grid=(width //...]
    ppermute x0 -> x3, starting transfers between devices: none -> 9.82 us  [reduce_weights(): got = lax.ppermute(mine, 'dp', [(c, c ^ m) for c in range(2)])]
  transfers between devices with their start and end apart: 124 -> 131, of which waited for: 51 -> 45; matrix products, arithmetic and copies ran while one was open for 23% -> 23% of each run, Pallas kernels for 12% -> 11%
where the time goes in v4:
time: 837 us; the launch traced here: 827 us
  starting transfers between devices  209 us (25%)
  waiting for transfers between devices  192 us (23%)
  Pallas kernels  133 us (16%)
  other arithmetic  99.1 us (12%)
  matrix products  90.8 us (11%)
  local copies, waits for them, and re-layouts  79.3 us (9%)
  between operations  24.3 us (3%)
    ppermute x107, waiting for transfers between devices, xor_move(): return lax.ppermute(x, axis, [(i, i ^ mask) for i in range(n)])  165 us
    ppermute x107, starting transfers between devices, xor_move(): return lax.ppermute(x, axis, [(i, i ^ mask) for i in range(n)])  147 us
    dot_general x13, matrix products, dot(): lax.dot_general(a, b, ((ca, cb), ((), ())), preferred_element_type=F32)  48.5 us
    pallas_call x1, Pallas kernels, aspp_forward(): pl.pallas_call(aspp_forward_kernel, grid_spec=pltpu.PrefetchScalarGridSpe...  39.3 us
    pallas_call x1, Pallas kernels, aspp_backward(): pl.pallas_call(aspp_backward_kernel, grid=(quads,), in_specs=[pl.BlockSpe...  29.3 us
    ppermute x6, starting transfers between devices, line_shift(): lax.ppermute(x, 'head', [(i, i + by) for i in range(n) if 0 <= i + by < n])  28.6 us
    pallas_call x2, Pallas kernels, taps_grad(): pl.pallas_call(functools.partial(taps_grad_kernel, starts), grid=(width /...  26.3 us
    unnamed x253, local copies, waits for them, and re-layouts  20 us
  transfers between devices with their start and end apart: 131, of which 45 were waited for; matrix products, arithmetic and copies ran while one was open for 23% of the time, Pallas kernels for 11%

profile of v4, /device:TPU:0, one launch (start us, length us, event | category | flops | bytes accessed | tf_op | source)
XLA Modules:
  0.0 826.6 jit_solution(4669434897525233903)
XLA Ops:
  8.7 5.8 collective-permute-start
  22.0 5.0 collective-permute-done.2
  35.6 5.3 collective-permute-done.3
  40.9 12.1 %collective-permute-done.4 = bf16[72,2048]{1,0:T(8,128)(2,1)S(1)} collective-permute-done((bf16[72,2048]{1,0:T(8,128)(2,1)S(1)}, bf16[72,2048]{1,0:T(8,128)(2,1)S(1)}, u32[]{:S(2)}, u32[]{:S(2)}) %collective-permute-start.4) | collective-permute-done | bytes 294944 | tf_op jit(solution)/shard_map/ppermute | solution.py:43
  53.0 7.8 collective-permute-start.14
  70.6 3.5 convolution_convert_fusion.2
  77.7 3.6 collective-permute-start.8
  90.7 35.5 %collective-permute-done.11 = f32[1152]{0:T(1024)S(1)} collective-permute-done((f32[1152]{0:T(1024)S(1)}, f32[1152]{0:T(1024)S(1)}, u32[]{:S(2)}, u32[]{:S(2)}) %collective-permute-start.11) | collective-permute-done | bytes 4640 | tf_op jit(solution)/shard_map/ppermute | solution.py:43
  131.7 4.0 collective-permute-start.18
  135.7 15.7 %collective-permute-done.16.s1 = bf16[512,512]{1,0:T(8,128)(2,1)S(1)} collective-permute-done((bf16[512,512]{1,0:T(8,128)(2,1)S(1)}, bf16[512,512]{1,0:T(8,128)(2,1)S(1)}, u32[]{:S(2)}, u32[]{:S(2)}) %collective-permute-start.16) | collective-permute-done | bytes 524320 | tf_op jit(solution)/shard_map/ppermute | solution.py:43
  151.4 18.6 %collective-permute-done.17.s2 = bf16[512,512]{1,0:T(8,128)(2,1)S(1)} collective-permute-done((bf16[512,512]{1,0:T(8,128)(2,1)S(1)}, bf16[512,512]{1,0:T(8,128)(2,1)S(1)}, u32[]{:S(2)}, u32[]{:S(2)}) %collective-permute-start.17) | collective-permute-done | bytes 524320 | tf_op jit(solution)/shard_map/ppermute | solution.py:43
  175.9 10.8 %collective-permute-start.31 = (bf16[2048,512]{1,0:T(8,128)(2,1)}, bf16[2048,512]{1,0:T(8,128)(2,1)}, u32[]{:S(2)}, u32[]{:S(2)}) collective-permute-start(bf16[2048,512]{1,0:T(8,128)(2,1)} %collective-permute-done.14.x4), channel_id=1, source_target_pairs={{0,1},{1,2},{2,3},{4,5},{5,6},{6,7},{8,9},{9,10},{10,11},{12,13},{... | collective-permute-start | bytes 6291464 | tf_op jit(solution)/shard_map/ppermute | solution.py:105
  191.8 15.4 %shard_map.359 = (f32[512,2048]{1,0:T(8,128)}, bf16[512,2048]{1,0:T(8,128)(2,1)S(1)}, f32[512,128]{1,0:T(8,128)S(1)}, f32[512,128]{1,0:T(8,128)S(1)}) custom-call(s32[1]{0:T(128)} %bitcast.2.z_ref, bf16[512,512]{1,0:T(8,128)(2,1)S(1)} %multiply_convert_fusion.7.s0, bf16[512,512]{1,0:T(8,128)(2,1)S(1)} %collective-permute-done.16.s1, ...), custom_call_target="tpu_custom_call" | custom-call | flops 9663676416 | bytes 16777216 | tf_op jit(solution)/shard_map/pallas_call | solution.py:323
  212.2 3.9 collective-permute-start.21
  220.9 5.7 collective-permute-done.29.x2
  228.5 6.1 collective-permute-start.32
  237.7 8.6 %multiply_reduce_fusion = (f32[2048]{0:T(1024)S(1)}, f32[2048]{0:T(1024)S(1)}, bf16[2048,2048]{1,0:T(8,128)(2,1)}) fusion(f32[2048]{0:T(1024)S(1)} %fusion.112, bf16[2048,512]{1,0:T(8,128)(2,1)S(1)} %bitcast.489, f32[512,2048]{1,0:T(8,128)S(1)} %copy-done.26, f32[512]{0:T(512)S(1)} %bitcast.533, f32[512]{0:T(512)S(1)} %get-tuple-element.196, ...), kind=kOutput, calls=%fused_computation.1 | convolution fusion | flops 4326420480 | bytes 14712832 | tf_op jit(solution)/shard_map/dot_general | solution.py:846
  250.3 5.0 collective-permute-start.26
  259.1 6.3 shard_map.360.w_ref
  271.2 3.4 collective-permute-done.30.x3
  276.7 39.3 %shard_map.361 = (bf16[2048,2048]{1,0:T(8,128)(2,1)}, bf16[2048,2048]{1,0:T(8,128)(2,1)}, f32[4,64,2048]{2,1,0:T(8,128)}, bf16[6,4,64,512]{3,2,1,0:T(8,128)(2,1)}, f32[4,64,128]{2,1,0:T(8,128)}) custom-call(s32[1]{0:T(128)} %bitcast.2.z_ref, bf16[2048,2048]{1,0:T(8,128)(2,1)} %get-tuple-element.219.pre_ref, f32[2048,2]{1,0:T(8,128)} %copy.87.coef_ref, ...), custom_call_target="tpu_custom_call" | custom-call | flops 15569256448 | bytes 50331648 | tf_op jit(solution)/shard_map/pallas_call | solution.py:476
  325.8 7.2 collective-permute-start.38
  363.4 3.5 collective-permute-start.44
  371.2 8.2 shard_map.362
  379.4 6.3 collective-permute-done.44
  399.0 3.6 collective-permute-start.50
  445.2 10.5 %copy.92 = bf16[1920,2048]{0,1:T(8,128)(2,1)} copy(bf16[1920,2048]{1,0:T(8,128)(2,1)} %copy-done) | data formatting | bytes 15728640 | tf_op jit(solution)/shard_map/optimization_barrier | solution.py:170
  455.7 5.5 collective-permute-done.61
  471.2 4.1 collective-permute-start.71
  477.8 3.4 collective-permute-done.65
  494.4 5.9 collective-permute-done.69
  503.8 29.3 %shard_map.363 = (bf16[1920,2048]{1,0:T(8,128)(2,1)}, bf16[2048,2048]{1,0:T(8,128)(2,1)}, f32[2048,128]{1,0:T(8,128)}, f32[2048,128]{1,0:T(8,128)}) custom-call(bf16[64,2048]{1,0:T(8,128)(2,1)} %slice.679.one_ref, bf16[3,3,4,64,512]{4,3,2,1,0:T(8,128)(2,1)} %pad_maximum_fusion.1.rows_ref, f32[64,128]{1,0:T(8,128)} %broadcast_in_dim.31.pool_in, ...), custom_call_target="tpu_custom_call" | custom-call | flops 16106127360 | bytes 50331648 | tf_op jit(solution)/shard_map/pallas_call | solution.py:556
  542.1 13.1 %shard_map.364 = bf16[8,256,1024]{2,1,0:T(8,128)(2,1)S(1)} custom-call(bf16[1920,2048]{1,0:T(8,128)(2,1)} %get-tuple-element.120.spread_ref, bf16[2048,2048]{1,0:T(8,128)(2,1)} %get-tuple-element.116.y_ref, bf16[48,2048]{1,0:T(8,128)(2,1)S(1)} %concatenate.182.project_ref), custom_call_target="tpu_custom_call" | custom-call | flops 8053063680 | bytes 20971520 | tf_op jit(solution)/shard_map/pallas_call | solution.py:600
  561.7 13.2 %shard_map.365 = bf16[8,256,1024]{2,1,0:T(8,128)(2,1)S(1)} custom-call(bf16[1920,2048]{1,0:T(8,128)(2,1)} %get-tuple-element.120.spread_ref, bf16[2048,2048]{1,0:T(8,128)(2,1)} %get-tuple-element.116.y_ref, bf16[48,2048]{1,0:T(8,128)(2,1)S(1)} %concatenate.182.project_ref), custom_call_target="tpu_custom_call" | custom-call | flops 8053063680 | bytes 20971520 | tf_op jit(solution)/shard_map/pallas_call | solution.py:600
  577.0 9.9 %multiply_convert_fusion = bf16[2048,2048]{1,0:T(8,128)(2,1)S(1)} fusion(bf16[2048,2048]{1,0:T(8,128)(2,1)} %get-tuple-element.219.pre_ref, bf16[2048,2048]{1,0:T(8,128)(2,1)} %get-tuple-element.110, f32[2048]{0:T(1024)S(1)} %get-tuple-element.344, f32[2048]{0:T(1024)S(1)} %copy-done.65, f32[2048]{0:T(1024)S(1)} %copy-done.66, ...), kind=kLoop, calls=%fused_computation.3 | loop fusion | flops 41943040 | bytes 25214976 | tf_op jit(solution)/shard_map/convert_element_type | solution.py:1029
  586.9 8.5 %fusion.148 = (f32[512]{0:T(512)S(1)}, f32[512]{0:T(512)S(1)}, f32[512,2048]{1,0:T(8,128)}) fusion(f32[512]{0:T(512)S(1)} %copy-done.91, f32[512,2048]{1,0:T(8,128)S(1)} %copy-done.27, f32[512]{0:T(512)S(1)} %copy-done.93, f32[512]{0:T(512)S(1)} %bitcast.534, f32[512]{0:T(512)S(1)} %bitcast.526, f32[2048]{0:T(1024)S(1)} %fusion.112, ...), kind=kOutput, calls=%fused_computation.526 | convolution fusion | flops 4311743488 | bytes 18894848 | tf_op jit(solution)/shard_map/dot_general | solution.py:38
  608.6 6.9 convolution_convert_fusion.1
  623.4 6.2 fusion.178
  629.7 3.8 collective-permute-start.93
  635.0 7.8 shard_map.366
  642.8 18.7 %fusion.147 = (f32[512]{0:T(512)S(1)}, f32[512]{0:T(512)S(1)}, f32[512,2048]{1,0:T(8,128)}) fusion(f32[512]{0:T(512)S(1)} %copy-done.80, f32[512,2048]{1,0:T(8,128)} %fusion.178, f32[512]{0:T(512)S(1)} %copy-done.82, f32[512]{0:T(512)S(1)} %bitcast.522, f32[512]{0:T(512)S(1)} %bitcast.520, f32[2048]{0:T(1024)S(1)} %fusion.112, ...), kind=kOutput, calls=%fused_computation.525 | convolution fusion | flops 9680453632 | bytes 32002048 | tf_op jit(solution)/shard_map/dot_general | solution.py:1054
  680.5 15.6 %convolution_convert_fusion.3 = bf16[9,512,512]{2,1,0:T(8,128)(2,1)} fusion(bf16[9,512,2048]{2,1,0:T(8,128)(2,1)} %shard_map.366, bf16[512,2048]{1,0:T(8,128)(2,1)S(1)} %copy-done.18), kind=kOutput, calls=%fused_computation.29 | convolution fusion | flops 9666035712 | bytes 25690112 | tf_op jit(solution)/shard_map/dot_general | solution.py:38
  705.1 8.3 %convolution_convert_fusion = bf16[512,2048]{1,0:T(8,128)(2,1)S(1)} fusion(bf16[2048,2048]{1,0:T(8,128)(2,1)S(1)} %bitcast.472, f32[512,2048]{1,0:T(8,128)} %get-tuple-element.371, f32[512,2048]{1,0:T(8,128)} %fusion.178, f32[512]{0:T(512)S(1)} %get-tuple-element.348, f32[512]{0:T(512)S(1)} %get-tuple-element.350, f32[512]{0:T(512)S(1)} %copy-done.80, ...), kind=kOutput, calls=%fused_computation.25 | convolution fusion | flops 4304404480 | bytes 18892800 | tf_op jit(solution)/shard_map/dot_general | solution.py:38
  721.4 4.9 collective-permute-done.108
  735.3 16.7 %collective-permute-done.114 = bf16[13,4,1,2,16,256]{5,4,3,1,0,2:T(8,128)(2,1)S(1)} collective-permute-done((bf16[13,4,1,2,16,256]{5,4,3,1,0,2:T(8,128)(2,1)S(1)}, bf16[13,4,1,2,16,256]{5,4,3,1,0,2:T(8,128)(2,1)S(1)}, u32[]{:S(2)}, u32[]{:S(2)}) %collective-permute-start.114) | collective-permute-done | bytes 852000 | tf_op jit(solution)/shard_map/ppermute | solution.py:43
  775.3 6.8 collective-permute-done.117
  799.6 3.5 all-to-all-start
  806.1 6.3 multiply_subtract_fusion
  (779 shorter events, 343.1 us)
Async XLA Ops:
  7.2 120.8 %all-gather.6.cloned.1.call-start = ((), (), s32[]{:S(2)}) async-start(), calls=%async_computation.2 | async-start | bytes 1392640 | tf_op jit(solution)/shard_map/all_gather | solution.py:746
  29.5 23.5 %collective-permute-start.4 = (bf16[72,2048]{1,0:T(8,128)(2,1)S(1)}, bf16[72,2048]{1,0:T(8,128)(2,1)S(1)}, u32[]{:S(2)}, u32[]{:S(2)}) collective-permute-start(bf16[72,2048]{1,0:T(8,128)(2,1)S(1)} %get-tuple-element.218), channel_id=1, source_target_pairs={{0,2},{1,3},{2,0},{3,1},{4,6},{5,7},{6,4},{7,5},{8,10},{9,11},{10,... | collective-permute-start | bytes 884744 | tf_op jit(solution)/shard_map/ppermute | solution.py:43
  32.1 20.9 %collective-permute-start.5 = (bf16[72,2048]{1,0:T(8,128)(2,1)S(1)}, bf16[72,2048]{1,0:T(8,128)(2,1)S(1)}, u32[]{:S(2)}, u32[]{:S(2)}) collective-permute-start(bf16[72,2048]{1,0:T(8,128)(2,1)S(1)} %get-tuple-element.218), channel_id=1, source_target_pairs={{0,3},{1,2},{2,1},{3,0},{4,7},{5,6},{6,5},{7,4},{8,11},{9,10},{10,... | collective-permute-start | bytes 884744 | tf_op jit(solution)/shard_map/ppermute | solution.py:43
  53.0 75.0 %collective-permute-start.14 = (bf16[2048,512]{1,0:T(8,128)(2,1)S(1)}, bf16[2048,512]{1,0:T(8,128)(2,1)}, u32[]{:S(2)}, u32[]{:S(2)}) collective-permute-start(bf16[2048,512]{1,0:T(8,128)(2,1)S(1)} %copy-done.5), channel_id=1, source_target_pairs={{0,1},{1,2},{2,3},{4,5},{5,6},{6,7},{8,9},{9,10},{10,11},{12,13},{... | collective-permute-start | bytes 6291464 | tf_op jit(solution)/shard_map/ppermute | solution.py:105
  60.8 67.2 %collective-permute-start.15 = (bf16[2048,512]{1,0:T(8,128)(2,1)S(1)}, bf16[2048,512]{1,0:T(8,128)(2,1)}, u32[]{:S(2)}, u32[]{:S(2)}) collective-permute-start(bf16[2048,512]{1,0:T(8,128)(2,1)S(1)} %copy-done.5), channel_id=1, source_target_pairs={{1,0},{2,1},{3,2},{5,4},{6,5},{7,6},{9,8},{10,9},{11,10},{13,12},{... | collective-permute-start | bytes 6291464 | tf_op jit(solution)/shard_map/ppermute | solution.py:105
  65.9 120.7 %all-gather.8.cloned.1.call-start = ((), (), s32[]{:S(2)}) async-start(), calls=%async_computation.3 | async-start | bytes 10027008 | tf_op jit(solution)/shard_map/all_gather | solution.py:816
  84.9 41.3 %collective-permute-start.11 = (f32[1152]{0:T(1024)S(1)}, f32[1152]{0:T(1024)S(1)}, u32[]{:S(2)}, u32[]{:S(2)}) collective-permute-start(f32[1152]{0:T(1024)S(1)} %add_add_fusion.4), channel_id=1, source_target_pairs={{0,1},{1,0},{2,3},{3,2},{4,5},{5,4},{6,7},{7,6},{8,9},{9,8},{10,11... | collective-permute-start | bytes 13832 | tf_op jit(solution)/shard_map/ppermute | solution.py:43
  87.7 38.6 %collective-permute-start.12 = (f32[1152]{0:T(1024)S(1)}, f32[1152]{0:T(1024)S(1)}, u32[]{:S(2)}, u32[]{:S(2)}) collective-permute-start(f32[1152]{0:T(1024)S(1)} %add_add_fusion.4), channel_id=1, source_target_pairs={{0,2},{1,3},{2,0},{3,1},{4,6},{5,7},{6,4},{7,5},{8,10},{9,11},{10,... | collective-permute-start | bytes 13832 | tf_op jit(solution)/shard_map/ppermute | solution.py:43
  88.6 37.6 %collective-permute-start.13 = (f32[1152]{0:T(1024)S(1)}, f32[1152]{0:T(1024)S(1)}, u32[]{:S(2)}, u32[]{:S(2)}) collective-permute-start(f32[1152]{0:T(1024)S(1)} %add_add_fusion.4), channel_id=1, source_target_pairs={{0,3},{1,2},{2,1},{3,0},{4,7},{5,6},{6,5},{7,4},{8,11},{9,10},{10,... | collective-permute-start | bytes 13832 | tf_op jit(solution)/shard_map/ppermute | solution.py:43
  128.0 131.0 %all-gather.4.cloned.1.call-start = ((), (), s32[]{:S(2)}) async-start(), calls=%async_computation.1 | async-start | bytes 9437184 | tf_op jit(solution)/shard_map/all_gather | solution.py:760
  131.2 445.7 %all-reduce.4.cloned.1.call-start = ((), (), s32[]{:S(2)}) async-start(), calls=%async_computation.4 | async-start | bytes 1622016 | tf_op jit(solution)/shard_map/psum | solution.py:928
  131.3 20.1 %collective-permute-start.16 = (bf16[512,512]{1,0:T(8,128)(2,1)S(1)}, bf16[512,512]{1,0:T(8,128)(2,1)S(1)}, u32[]{:S(2)}, u32[]{:S(2)}) collective-permute-start(bf16[512,512]{1,0:T(8,128)(2,1)S(1)} %multiply_convert_fusion.7.s0), channel_id=1, source_target_pairs={{0,1},{1,0},{2,3},{3,2},{4,5},{5,4},{6,7},{7,6},{8,9},{9,8},{10,11... | collective-permute-start | bytes 1572872 | tf_op jit(solution)/shard_map/ppermute | solution.py:43
  131.7 38.2 %collective-permute-start.17 = (bf16[512,512]{1,0:T(8,128)(2,1)S(1)}, bf16[512,512]{1,0:T(8,128)(2,1)S(1)}, u32[]{:S(2)}, u32[]{:S(2)}) collective-permute-start(bf16[512,512]{1,0:T(8,128)(2,1)S(1)} %multiply_convert_fusion.7.s0), channel_id=1, source_target_pairs={{0,2},{1,3},{2,0},{3,1},{4,6},{5,7},{6,4},{7,5},{8,10},{9,11},{10,... | collective-permute-start | bytes 1572872 | tf_op jit(solution)/shard_map/ppermute | solution.py:43
  131.7 38.2 %collective-permute-start.18 = (bf16[512,512]{1,0:T(8,128)(2,1)S(1)}, bf16[512,512]{1,0:T(8,128)(2,1)S(1)}, u32[]{:S(2)}, u32[]{:S(2)}) collective-permute-start(bf16[512,512]{1,0:T(8,128)(2,1)S(1)} %multiply_convert_fusion.7.s0), channel_id=1, source_target_pairs={{0,3},{1,2},{2,1},{3,0},{4,7},{5,6},{6,5},{7,4},{8,11},{9,10},{10,... | collective-permute-start | bytes 1572872 | tf_op jit(solution)/shard_map/ppermute | solution.py:43
  171.2 20.6 %collective-permute-start.19 = (bf16[512,512]{1,0:T(8,128)(2,1)}, bf16[512,512]{1,0:T(8,128)(2,1)}, u32[]{:S(2)}, u32[]{:S(2)}) collective-permute-start(bf16[512,512]{1,0:T(8,128)(2,1)} %get-tuple-element.231), channel_id=1, source_target_pairs={{0,4},{4,8},{8,12},{16,20},{20,24},{24,28},{1,5},{5,9},{9,13},{17,... | collective-permute-start | bytes 1572872 | tf_op jit(solution)/shard_map/ppermute | solution.py:100
  173.3 18.5 %collective-permute-start.20 = (bf16[512,512]{1,0:T(8,128)(2,1)}, bf16[512,512]{1,0:T(8,128)(2,1)}, u32[]{:S(2)}, u32[]{:S(2)}) collective-permute-start(bf16[512,512]{1,0:T(8,128)(2,1)} %get-tuple-element.230), channel_id=1, source_target_pairs={{4,0},{8,4},{12,8},{20,16},{24,20},{28,24},{5,1},{9,5},{13,9},{21,... | collective-permute-start | bytes 1572872 | tf_op jit(solution)/shard_map/ppermute | solution.py:100
  174.6 52.0 %collective-permute-start.29 = (bf16[2048,512]{1,0:T(8,128)(2,1)}, bf16[2048,512]{1,0:T(8,128)(2,1)S(1)}, u32[]{:S(2)}, u32[]{:S(2)}) collective-permute-start(bf16[2048,512]{1,0:T(8,128)(2,1)} %collective-permute-done.15.x1), channel_id=1, source_target_pairs={{1,0},{2,1},{3,2},{5,4},{6,5},{7,6},{9,8},{10,9},{11,10},{13,12},{... | collective-permute-start | bytes 6291464 | tf_op jit(solution)/shard_map/ppermute | solution.py:105
  175.9 52.6 %collective-permute-start.31 = (bf16[2048,512]{1,0:T(8,128)(2,1)}, bf16[2048,512]{1,0:T(8,128)(2,1)}, u32[]{:S(2)}, u32[]{:S(2)}) collective-permute-start(bf16[2048,512]{1,0:T(8,128)(2,1)} %collective-permute-done.14.x4), channel_id=1, source_target_pairs={{0,1},{1,2},{2,3},{4,5},{5,6},{6,7},{8,9},{9,10},{10,11},{12,13},{... | collective-permute-start | bytes 6291464 | tf_op jit(solution)/shard_map/ppermute | solution.py:105
  217.0 19.4 %collective-permute-start.22 = (f32[1024]{0:T(1024)S(1)}, f32[1024]{0:T(1024)S(1)}, u32[]{:S(2)}, u32[]{:S(2)}) collective-permute-start(f32[1024]{0:T(1024)S(1)} %fusion.140), channel_id=1, source_target_pairs={{0,8},{4,12},{8,0},{12,4},{16,24},{20,28},{24,16},{28,20},{1,9},{5... | collective-permute-start | bytes 12296 | tf_op jit(solution)/shard_map/ppermute | solution.py:43
  219.3 17.1 %collective-permute-start.24 = (f32[1024]{0:T(1024)S(1)}, f32[1024]{0:T(1024)S(1)}, u32[]{:S(2)}, u32[]{:S(2)}) collective-permute-start(f32[1024]{0:T(1024)S(1)} %fusion.140), channel_id=1, source_target_pairs={{0,24},{4,28},{8,16},{12,20},{16,8},{20,12},{24,0},{28,4},{1,25},{... | collective-permute-start | bytes 12296 | tf_op jit(solution)/shard_map/ppermute | solution.py:43
  226.6 47.9 %collective-permute-start.30 = (bf16[2048,512]{1,0:T(8,128)(2,1)S(1)}, bf16[2048,512]{1,0:T(8,128)(2,1)}, u32[]{:S(2)}, u32[]{:S(2)}) collective-permute-start(bf16[2048,512]{1,0:T(8,128)(2,1)S(1)} %collective-permute-done.29.x2), channel_id=1, source_target_pairs={{1,0},{2,1},{3,2},{5,4},{6,5},{7,6},{9,8},{10,9},{11,10},{13,12},{... | collective-permute-start | bytes 6291464 | tf_op jit(solution)/shard_map/ppermute | solution.py:105
  228.5 48.3 %collective-permute-start.32 = (bf16[2048,512]{1,0:T(8,128)(2,1)}, bf16[2048,512]{1,0:T(8,128)(2,1)}, u32[]{:S(2)}, u32[]{:S(2)}) collective-permute-start(bf16[2048,512]{1,0:T(8,128)(2,1)} %collective-permute-done.31.x5), channel_id=1, source_target_pairs={{0,1},{1,2},{2,3},{4,5},{5,6},{6,7},{8,9},{9,10},{10,11},{12,13},{... | collective-permute-start | bytes 6291464 | tf_op jit(solution)/shard_map/ppermute | solution.py:105
  250.3 18.2 %collective-permute-start.26 = (f32[4096]{0:T(1024)S(1)}, f32[4096]{0:T(1024)S(1)}, u32[]{:S(2)}, u32[]{:S(2)}) collective-permute-start(f32[4096]{0:T(1024)S(1)} %fusion.143), channel_id=1, source_target_pairs={{0,8},{4,12},{8,0},{12,4},{16,24},{20,28},{24,16},{28,20},{1,9},{5... | collective-permute-start | bytes 49160 | tf_op jit(solution)/shard_map/ppermute | solution.py:43
  319.8 29.1 %collective-permute-start.33 = (bf16[64,320]{0,1:T(8,128)(2,1)}, bf16[64,320]{0,1:T(8,128)(2,1)}, u32[]{:S(2)}, u32[]{:S(2)}) collective-permute-start(bf16[64,320]{0,1:T(8,128)(2,1)} %get-tuple-element.286), channel_id=1, source_target_pairs={{0,1},{1,0},{2,3},{3,2},{4,5},{5,4},{6,7},{7,6},{8,9},{9,8},{10,11... | collective-permute-start | bytes 122888 | tf_op jit(solution)/shard_map/ppermute | solution.py:43
  322.4 26.5 %collective-permute-start.34 = (bf16[64,320]{0,1:T(8,128)(2,1)}, bf16[64,320]{0,1:T(8,128)(2,1)}, u32[]{:S(2)}, u32[]{:S(2)}) collective-permute-start(bf16[64,320]{0,1:T(8,128)(2,1)} %get-tuple-element.285), channel_id=1, source_target_pairs={{0,2},{1,3},{2,0},{3,1},{4,6},{5,7},{6,4},{7,5},{8,10},{9,11},{10,... | collective-permute-start | bytes 122888 | tf_op jit(solution)/shard_map/ppermute | solution.py:43
  325.6 23.2 %collective-permute-start.35 = (bf16[64,320]{0,1:T(8,128)(2,1)}, bf16[64,320]{0,1:T(8,128)(2,1)}, u32[]{:S(2)}, u32[]{:S(2)}) collective-permute-start(bf16[64,320]{0,1:T(8,128)(2,1)} %get-tuple-element.284), channel_id=1, source_target_pairs={{0,3},{1,2},{2,1},{3,0},{4,7},{5,6},{6,5},{7,4},{8,11},{9,10},{10,... | collective-permute-start | bytes 122888 | tf_op jit(solution)/shard_map/ppermute | solution.py:43
  363.4 22.3 %collective-permute-start.44 = (bf16[256,512]{1,0:T(8,128)(2,1)}, bf16[256,512]{1,0:T(8,128)(2,1)}, u32[]{:S(2)}, u32[]{:S(2)}) collective-permute-start(bf16[256,512]{1,0:T(8,128)(2,1)} %get-tuple-element.265), channel_id=1, source_target_pairs={{0,2},{1,3},{2,0},{3,1},{4,6},{5,7},{6,4},{7,5},{8,10},{9,11},{10,... | collective-permute-start | bytes 786440 | tf_op jit(solution)/shard_map/ppermute | solution.py:43
  366.9 18.8 %collective-permute-start.45 = (bf16[256,512]{1,0:T(8,128)(2,1)}, bf16[256,512]{1,0:T(8,128)(2,1)}, u32[]{:S(2)}, u32[]{:S(2)}) collective-permute-start(bf16[256,512]{1,0:T(8,128)(2,1)} %get-tuple-element.264), channel_id=1, source_target_pairs={{0,3},{1,2},{2,1},{3,0},{4,7},{5,6},{6,5},{7,4},{8,11},{9,10},{10,... | collective-permute-start | bytes 786440 | tf_op jit(solution)/shard_map/ppermute | solution.py:43
  439.7 21.5 %collective-permute-start.61 = (bf16[256,512]{1,0:T(8,128)(2,1)S(1)}, bf16[256,512]{1,0:T(8,128)(2,1)S(1)}, u32[]{:S(2)}, u32[]{:S(2)}) collective-permute-start(bf16[256,512]{1,0:T(8,128)(2,1)S(1)} %multiply_convert_fusion.8), channel_id=1, source_target_pairs={{0,2},{1,3},{2,0},{3,1},{4,6},{5,7},{6,4},{7,5},{8,10},{9,11},{10,... | collective-permute-start | bytes 786440 | tf_op jit(solution)/shard_map/ppermute | solution.py:43
  442.6 18.6 %collective-permute-start.62 = (bf16[256,512]{1,0:T(8,128)(2,1)S(1)}, bf16[256,512]{1,0:T(8,128)(2,1)S(1)}, u32[]{:S(2)}, u32[]{:S(2)}) collective-permute-start(bf16[256,512]{1,0:T(8,128)(2,1)S(1)} %multiply_convert_fusion.8), channel_id=1, source_target_pairs={{0,3},{1,2},{2,1},{3,0},{4,7},{5,6},{6,5},{7,4},{8,11},{9,10},{10,... | collective-permute-start | bytes 786440 | tf_op jit(solution)/shard_map/ppermute | solution.py:43
  471.2 19.0 %collective-permute-start.71 = (bf16[64,320]{1,0:T(8,128)(2,1)}, bf16[64,320]{1,0:T(8,128)(2,1)}, u32[]{:S(2)}, u32[]{:S(2)}) collective-permute-start(bf16[64,320]{1,0:T(8,128)(2,1)} %get-tuple-element.327), channel_id=1, source_target_pairs={{0,1},{1,0},{2,3},{3,2},{4,5},{5,4},{6,7},{7,6},{8,9},{9,8},{10,11... | collective-permute-start | bytes 122888 | tf_op jit(solution)/shard_map/ppermute | solution.py:43
  476.0 17.5 %collective-permute-start.73 = (bf16[64,320]{1,0:T(8,128)(2,1)}, bf16[64,320]{1,0:T(8,128)(2,1)}, u32[]{:S(2)}, u32[]{:S(2)}) collective-permute-start(bf16[64,320]{1,0:T(8,128)(2,1)} %get-tuple-element.325), channel_id=1, source_target_pairs={{0,3},{1,2},{2,1},{3,0},{4,7},{5,6},{6,5},{7,4},{8,11},{9,10},{10,... | collective-permute-start | bytes 122888 | tf_op jit(solution)/shard_map/ppermute | solution.py:43
  538.3 18.9 %collective-permute-start.74 = (f32[6144]{0:T(1024)S(1)}, f32[6144]{0:T(1024)S(1)}, u32[]{:S(2)}, u32[]{:S(2)}) collective-permute-start(f32[6144]{0:T(1024)S(1)} %fusion.144), channel_id=1, source_target_pairs={{0,8},{4,12},{8,0},{12,4},{16,24},{20,28},{24,16},{28,20},{1,9},{5... | collective-permute-start | bytes 73736 | tf_op jit(solution)/shard_map/ppermute | solution.py:43
  557.3 19.6 %collective-permute-start.77 = (f32[6144]{0:T(1024)S(1)}, f32[6144]{0:T(1024)S(1)}, u32[]{:S(2)}, u32[]{:S(2)}) collective-permute-start(f32[6144]{0:T(1024)S(1)} %add_add_fusion.1), channel_id=1, source_target_pairs={{0,1},{1,0},{2,3},{3,2},{4,5},{5,4},{6,7},{7,6},{8,9},{9,8},{10,11... | collective-permute-start | bytes 73736 | tf_op jit(solution)/shard_map/ppermute | solution.py:43
  558.4 18.4 %collective-permute-start.78 = (f32[6144]{0:T(1024)S(1)}, f32[6144]{0:T(1024)S(1)}, u32[]{:S(2)}, u32[]{:S(2)}) collective-permute-start(f32[6144]{0:T(1024)S(1)} %add_add_fusion.1), channel_id=1, source_target_pairs={{0,2},{1,3},{2,0},{3,1},{4,6},{5,7},{6,4},{7,5},{8,10},{9,11},{10,... | collective-permute-start | bytes 73736 | tf_op jit(solution)/shard_map/ppermute | solution.py:43
  595.6 19.9 %collective-permute-start.88 = (bf16[4,1,256,1024]{3,2,0,1:T(8,128)(2,1)S(1)}, bf16[4,1,256,1024]{3,2,0,1:T(8,128)(2,1)S(1)}, u32[]{:S(2)}, u32[]{:S(2)}) collective-permute-start(bf16[4,1,256,1024]{3,2,0,1:T(8,128)(2,1)S(1)} %dynamic-slice_bitcast_fusion.1), channel_id=1, source_target_pairs={{0,4},{4,0},{8,12},{12,8},{16,20},{20,16},{24,28},{28,24},{1,5},{5... | collective-permute-start | bytes 6291464 | tf_op jit(solution)/shard_map/ppermute | solution.py:43
  629.7 31.9 %collective-permute-start.93 = (bf16[4,4,1,64,512]{4,3,1,0,2:T(8,128)(2,1)S(1)}, bf16[4,4,1,64,512]{4,3,1,0,2:T(8,128)(2,1)}, u32[]{:S(2)}, u32[]{:S(2)}) collective-permute-start(bf16[4,4,1,64,512]{4,3,1,0,2:T(8,128)(2,1)S(1)} %dynamic-slice_bitcast_fusion.4), channel_id=1, source_target_pairs={{0,4},{4,0},{8,12},{12,8},{16,20},{20,16},{24,28},{28,24},{1,5},{5... | collective-permute-start | bytes 3145736 | tf_op jit(solution)/shard_map/ppermute | solution.py:43
  633.6 29.6 %collective-permute-start.92 = (bf16[1,2,256,1024]{3,2,1,0:T(8,128)(2,1)S(1)}, bf16[1,2,256,1024]{3,2,1,0:T(8,128)(2,1)}, u32[]{:S(2)}, u32[]{:S(2)}) collective-permute-start(bf16[1,2,256,1024]{3,2,1,0:T(8,128)(2,1)S(1)} %dynamic-slice_bitcast_fusion.5), channel_id=1, source_target_pairs={{0,16},{4,20},{8,24},{12,28},{16,0},{20,4},{24,8},{28,12},{1,17},{... | collective-permute-start | bytes 3145736 | tf_op jit(solution)/shard_map/ppermute | solution.py:43
  634.6 30.3 %collective-permute-start.91 = (bf16[2,1,256,1024]{3,2,0,1:T(8,128)(2,1)S(1)}, bf16[2,1,256,1024]{3,2,0,1:T(8,128)(2,1)S(1)}, u32[]{:S(2)}, u32[]{:S(2)}) collective-permute-start(bf16[2,1,256,1024]{3,2,0,1:T(8,128)(2,1)S(1)} %dynamic-slice_bitcast_fusion.6), channel_id=1, source_target_pairs={{0,8},{4,12},{8,0},{12,4},{16,24},{20,28},{24,16},{28,20},{1,9},{5... | collective-permute-start | bytes 3145736 | tf_op jit(solution)/shard_map/ppermute | solution.py:43
  676.1 20.0 %collective-permute-start.100 = (f32[1024]{0:T(1024)S(1)}, f32[1024]{0:T(1024)S(1)}, u32[]{:S(2)}, u32[]{:S(2)}) collective-permute-start(f32[1024]{0:T(1024)S(1)} %add_add_fusion.6), channel_id=1, source_target_pairs={{0,3},{1,2},{2,1},{3,0},{4,7},{5,6},{6,5},{7,4},{8,11},{9,10},{10,... | collective-permute-start | bytes 12296 | tf_op jit(solution)/shard_map/ppermute | solution.py:43
  678.7 17.4 %collective-permute-start.98 = (f32[1024]{0:T(1024)S(1)}, f32[1024]{0:T(1024)S(1)}, u32[]{:S(2)}, u32[]{:S(2)}) collective-permute-start(f32[1024]{0:T(1024)S(1)} %add_add_fusion.6), channel_id=1, source_target_pairs={{0,1},{1,0},{2,3},{3,2},{4,5},{5,4},{6,7},{7,6},{8,9},{9,8},{10,11... | collective-permute-start | bytes 12296 | tf_op jit(solution)/shard_map/ppermute | solution.py:43
  678.7 17.4 %collective-permute-start.99 = (f32[1024]{0:T(1024)S(1)}, f32[1024]{0:T(1024)S(1)}, u32[]{:S(2)}, u32[]{:S(2)}) collective-permute-start(f32[1024]{0:T(1024)S(1)} %add_add_fusion.6), channel_id=1, source_target_pairs={{0,2},{1,3},{2,0},{3,1},{4,6},{5,7},{6,4},{7,5},{8,10},{9,11},{10,... | collective-permute-start | bytes 12296 | tf_op jit(solution)/shard_map/ppermute | solution.py:43
  697.8 18.1 %collective-permute-start.107 = (bf16[4,1,2,64,256]{4,3,2,0,1:T(8,128)(2,1)}, bf16[4,1,2,64,256]{4,3,2,0,1:T(8,128)(2,1)}, u32[]{:S(2)}, u32[]{:S(2)}) collective-permute-start(bf16[4,1,2,64,256]{4,3,2,0,1:T(8,128)(2,1)} %dynamic-slice_bitcast_fusion.10), channel_id=1, source_target_pairs={{0,16},{4,20},{8,24},{12,28},{16,0},{20,4},{24,8},{28,12},{1,17},{... | collective-permute-start | bytes 786440 | tf_op jit(solution)/shard_map/ppermute | solution.py:43
  699.5 26.8 %collective-permute-start.103 = (bf16[1,1,256,1024]{3,2,1,0:T(8,128)(2,1)}, bf16[1,1,256,1024]{3,2,1,0:T(8,128)(2,1)}, u32[]{:S(2)}, u32[]{:S(2)}) collective-permute-start(bf16[1,1,256,1024]{3,2,1,0:T(8,128)(2,1)} %dynamic-slice_bitcast_fusion.9), channel_id=1, source_target_pairs={{0,16},{4,20},{8,24},{12,28},{16,0},{20,4},{24,8},{28,12},{1,17},{... | collective-permute-start | bytes 1572872 | tf_op jit(solution)/shard_map/ppermute | solution.py:43
  701.5 26.1 %collective-permute-start.104 = (bf16[1,1,256,1024]{3,2,1,0:T(8,128)(2,1)}, bf16[1,1,256,1024]{3,2,1,0:T(8,128)(2,1)}, u32[]{:S(2)}, u32[]{:S(2)}) collective-permute-start(bf16[1,1,256,1024]{3,2,1,0:T(8,128)(2,1)} %dynamic-slice_bitcast_fusion.8), channel_id=1, source_target_pairs={{0,8},{4,12},{8,0},{12,4},{16,24},{20,28},{24,16},{28,20},{1,9},{5... | collective-permute-start | bytes 1572872 | tf_op jit(solution)/shard_map/ppermute | solution.py:43
  705.1 24.3 %collective-permute-start.102 = (bf16[9,4,4,1,16,512]{5,4,2,1,0,3:T(8,128)(2,1)}, bf16[9,4,4,1,16,512]{5,4,2,1,0,3:T(8,128)(2,1)}, u32[]{:S(2)}, u32[]{:S(2)}) collective-permute-start(bf16[9,4,4,1,16,512]{5,4,2,1,0,3:T(8,128)(2,1)} %dynamic-slice_bitcast_fusion), channel_id=1, source_target_pairs={{0,4},{4,0},{8,12},{12,8},{16,20},{20,16},{24,28},{28,24},{1,5},{5... | collective-permute-start | bytes 7077896 | tf_op jit(solution)/shard_map/ppermute | solution.py:43
  733.2 18.8 %collective-permute-start.114 = (bf16[13,4,1,2,16,256]{5,4,3,1,0,2:T(8,128)(2,1)S(1)}, bf16[13,4,1,2,16,256]{5,4,3,1,0,2:T(8,128)(2,1)S(1)}, u32[]{:S(2)}, u32[]{:S(2)}) collective-permute-start(bf16[13,4,1,2,16,256]{5,4,3,1,0,2:T(8,128)(2,1)S(1)} %dynamic-slice_bitcast_fusion.7), channel_id=1, source_target_pairs={{0,16},{4,20},{8,24},{12,28},{16,0},{20,4},{24,8},{28,12},{1,17},{... | collective-permute-start | bytes 2555912 | tf_op jit(solution)/shard_map/ppermute | solution.py:43
  734.4 19.0 %collective-permute-start.112 = (bf16[13,4,2,1,16,256]{5,4,1,0,3,2:T(8,128)(2,1)S(1)}, bf16[13,4,2,1,16,256]{5,4,1,0,3,2:T(8,128)(2,1)S(1)}, u32[]{:S(2)}, u32[]{:S(2)}) collective-permute-start(bf16[13,4,2,1,16,256]{5,4,1,0,3,2:T(8,128)(2,1)S(1)} %bitcast.506), channel_id=1, source_target_pairs={{0,8},{4,12},{8,0},{12,4},{16,24},{20,28},{24,16},{28,20},{1,9},{5... | collective-permute-start | bytes 2555912 | tf_op jit(solution)/shard_map/ppermute | solution.py:43
  (209 other events, 2294.3 us)
Sparse Core Ops, SparseCore 0:
  66.1 46.0 all-gather.5
  128.2 55.9 all-gather.7
  186.6 59.8 all-gather.3
  445.3 130.4 all-reduce.3

commit v5 on v3

--- a/solution.py
+++ b/solution.py
@@ -544,7 +544,7 @@
         dot_ref[at, :] += lane_parts(act * pre_ref[at, :].astype(F32))
         return carry
 
-    lax.fori_loop(0, act_ref.shape[0] // CHUNK, multiply, 0)
+    lax.fori_loop(0, act_ref.shape[0] // CHUNK, multiply, 0, unroll=4)
 
 
 def aspp_backward(one, rows, pool, mask8, weights_t, slope, pre):

time: 841 us -> 837 us (level)
  transfers between devices with their start and end apart: 124 -> 124, of which waited for: 51 -> 50; matrix products, arithmetic and copies ran while one was open for 23% -> 23% of each run, Pallas kernels for 12% -> 11%
where the time goes in v5:
time: 837 us; the launch traced here: 827 us
  waiting for transfers between devices  234 us (28%)
  starting transfers between devices  171 us (20%)
  Pallas kernels  132 us (16%)
  other arithmetic  96.9 us (12%)
  matrix products  91.6 us (11%)
  local copies, waits for them, and re-layouts  77.7 us (9%)
  between operations  24.2 us (3%)
    ppermute x103, starting transfers between devices, xor_move(): return lax.ppermute(x, axis, [(i, i ^ mask) for i in range(n)])  127 us
    ppermute x103, waiting for transfers between devices, xor_move(): return lax.ppermute(x, axis, [(i, i ^ mask) for i in range(n)])  99.4 us
    ppermute x6, waiting for transfers between devices, line_shift(): lax.ppermute(x, 'head', [(i, i + by) for i in range(n) if 0 <= i + by < n])  70.5 us
    dot_general x13, matrix products, dot(): lax.dot_general(a, b, ((ca, cb), ((), ())), preferred_element_type=F32)  48 us
    pallas_call x1, Pallas kernels, aspp_forward(): pl.pallas_call(aspp_forward_kernel, grid_spec=pltpu.PrefetchScalarGridSpe...  39.2 us
    all_gather x1, waiting for transfers between devices, shards(): neck_low = lax.all_gather(neck_low, 'head', axis=0, tiled=True)  32.5 us
    pallas_call x1, Pallas kernels, aspp_backward(): pl.pallas_call(aspp_backward_kernel, grid=(quads,), in_specs=[pl.BlockSpe...  29.3 us
    pallas_call x2, Pallas kernels, taps_grad(): pl.pallas_call(functools.partial(taps_grad_kernel, starts), grid=(width /...  26.3 us
  transfers between devices with their start and end apart: 124, of which 50 were waited for; matrix products, arithmetic and copies ran while one was open for 23% of the time, Pallas kernels for 11%

profile of v5, /device:TPU:0, one launch (start us, length us, event | category | flops | bytes accessed | tf_op | source)
XLA Modules:
  0.0 827.0 jit_solution(10363300508306201485)
XLA Ops:
  9.4 32.5 %all-gather.4.cloned.1.call-done = bf16[4,272,512]{2,1,0:T(8,128)(2,1)} async-done(((bf16[1,272,512]{2,1,0:T(8,128)(2,1)}), bf16[4,272,512]{2,1,0:T(8,128)(2,1)}) %all-gather.4.cloned.1.call-update) | async-done | bytes 1114128 | tf_op jit(solution)/shard_map/all_gather | solution.py:720
  44.2 4.7 collective-permute-start
  54.1 38.1 %collective-permute-done.x4 = bf16[2048,512]{1,0:T(8,128)(2,1)} collective-permute-done((bf16[2048,512]{1,0:T(8,128)(2,1)S(1)}, bf16[2048,512]{1,0:T(8,128)(2,1)}, u32[]{:S(2)}, u32[]{:S(2)}) %collective-permute-start) | collective-permute-done | bytes 2097184 | tf_op jit(solution)/shard_map/ppermute | solution.py:105
  92.2 5.6 collective-permute-done.1.x1
  99.9 4.5 fusion.153
  104.4 4.3 reshape.656
  108.8 4.1 multiply_reduce_fusion.6
  127.4 3.2 collective-permute-done.8
  137.3 19.9 %all-gather.8.cloned.1.call-done.in_ref = bf16[8,256,2048]{2,1,0:T(8,128)(2,1)} async-done(((bf16[1,256,2048]{2,1,0:T(8,128)(2,1)}), bf16[8,256,2048]{2,1,0:T(8,128)(2,1)}) %all-gather.8.cloned.1.call-update) | async-done | bytes 8388624 | tf_op jit(solution)/shard_map/all_gather | solution.py:740
  157.2 6.3 shard_map.359.w_ref
  163.5 3.1 copy-done
  172.0 3.3 collective-permute-start.14
  175.3 10.4 %copy.83 = bf16[1920,2048]{0,1:T(8,128)(2,1)} copy(bf16[1920,2048]{1,0:T(8,128)(2,1)} %copy-done) | data formatting | bytes 15728640 | tf_op jit(solution)/shard_map/pallas_call | solution.py:256
  190.8 5.9 collective-permute-start.27
  201.8 15.1 %shard_map.360 = (f32[512,2048]{1,0:T(8,128)}, bf16[512,2048]{1,0:T(8,128)(2,1)S(1)}, f32[512,128]{1,0:T(8,128)S(1)}, f32[512,128]{1,0:T(8,128)S(1)}) custom-call(s32[1]{0:T(128)} %bitcast.20.z_ref, bf16[512,512]{1,0:T(8,128)(2,1)S(1)} %multiply_convert_fusion.7.s0, bf16[512,512]{1,0:T(8,128)(2,1)S(1)} %copy-done.12, ...), custom_call_target="tpu_custom_call" | custom-call | flops 9663676416 | bytes 16777216 | tf_op jit(solution)/shard_map/pallas_call | solution.py:323
  232.2 6.0 collective-permute-done.25.x2
  240.0 6.2 collective-permute-start.28
  246.3 10.6 %multiply_reduce_fusion = (f32[2048]{0:T(1024)S(1)}, f32[2048]{0:T(1024)S(1)}, bf16[2048,2048]{1,0:T(8,128)(2,1)}) fusion(f32[2048]{0:T(1024)S(1)} %fusion.111, bf16[2048,512]{1,0:T(8,128)(2,1)} %bitcast.485, f32[512,2048]{1,0:T(8,128)} %get-tuple-element.88, f32[512]{0:T(512)S(1)} %bitcast.523, f32[512]{0:T(512)S(1)} %get-tuple-element.188, ...), kind=kOutput, calls=%fused_computation.1 | convolution fusion | flops 4326420480 | bytes 14712832 | tf_op jit(solution)/shard_map/dot_general | solution.py:823
  269.7 18.2 %collective-permute-done.26.x3 = bf16[2048,512]{1,0:T(8,128)(2,1)} collective-permute-done((bf16[2048,512]{1,0:T(8,128)(2,1)S(1)}, bf16[2048,512]{1,0:T(8,128)(2,1)}, u32[]{:S(2)}, u32[]{:S(2)}) %collective-permute-start.26) | collective-permute-done | bytes 2097184 | tf_op jit(solution)/shard_map/ppermute | solution.py:105
  290.0 39.2 %shard_map.361 = (bf16[2048,2048]{1,0:T(8,128)(2,1)}, bf16[2048,2048]{1,0:T(8,128)(2,1)}, f32[4,64,2048]{2,1,0:T(8,128)}, bf16[6,4,64,512]{3,2,1,0:T(8,128)(2,1)}, f32[4,64,128]{2,1,0:T(8,128)}) custom-call(s32[1]{0:T(128)} %bitcast.20.z_ref, bf16[2048,2048]{1,0:T(8,128)(2,1)} %get-tuple-element.209.pre_ref, f32[2048,2]{1,0:T(8,128)} %copy.89.coef_ref, ...), custom_call_target="tpu_custom_call" | custom-call | flops 15569256448 | bytes 50331648 | tf_op jit(solution)/shard_map/pallas_call | solution.py:476
  336.6 3.8 collective-permute-start.29
  373.9 8.2 shard_map.362
  382.1 6.3 collective-permute-done.37
  402.6 3.6 collective-permute-start.43
  445.8 5.6 collective-permute-done.53
  451.4 10.9 %collective-permute-done.54 = bf16[256,512]{1,0:T(8,128)(2,1)S(1)} collective-permute-done((bf16[256,512]{1,0:T(8,128)(2,1)S(1)}, bf16[256,512]{1,0:T(8,128)(2,1)S(1)}, u32[]{:S(2)}, u32[]{:S(2)}) %collective-permute-start.54) | collective-permute-done | bytes 262176 | tf_op jit(solution)/shard_map/ppermute | solution.py:43
  470.5 4.6 collective-permute-start.64
  495.9 6.3 collective-permute-done.62
  505.3 29.3 %shard_map.363 = (bf16[1920,2048]{1,0:T(8,128)(2,1)}, bf16[2048,2048]{1,0:T(8,128)(2,1)}, f32[2048,128]{1,0:T(8,128)}, f32[2048,128]{1,0:T(8,128)}) custom-call(bf16[64,2048]{1,0:T(8,128)(2,1)} %slice.682.one_ref, bf16[3,3,4,64,512]{4,3,2,1,0:T(8,128)(2,1)} %pad_maximum_fusion.1.rows_ref, f32[64,128]{1,0:T(8,128)} %broadcast_in_dim.31.pool_in, ...), custom_call_target="tpu_custom_call" | custom-call | flops 16106127360 | bytes 50331648 | tf_op jit(solution)/shard_map/pallas_call | solution.py:556
  542.9 13.1 %shard_map.364 = bf16[8,256,1024]{2,1,0:T(8,128)(2,1)S(1)} custom-call(bf16[1920,2048]{1,0:T(8,128)(2,1)} %get-tuple-element.112.spread_ref, bf16[2048,2048]{1,0:T(8,128)(2,1)} %get-tuple-element.108.y_ref, bf16[48,2048]{1,0:T(8,128)(2,1)S(1)} %concatenate.173.project_ref), custom_call_target="tpu_custom_call" | custom-call | flops 8053063680 | bytes 20971520 | tf_op jit(solution)/shard_map/pallas_call | solution.py:600
  562.6 13.2 %shard_map.365 = bf16[8,256,1024]{2,1,0:T(8,128)(2,1)S(1)} custom-call(bf16[1920,2048]{1,0:T(8,128)(2,1)} %get-tuple-element.112.spread_ref, bf16[2048,2048]{1,0:T(8,128)(2,1)} %get-tuple-element.108.y_ref, bf16[48,2048]{1,0:T(8,128)(2,1)S(1)} %concatenate.173.project_ref), custom_call_target="tpu_custom_call" | custom-call | flops 8053063680 | bytes 20971520 | tf_op jit(solution)/shard_map/pallas_call | solution.py:600
  577.8 9.9 %multiply_convert_fusion = bf16[2048,2048]{1,0:T(8,128)(2,1)S(1)} fusion(bf16[2048,2048]{1,0:T(8,128)(2,1)} %get-tuple-element.209.pre_ref, bf16[2048,2048]{1,0:T(8,128)(2,1)} %get-tuple-element.102, f32[2048]{0:T(1024)S(1)} %get-tuple-element.336, f32[2048]{0:T(1024)S(1)} %copy-done.60, f32[2048]{0:T(1024)S(1)} %copy-done.61, ...), kind=kLoop, calls=%fused_computation.3 | loop fusion | flops 41943040 | bytes 25214976 | tf_op jit(solution)/shard_map/convert_element_type | solution.py:998
  587.8 8.5 %fusion.135 = (f32[512]{0:T(512)S(1)}, f32[512]{0:T(512)S(1)}, f32[512,2048]{1,0:T(8,128)}) fusion(f32[512]{0:T(512)S(1)} %copy-done.82, f32[512,2048]{1,0:T(8,128)S(1)} %copy-done.24, f32[512]{0:T(512)S(1)} %copy-done.84, f32[512]{0:T(512)S(1)} %bitcast.524, f32[512]{0:T(512)S(1)} %bitcast.516, f32[2048]{0:T(1024)S(1)} %fusion.111, ...), kind=kOutput, calls=%fused_computation.496 | convolution fusion | flops 4311743488 | bytes 18894848 | tf_op jit(solution)/shard_map/dot_general | solution.py:38
  609.2 6.9 convolution_convert_fusion.1
  623.9 6.3 fusion.166
  630.3 3.9 collective-permute-start.86
  635.8 7.9 shard_map.366
  643.7 18.8 %fusion.134 = (f32[512]{0:T(512)S(1)}, f32[512]{0:T(512)S(1)}, f32[512,2048]{1,0:T(8,128)}) fusion(f32[512]{0:T(512)S(1)} %copy-done.72, f32[512,2048]{1,0:T(8,128)} %fusion.166, f32[512]{0:T(512)S(1)} %copy-done.74, f32[512]{0:T(512)S(1)} %bitcast.512, f32[512]{0:T(512)S(1)} %bitcast.510, f32[2048]{0:T(1024)S(1)} %fusion.111, ...), kind=kOutput, calls=%fused_computation.495 | convolution fusion | flops 9680453632 | bytes 32002048 | tf_op jit(solution)/shard_map/dot_general | solution.py:1023
  680.6 15.6 %convolution_convert_fusion.2 = bf16[9,512,512]{2,1,0:T(8,128)(2,1)} fusion(bf16[9,512,2048]{2,1,0:T(8,128)(2,1)} %shard_map.366, bf16[512,2048]{1,0:T(8,128)(2,1)S(1)} %copy-done.17), kind=kOutput, calls=%fused_computation.28 | convolution fusion | flops 9666035712 | bytes 25690112 | tf_op jit(solution)/shard_map/dot_general | solution.py:38
  705.3 8.3 %convolution_convert_fusion = bf16[512,2048]{1,0:T(8,128)(2,1)S(1)} fusion(bf16[2048,2048]{1,0:T(8,128)(2,1)S(1)} %bitcast.464, f32[512,2048]{1,0:T(8,128)} %get-tuple-element.363, f32[512,2048]{1,0:T(8,128)} %fusion.166, f32[512]{0:T(512)S(1)} %get-tuple-element.340, f32[512]{0:T(512)S(1)} %get-tuple-element.342, f32[512]{0:T(512)S(1)} %copy-done.72, ...), kind=kOutput, calls=%fused_computation.25 | convolution fusion | flops 4304404480 | bytes 18892800 | tf_op jit(solution)/shard_map/dot_general | solution.py:38
  718.2 3.2 collective-permute-done.99
  721.5 4.9 collective-permute-done.101
  734.9 17.3 %collective-permute-done.107 = bf16[13,4,1,2,16,256]{5,4,3,1,0,2:T(8,128)(2,1)S(1)} collective-permute-done((bf16[13,4,1,2,16,256]{5,4,3,1,0,2:T(8,128)(2,1)S(1)}, bf16[13,4,1,2,16,256]{5,4,3,1,0,2:T(8,128)(2,1)S(1)}, u32[]{:S(2)}, u32[]{:S(2)}) %collective-permute-start.107) | collective-permute-done | bytes 852000 | tf_op jit(solution)/shard_map/ppermute | solution.py:43
  756.9 3.3 collective-permute-start.103
  765.9 3.7 collective-permute-start.110
  775.5 7.0 collective-permute-done.110
  800.0 3.5 all-to-all-start
  806.5 6.3 multiply_subtract_fusion
  (715 shorter events, 321.6 us)
Async XLA Ops:
  7.2 34.7 %all-gather.4.cloned.1.call-start = ((), (), s32[]{:S(2)}) async-start(), calls=%async_computation.1 | async-start | bytes 1392640 | tf_op jit(solution)/shard_map/all_gather | solution.py:720
  9.4 90.6 %all-gather.6.cloned.1.call-start = ((), (), s32[]{:S(2)}) async-start(), calls=%async_computation.2 | async-start | bytes 10027008 | tf_op jit(solution)/shard_map/all_gather | solution.py:721
  41.9 115.2 %all-gather.8.cloned.1.call-start = ((), (), s32[]{:S(2)}) async-start(), calls=%async_computation.3 | async-start | bytes 9437184 | tf_op jit(solution)/shard_map/all_gather | solution.py:740
  43.6 534.1 %all-reduce.3.cloned.1.call-start = ((), (), s32[]{:S(2)}) async-start(), calls=%async_computation.4 | async-start | bytes 1622016 | tf_op jit(solution)/shard_map/psum | solution.py:899
  44.2 47.9 %collective-permute-start = (bf16[2048,512]{1,0:T(8,128)(2,1)S(1)}, bf16[2048,512]{1,0:T(8,128)(2,1)}, u32[]{:S(2)}, u32[]{:S(2)}) collective-permute-start(bf16[2048,512]{1,0:T(8,128)(2,1)S(1)} %copy-done.5), channel_id=1, source_target_pairs={{0,1},{1,2},{2,3},{4,5},{5,6},{6,7},{8,9},{9,10},{10,11},{12,13},{... | collective-permute-start | bytes 6291464 | tf_op jit(solution)/shard_map/ppermute | solution.py:105
  48.9 48.9 %collective-permute-start.1 = (bf16[2048,512]{1,0:T(8,128)(2,1)S(1)}, bf16[2048,512]{1,0:T(8,128)(2,1)}, u32[]{:S(2)}, u32[]{:S(2)}) collective-permute-start(bf16[2048,512]{1,0:T(8,128)(2,1)S(1)} %copy-done.5), channel_id=1, source_target_pairs={{1,0},{2,1},{3,2},{5,4},{6,5},{7,6},{9,8},{10,9},{11,10},{13,12},{... | collective-permute-start | bytes 6291464 | tf_op jit(solution)/shard_map/ppermute | solution.py:105
  133.8 52.9 %collective-permute-start.10 = (bf16[512,512]{1,0:T(8,128)(2,1)S(1)}, bf16[512,512]{1,0:T(8,128)(2,1)S(1)}, u32[]{:S(2)}, u32[]{:S(2)}) collective-permute-start(bf16[512,512]{1,0:T(8,128)(2,1)S(1)} %multiply_convert_fusion.7.s0), channel_id=1, source_target_pairs={{0,2},{1,3},{2,0},{3,1},{4,6},{5,7},{6,4},{7,5},{8,10},{9,11},{10,... | collective-permute-start | bytes 1572872 | tf_op jit(solution)/shard_map/ppermute | solution.py:43
  133.9 52.8 %collective-permute-start.11 = (bf16[512,512]{1,0:T(8,128)(2,1)S(1)}, bf16[512,512]{1,0:T(8,128)(2,1)S(1)}, u32[]{:S(2)}, u32[]{:S(2)}) collective-permute-start(bf16[512,512]{1,0:T(8,128)(2,1)S(1)} %multiply_convert_fusion.7.s0), channel_id=1, source_target_pairs={{0,3},{1,2},{2,1},{3,0},{4,7},{5,6},{6,5},{7,4},{8,11},{9,10},{10,... | collective-permute-start | bytes 1572872 | tf_op jit(solution)/shard_map/ppermute | solution.py:43
  134.9 51.7 %collective-permute-start.9 = (bf16[512,512]{1,0:T(8,128)(2,1)S(1)}, bf16[512,512]{1,0:T(8,128)(2,1)S(1)}, u32[]{:S(2)}, u32[]{:S(2)}) collective-permute-start(bf16[512,512]{1,0:T(8,128)(2,1)S(1)} %multiply_convert_fusion.7.s0), channel_id=1, source_target_pairs={{0,1},{1,0},{2,3},{3,2},{4,5},{5,4},{6,7},{7,6},{8,9},{9,8},{10,11... | collective-permute-start | bytes 1572872 | tf_op jit(solution)/shard_map/ppermute | solution.py:43
  168.9 16.8 %collective-permute-start.13 = (bf16[64,320]{0,1:T(8,128)(2,1)S(1)}, bf16[64,320]{0,1:T(8,128)(2,1)S(1)}, u32[]{:S(2)}, u32[]{:S(2)}) collective-permute-start(bf16[64,320]{0,1:T(8,128)(2,1)S(1)} %get-tuple-element.299), channel_id=1, source_target_pairs={{0,2},{1,3},{2,0},{3,1},{4,6},{5,7},{6,4},{7,5},{8,10},{9,11},{10,... | collective-permute-start | bytes 122888 | tf_op jit(solution)/shard_map/ppermute | solution.py:43
  189.5 48.7 %collective-permute-start.25 = (bf16[2048,512]{1,0:T(8,128)(2,1)}, bf16[2048,512]{1,0:T(8,128)(2,1)S(1)}, u32[]{:S(2)}, u32[]{:S(2)}) collective-permute-start(bf16[2048,512]{1,0:T(8,128)(2,1)} %collective-permute-done.1.x1), channel_id=1, source_target_pairs={{1,0},{2,1},{3,2},{5,4},{6,5},{7,6},{9,8},{10,9},{11,10},{13,12},{... | collective-permute-start | bytes 6291464 | tf_op jit(solution)/shard_map/ppermute | solution.py:105
  190.8 49.3 %collective-permute-start.27 = (bf16[2048,512]{1,0:T(8,128)(2,1)}, bf16[2048,512]{1,0:T(8,128)(2,1)}, u32[]{:S(2)}, u32[]{:S(2)}) collective-permute-start(bf16[2048,512]{1,0:T(8,128)(2,1)} %collective-permute-done.x4), channel_id=1, source_target_pairs={{0,1},{1,2},{2,3},{4,5},{5,6},{6,7},{8,9},{9,10},{10,11},{12,13},{... | collective-permute-start | bytes 6291464 | tf_op jit(solution)/shard_map/ppermute | solution.py:105
  238.2 49.8 %collective-permute-start.26 = (bf16[2048,512]{1,0:T(8,128)(2,1)S(1)}, bf16[2048,512]{1,0:T(8,128)(2,1)}, u32[]{:S(2)}, u32[]{:S(2)}) collective-permute-start(bf16[2048,512]{1,0:T(8,128)(2,1)S(1)} %collective-permute-done.25.x2), channel_id=1, source_target_pairs={{1,0},{2,1},{3,2},{5,4},{6,5},{7,6},{9,8},{10,9},{11,10},{13,12},{... | collective-permute-start | bytes 6291464 | tf_op jit(solution)/shard_map/ppermute | solution.py:105
  240.0 50.0 %collective-permute-start.28 = (bf16[2048,512]{1,0:T(8,128)(2,1)}, bf16[2048,512]{1,0:T(8,128)(2,1)}, u32[]{:S(2)}, u32[]{:S(2)}) collective-permute-start(bf16[2048,512]{1,0:T(8,128)(2,1)} %collective-permute-done.27.x5), channel_id=1, source_target_pairs={{0,1},{1,2},{2,3},{4,5},{5,6},{6,7},{8,9},{9,10},{10,11},{12,13},{... | collective-permute-start | bytes 6291464 | tf_op jit(solution)/shard_map/ppermute | solution.py:105
  365.1 17.0 %collective-permute-start.36 = (bf16[256,512]{1,0:T(8,128)(2,1)}, bf16[256,512]{1,0:T(8,128)(2,1)}, u32[]{:S(2)}, u32[]{:S(2)}) collective-permute-start(bf16[256,512]{1,0:T(8,128)(2,1)} %get-tuple-element.255), channel_id=1, source_target_pairs={{0,1},{1,0},{2,3},{3,2},{4,5},{5,4},{6,7},{7,6},{8,9},{9,8},{10,11... | collective-permute-start | bytes 786440 | tf_op jit(solution)/shard_map/ppermute | solution.py:43
  367.3 21.2 %collective-permute-start.37 = (bf16[256,512]{1,0:T(8,128)(2,1)}, bf16[256,512]{1,0:T(8,128)(2,1)}, u32[]{:S(2)}, u32[]{:S(2)}) collective-permute-start(bf16[256,512]{1,0:T(8,128)(2,1)} %get-tuple-element.257), channel_id=1, source_target_pairs={{0,2},{1,3},{2,0},{3,1},{4,6},{5,7},{6,4},{7,5},{8,10},{9,11},{10,... | collective-permute-start | bytes 786440 | tf_op jit(solution)/shard_map/ppermute | solution.py:43
  368.9 19.6 %collective-permute-start.38 = (bf16[256,512]{1,0:T(8,128)(2,1)}, bf16[256,512]{1,0:T(8,128)(2,1)}, u32[]{:S(2)}, u32[]{:S(2)}) collective-permute-start(bf16[256,512]{1,0:T(8,128)(2,1)} %get-tuple-element.256), channel_id=1, source_target_pairs={{0,3},{1,2},{2,1},{3,0},{4,7},{5,6},{6,5},{7,4},{8,11},{9,10},{10,... | collective-permute-start | bytes 786440 | tf_op jit(solution)/shard_map/ppermute | solution.py:43
  440.3 22.0 %collective-permute-start.54 = (bf16[256,512]{1,0:T(8,128)(2,1)S(1)}, bf16[256,512]{1,0:T(8,128)(2,1)S(1)}, u32[]{:S(2)}, u32[]{:S(2)}) collective-permute-start(bf16[256,512]{1,0:T(8,128)(2,1)S(1)} %multiply_convert_fusion.8), channel_id=1, source_target_pairs={{0,2},{1,3},{2,0},{3,1},{4,6},{5,7},{6,4},{7,5},{8,10},{9,11},{10,... | collective-permute-start | bytes 786440 | tf_op jit(solution)/shard_map/ppermute | solution.py:43
  442.6 19.7 %collective-permute-start.55 = (bf16[256,512]{1,0:T(8,128)(2,1)S(1)}, bf16[256,512]{1,0:T(8,128)(2,1)S(1)}, u32[]{:S(2)}, u32[]{:S(2)}) collective-permute-start(bf16[256,512]{1,0:T(8,128)(2,1)S(1)} %multiply_convert_fusion.8), channel_id=1, source_target_pairs={{0,3},{1,2},{2,1},{3,0},{4,7},{5,6},{6,5},{7,4},{8,11},{9,10},{10,... | collective-permute-start | bytes 786440 | tf_op jit(solution)/shard_map/ppermute | solution.py:43
  470.5 20.2 %collective-permute-start.64 = (bf16[64,320]{1,0:T(8,128)(2,1)}, bf16[64,320]{1,0:T(8,128)(2,1)}, u32[]{:S(2)}, u32[]{:S(2)}) collective-permute-start(bf16[64,320]{1,0:T(8,128)(2,1)} %get-tuple-element.319), channel_id=1, source_target_pairs={{0,1},{1,0},{2,3},{3,2},{4,5},{5,4},{6,7},{7,6},{8,9},{9,8},{10,11... | collective-permute-start | bytes 122888 | tf_op jit(solution)/shard_map/ppermute | solution.py:43
  475.1 16.9 %collective-permute-start.65 = (bf16[64,320]{1,0:T(8,128)(2,1)}, bf16[64,320]{1,0:T(8,128)(2,1)}, u32[]{:S(2)}, u32[]{:S(2)}) collective-permute-start(bf16[64,320]{1,0:T(8,128)(2,1)} %get-tuple-element.318), channel_id=1, source_target_pairs={{0,2},{1,3},{2,0},{3,1},{4,6},{5,7},{6,4},{7,5},{8,10},{9,11},{10,... | collective-permute-start | bytes 122888 | tf_op jit(solution)/shard_map/ppermute | solution.py:43
  475.1 19.8 %collective-permute-start.66 = (bf16[64,320]{1,0:T(8,128)(2,1)}, bf16[64,320]{1,0:T(8,128)(2,1)}, u32[]{:S(2)}, u32[]{:S(2)}) collective-permute-start(bf16[64,320]{1,0:T(8,128)(2,1)} %get-tuple-element.317), channel_id=1, source_target_pairs={{0,3},{1,2},{2,1},{3,0},{4,7},{5,6},{6,5},{7,4},{8,11},{9,10},{10,... | collective-permute-start | bytes 122888 | tf_op jit(solution)/shard_map/ppermute | solution.py:43
  485.4 17.0 %collective-permute-start.59 = (bf16[5,64,512]{2,1,0:T(8,128)(2,1)S(1)}, bf16[5,64,512]{2,1,0:T(8,128)(2,1)S(1)}, u32[]{:S(2)}, u32[]{:S(2)}) collective-permute-start(bf16[5,64,512]{2,1,0:T(8,128)(2,1)S(1)} %get-tuple-element.320), channel_id=1, source_target_pairs={{4,0},{8,4},{12,8},{20,16},{24,20},{28,24},{5,1},{9,5},{13,9},{21,... | collective-permute-start | bytes 983048 | tf_op jit(solution)/shard_map/ppermute | solution.py:100
  486.7 15.8 %collective-permute-start.60 = (bf16[5,64,512]{2,1,0:T(8,128)(2,1)S(1)}, bf16[5,64,512]{2,1,0:T(8,128)(2,1)S(1)}, u32[]{:S(2)}, u32[]{:S(2)}) collective-permute-start(bf16[5,64,512]{2,1,0:T(8,128)(2,1)S(1)} %get-tuple-element.322), channel_id=1, source_target_pairs={{0,4},{4,8},{8,12},{16,20},{20,24},{24,28},{1,5},{5,9},{9,13},{17,... | collective-permute-start | bytes 983048 | tf_op jit(solution)/shard_map/ppermute | solution.py:100
  539.1 19.0 %collective-permute-start.67 = (f32[6144]{0:T(1024)S(1)}, f32[6144]{0:T(1024)S(1)}, u32[]{:S(2)}, u32[]{:S(2)}) collective-permute-start(f32[6144]{0:T(1024)S(1)} %fusion.131), channel_id=1, source_target_pairs={{0,8},{4,12},{8,0},{12,4},{16,24},{20,28},{24,16},{28,20},{1,9},{5... | collective-permute-start | bytes 73736 | tf_op jit(solution)/shard_map/ppermute | solution.py:43
  541.4 16.7 %collective-permute-start.68 = (f32[6144]{0:T(1024)S(1)}, f32[6144]{0:T(1024)S(1)}, u32[]{:S(2)}, u32[]{:S(2)}) collective-permute-start(f32[6144]{0:T(1024)S(1)} %fusion.131), channel_id=1, source_target_pairs={{0,16},{4,20},{8,24},{12,28},{16,0},{20,4},{24,8},{28,12},{1,17},{... | collective-permute-start | bytes 73736 | tf_op jit(solution)/shard_map/ppermute | solution.py:43
  542.2 15.9 %collective-permute-start.69 = (f32[6144]{0:T(1024)S(1)}, f32[6144]{0:T(1024)S(1)}, u32[]{:S(2)}, u32[]{:S(2)}) collective-permute-start(f32[6144]{0:T(1024)S(1)} %fusion.131), channel_id=1, source_target_pairs={{0,24},{4,28},{8,16},{12,20},{16,8},{20,12},{24,0},{28,4},{1,25},{... | collective-permute-start | bytes 73736 | tf_op jit(solution)/shard_map/ppermute | solution.py:43
  558.1 19.6 %collective-permute-start.70 = (f32[6144]{0:T(1024)S(1)}, f32[6144]{0:T(1024)S(1)}, u32[]{:S(2)}, u32[]{:S(2)}) collective-permute-start(f32[6144]{0:T(1024)S(1)} %add_add_fusion.1), channel_id=1, source_target_pairs={{0,1},{1,0},{2,3},{3,2},{4,5},{5,4},{6,7},{7,6},{8,9},{9,8},{10,11... | collective-permute-start | bytes 73736 | tf_op jit(solution)/shard_map/ppermute | solution.py:43
  559.4 18.3 %collective-permute-start.71 = (f32[6144]{0:T(1024)S(1)}, f32[6144]{0:T(1024)S(1)}, u32[]{:S(2)}, u32[]{:S(2)}) collective-permute-start(f32[6144]{0:T(1024)S(1)} %add_add_fusion.1), channel_id=1, source_target_pairs={{0,2},{1,3},{2,0},{3,1},{4,6},{5,7},{6,4},{7,5},{8,10},{9,11},{10,... | collective-permute-start | bytes 73736 | tf_op jit(solution)/shard_map/ppermute | solution.py:43
  560.6 17.1 %collective-permute-start.72 = (f32[6144]{0:T(1024)S(1)}, f32[6144]{0:T(1024)S(1)}, u32[]{:S(2)}, u32[]{:S(2)}) collective-permute-start(f32[6144]{0:T(1024)S(1)} %add_add_fusion.1), channel_id=1, source_target_pairs={{0,3},{1,2},{2,1},{3,0},{4,7},{5,6},{6,5},{7,4},{8,11},{9,10},{10,... | collective-permute-start | bytes 73736 | tf_op jit(solution)/shard_map/ppermute | solution.py:43
  596.5 19.6 %collective-permute-start.81 = (bf16[4,1,256,1024]{3,2,0,1:T(8,128)(2,1)S(1)}, bf16[4,1,256,1024]{3,2,0,1:T(8,128)(2,1)S(1)}, u32[]{:S(2)}, u32[]{:S(2)}) collective-permute-start(bf16[4,1,256,1024]{3,2,0,1:T(8,128)(2,1)S(1)} %dynamic-slice_bitcast_fusion.1), channel_id=1, source_target_pairs={{0,4},{4,0},{8,12},{12,8},{16,20},{20,16},{24,28},{28,24},{1,5},{5... | collective-permute-start | bytes 6291464 | tf_op jit(solution)/shard_map/ppermute | solution.py:43
  601.1 16.0 %collective-permute-start.80 = (bf16[4,1,256,1024]{3,2,0,1:T(8,128)(2,1)S(1)}, bf16[4,1,256,1024]{3,2,0,1:T(8,128)(2,1)S(1)}, u32[]{:S(2)}, u32[]{:S(2)}) collective-permute-start(bf16[4,1,256,1024]{3,2,0,1:T(8,128)(2,1)S(1)} %dynamic-slice_bitcast_fusion.2), channel_id=1, source_target_pairs={{0,4},{4,0},{8,12},{12,8},{16,20},{20,16},{24,28},{28,24},{1,5},{5... | collective-permute-start | bytes 6291464 | tf_op jit(solution)/shard_map/ppermute | solution.py:43
  630.3 32.2 %collective-permute-start.86 = (bf16[4,4,1,64,512]{4,3,1,0,2:T(8,128)(2,1)S(1)}, bf16[4,4,1,64,512]{4,3,1,0,2:T(8,128)(2,1)}, u32[]{:S(2)}, u32[]{:S(2)}) collective-permute-start(bf16[4,4,1,64,512]{4,3,1,0,2:T(8,128)(2,1)S(1)} %dynamic-slice_bitcast_fusion.4), channel_id=1, source_target_pairs={{0,4},{4,0},{8,12},{12,8},{16,20},{20,16},{24,28},{28,24},{1,5},{5... | collective-permute-start | bytes 3145736 | tf_op jit(solution)/shard_map/ppermute | solution.py:43
  634.3 29.9 %collective-permute-start.85 = (bf16[1,2,256,1024]{3,2,1,0:T(8,128)(2,1)S(1)}, bf16[1,2,256,1024]{3,2,1,0:T(8,128)(2,1)}, u32[]{:S(2)}, u32[]{:S(2)}) collective-permute-start(bf16[1,2,256,1024]{3,2,1,0:T(8,128)(2,1)S(1)} %dynamic-slice_bitcast_fusion.5), channel_id=1, source_target_pairs={{0,16},{4,20},{8,24},{12,28},{16,0},{20,4},{24,8},{28,12},{1,17},{... | collective-permute-start | bytes 3145736 | tf_op jit(solution)/shard_map/ppermute | solution.py:43
  635.4 30.4 %collective-permute-start.84 = (bf16[2,1,256,1024]{3,2,0,1:T(8,128)(2,1)S(1)}, bf16[2,1,256,1024]{3,2,0,1:T(8,128)(2,1)S(1)}, u32[]{:S(2)}, u32[]{:S(2)}) collective-permute-start(bf16[2,1,256,1024]{3,2,0,1:T(8,128)(2,1)S(1)} %dynamic-slice_bitcast_fusion.6), channel_id=1, source_target_pairs={{0,8},{4,12},{8,0},{12,4},{16,24},{20,28},{24,16},{28,20},{1,9},{5... | collective-permute-start | bytes 3145736 | tf_op jit(solution)/shard_map/ppermute | solution.py:43
  676.2 20.0 %collective-permute-start.91 = (f32[1024]{0:T(1024)S(1)}, f32[1024]{0:T(1024)S(1)}, u32[]{:S(2)}, u32[]{:S(2)}) collective-permute-start(f32[1024]{0:T(1024)S(1)} %add_add_fusion.6), channel_id=1, source_target_pairs={{0,1},{1,0},{2,3},{3,2},{4,5},{5,4},{6,7},{7,6},{8,9},{9,8},{10,11... | collective-permute-start | bytes 12296 | tf_op jit(solution)/shard_map/ppermute | solution.py:43
  677.3 18.9 %collective-permute-start.92 = (f32[1024]{0:T(1024)S(1)}, f32[1024]{0:T(1024)S(1)}, u32[]{:S(2)}, u32[]{:S(2)}) collective-permute-start(f32[1024]{0:T(1024)S(1)} %add_add_fusion.6), channel_id=1, source_target_pairs={{0,2},{1,3},{2,0},{3,1},{4,6},{5,7},{6,4},{7,5},{8,10},{9,11},{10,... | collective-permute-start | bytes 12296 | tf_op jit(solution)/shard_map/ppermute | solution.py:43
  679.6 16.6 %collective-permute-start.93 = (f32[1024]{0:T(1024)S(1)}, f32[1024]{0:T(1024)S(1)}, u32[]{:S(2)}, u32[]{:S(2)}) collective-permute-start(f32[1024]{0:T(1024)S(1)} %add_add_fusion.6), channel_id=1, source_target_pairs={{0,3},{1,2},{2,1},{3,0},{4,7},{5,6},{6,5},{7,4},{8,11},{9,10},{10,... | collective-permute-start | bytes 12296 | tf_op jit(solution)/shard_map/ppermute | solution.py:43
  697.2 17.0 %collective-permute-start.98 = (bf16[4,2,1,64,256]{4,3,0,2,1:T(8,128)(2,1)}, bf16[4,2,1,64,256]{4,3,0,2,1:T(8,128)(2,1)}, u32[]{:S(2)}, u32[]{:S(2)}) collective-permute-start(bf16[4,2,1,64,256]{4,3,0,2,1:T(8,128)(2,1)} %bitcast.456), channel_id=1, source_target_pairs={{0,8},{4,12},{8,0},{12,4},{16,24},{20,28},{24,16},{28,20},{1,9},{5... | collective-permute-start | bytes 786440 | tf_op jit(solution)/shard_map/ppermute | solution.py:43
  698.0 18.1 %collective-permute-start.100 = (bf16[4,1,2,64,256]{4,3,2,0,1:T(8,128)(2,1)}, bf16[4,1,2,64,256]{4,3,2,0,1:T(8,128)(2,1)}, u32[]{:S(2)}, u32[]{:S(2)}) collective-permute-start(bf16[4,1,2,64,256]{4,3,2,0,1:T(8,128)(2,1)} %dynamic-slice_bitcast_fusion.10), channel_id=1, source_target_pairs={{0,16},{4,20},{8,24},{12,28},{16,0},{20,4},{24,8},{28,12},{1,17},{... | collective-permute-start | bytes 786440 | tf_op jit(solution)/shard_map/ppermute | solution.py:43
  699.8 26.7 %collective-permute-start.96 = (bf16[1,1,256,1024]{3,2,1,0:T(8,128)(2,1)}, bf16[1,1,256,1024]{3,2,1,0:T(8,128)(2,1)}, u32[]{:S(2)}, u32[]{:S(2)}) collective-permute-start(bf16[1,1,256,1024]{3,2,1,0:T(8,128)(2,1)} %dynamic-slice_bitcast_fusion.9), channel_id=1, source_target_pairs={{0,16},{4,20},{8,24},{12,28},{16,0},{20,4},{24,8},{28,12},{1,17},{... | collective-permute-start | bytes 1572872 | tf_op jit(solution)/shard_map/ppermute | solution.py:43
  701.6 26.1 %collective-permute-start.97 = (bf16[1,1,256,1024]{3,2,1,0:T(8,128)(2,1)}, bf16[1,1,256,1024]{3,2,1,0:T(8,128)(2,1)}, u32[]{:S(2)}, u32[]{:S(2)}) collective-permute-start(bf16[1,1,256,1024]{3,2,1,0:T(8,128)(2,1)} %dynamic-slice_bitcast_fusion.8), channel_id=1, source_target_pairs={{0,8},{4,12},{8,0},{12,4},{16,24},{20,28},{24,16},{28,20},{1,9},{5... | collective-permute-start | bytes 1572872 | tf_op jit(solution)/shard_map/ppermute | solution.py:43
  705.3 24.3 %collective-permute-start.95 = (bf16[9,4,4,1,16,512]{5,4,2,1,0,3:T(8,128)(2,1)}, bf16[9,4,4,1,16,512]{5,4,2,1,0,3:T(8,128)(2,1)}, u32[]{:S(2)}, u32[]{:S(2)}) collective-permute-start(bf16[9,4,4,1,16,512]{5,4,2,1,0,3:T(8,128)(2,1)} %dynamic-slice_bitcast_fusion), channel_id=1, source_target_pairs={{0,4},{4,0},{8,12},{12,8},{16,20},{20,16},{24,28},{28,24},{1,5},{5... | collective-permute-start | bytes 7077896 | tf_op jit(solution)/shard_map/ppermute | solution.py:43
  714.2 15.0 %collective-permute-start.94 = (bf16[4,4,4,1,16,512]{5,4,2,1,0,3:T(8,128)(2,1)S(1)}, bf16[4,4,4,1,16,512]{5,4,2,1,0,3:T(8,128)(2,1)S(1)}, u32[]{:S(2)}, u32[]{:S(2)}) collective-permute-start(bf16[4,4,4,1,16,512]{5,4,2,1,0,3:T(8,128)(2,1)S(1)} %dynamic-slice_bitcast_fusion.3), channel_id=1, source_target_pairs={{0,4},{4,0},{8,12},{12,8},{16,20},{20,16},{24,28},{28,24},{1,5},{5... | collective-permute-start | bytes 3145736 | tf_op jit(solution)/shard_map/ppermute | solution.py:43
  733.4 18.8 %collective-permute-start.107 = (bf16[13,4,1,2,16,256]{5,4,3,1,0,2:T(8,128)(2,1)S(1)}, bf16[13,4,1,2,16,256]{5,4,3,1,0,2:T(8,128)(2,1)S(1)}, u32[]{:S(2)}, u32[]{:S(2)}) collective-permute-start(bf16[13,4,1,2,16,256]{5,4,3,1,0,2:T(8,128)(2,1)S(1)} %dynamic-slice_bitcast_fusion.7), channel_id=1, source_target_pairs={{0,16},{4,20},{8,24},{12,28},{16,0},{20,4},{24,8},{28,12},{1,17},{... | collective-permute-start | bytes 2555912 | tf_op jit(solution)/shard_map/ppermute | solution.py:43
  734.7 18.9 %collective-permute-start.105 = (bf16[13,4,2,1,16,256]{5,4,1,0,3,2:T(8,128)(2,1)S(1)}, bf16[13,4,2,1,16,256]{5,4,1,0,3,2:T(8,128)(2,1)S(1)}, u32[]{:S(2)}, u32[]{:S(2)}) collective-permute-start(bf16[13,4,2,1,16,256]{5,4,1,0,3,2:T(8,128)(2,1)S(1)} %bitcast.494), channel_id=1, source_target_pairs={{0,8},{4,12},{8,0},{12,4},{16,24},{20,28},{24,16},{28,20},{1,9},{5... | collective-permute-start | bytes 2555912 | tf_op jit(solution)/shard_map/ppermute | solution.py:43
  765.9 16.7 %collective-permute-start.110 = (bf16[13,16,512]{2,1,0:T(8,128)(2,1)}, bf16[13,16,512]{2,1,0:T(8,128)(2,1)}, u32[]{:S(2)}, u32[]{:S(2)}) collective-permute-start(bf16[13,16,512]{2,1,0:T(8,128)(2,1)} %get-tuple-element.263), channel_id=1, source_target_pairs={{0,2},{1,3},{2,0},{3,1},{4,6},{5,7},{6,4},{7,5},{8,10},{9,11},{10,... | collective-permute-start | bytes 638984 | tf_op jit(solution)/shard_map/ppermute | solution.py:43
  800.0 15.2 %all-to-all-start = ((bf16[8,64,512]{2,1,0:T(8,128)(2,1)}), bf16[8,64,512]{2,1,0:T(8,128)(2,1)S(1)}, u32[]{:S(2)}, u32[]{:S(2)}) async-start(bf16[8,64,512]{2,1,0:T(8,128)(2,1)} %bitcast.216), calls=%async_computation | async-start | bytes 1048576 | tf_op jit(solution)/shard_map/all_to_all | solution.py:1066
  (181 other events, 1788.7 us)
Sparse Core Ops, SparseCore 0:
  10.2 31.6 all-gather.3
  43.8 56.0 all-gather.5
  102.4 54.7 all-gather.7
  445.9 130.7 all-reduce.2
